TPU v7x, 32 devices: a whole 2x2x4 slice. The times are simulated.
32 devices in a mesh: fsdp: 2 (over x), ctx: 8 (over z, y), tp: 2 (over core).
Axes of the slice: x: 2, y: 2, z: 4, core: 2. Of those that a mesh axis runs over, the one named last changes fastest.
Arguments:
- tokens: bfloat16 [8192, 768], P(('fsdp', 'ctx'), 'tp'), may hold values from -6 to 6
- cotangent: bfloat16 [8192, 768], P(('fsdp', 'ctx'), 'tp'), may hold values from -6 to 6
- w_qkv: float32 [768, 3, 768], P('fsdp', None, 'tp'), may hold values from -0.21875 to 0.21875
- w_attn: float32 [768, 768], P('tp', 'fsdp'), may hold values from -1.75 to 1.75
- w_up: float32 [768, 3072], P('fsdp', 'tp'), may hold values from -0.21875 to 0.21875
- w_down: float32 [3072, 768], P('tp', 'fsdp'), may hold values from -0.109375 to 0.109375
- norm_vectors: float32 [4, 768], replicated, may hold values from -0.8 to 1.5, as said below
- qkv_bias: float32 [3, 768], P(None, 'tp'), may hold values from -1 to 1
- up_bias: float32 [3072], P('tp'), may hold values from -1 to 1
- qkv_moment: float32 [768, 3, 768], P('fsdp', None, 'tp'), may hold values from -112 to 112
- attn_moment: float32 [768, 768], P('tp', 'fsdp'), may hold values from -80 to 80
- up_moment: float32 [768, 3072], P('fsdp', 'tp'), may hold values from -128 to 128
- down_moment: float32 [3072, 768], P('tp', 'fsdp'), may hold values from -256 to 256
- norm_moment: float32 [4, 768], replicated, may hold values from -256 to 256
- qbias_moment: float32 [3, 768], P(None, 'tp'), may hold values from -192 to 192
- ubias_moment: float32 [3072], P('tp'), may hold values from -128 to 128
- seq_lengths: int32 [2, 3], P('fsdp'), may hold values from 1024 to 2048, as said below
- block_source: int32 [2, 32], P('fsdp'), may hold values from 0 to 31, each once within a row
Outputs:
- mixed: bfloat16 [8192, 768], P(('fsdp', 'ctx'), 'tp')
- grad_tokens: float32 [8192, 768], P(('fsdp', 'ctx'), 'tp')
- mom_qkv: float32 [768, 3, 768], P('fsdp', None, 'tp')
- new_qkv: float32 [768, 3, 768], P(('fsdp', 'ctx'), None, 'tp')
- mom_attn: float32 [768, 768], P('tp', 'fsdp')
- new_attn: float32 [768, 768], P('tp', ('fsdp', 'ctx'))
- mom_up: float32 [768, 3072], P('fsdp', 'tp')
- new_up: float32 [768, 3072], P(('fsdp', 'ctx'), 'tp')
- mom_down: float32 [3072, 768], P('tp', 'fsdp')
- new_down: float32 [3072, 768], P('tp', ('fsdp', 'ctx'))
- mom_norm: float32 [4, 768], replicated
- new_norm: float32 [4, 768], replicated
- mom_qbias: float32 [3, 768], P(None, 'tp')
- new_qbias: float32 [3, 768], P(None, 'tp')
- mom_ubias: float32 [3072], P('tp')
- new_ubias: float32 [3072], P('tp')
Inputs may be any that keep to these rules, and one draw needn't show every extreme that they name: `seq_lengths`: each row holds the 3 lengths of one group's sequences in packed order; each row sums to 4096 and holds one length of exactly 2048. `block_source`: each row is a permutation of the 32 blocks of one group. `norm_vectors`: row 0 holds gains, rows 1 to 3 shifts and biases.
All inputs are finite; a program needn't handle non-finite values.
Results may differ from a plain program's by a relative error of at most 0.02.
Values may be sent and summed in bfloat16 or wider, within the bound.
No kernel may reach another device: no remote copies, remote signals or barrier semaphores. Data moves between devices by JAX's collectives and lax.ppermute only.
A program may use at most 320 MiB of HBM per device.

v0:
```python
from functools import partial
import math

import jax
import jax.numpy as jnp
from jax import lax
from jax.sharding import PartitionSpec as P

HD = 64
ROT = 16
BLK = 128
NS_STEPS = 5


HIGHEST = lax.Precision.HIGHEST
NS_COEF = (3.4445, -4.775, 2.0315)
NEG_BIG = -1e30


def for_sending(shard):

    def short(part):
        return part.astype(jnp.bfloat16) if part.dtype == jnp.float32 else part

    return jax.tree.map(short, shard)


def from_root(shard, axis, root):
    mine = lax.axis_index(axis) == root
    return lax.psum(jnp.where(mine, shard, jnp.zeros_like(shard)), axis)


def rotary_tables(places):
    exponent = jnp.arange(0, ROT, 2, dtype=jnp.float32) / ROT
    frequency = 1.0 / 10000.0**exponent
    angles = places.astype(jnp.float32)[:, None] * frequency[None, :]
    return (jnp.cos(angles)[:, None, :], jnp.sin(angles)[:, None, :])


def rotate(matrix, cosine, sine_tab):
    half_rot = ROT // 2
    first_half = matrix[..., :half_rot]
    second_half = matrix[..., half_rot:ROT]
    return jnp.concatenate(
        [
            first_half * cosine - second_half * sine_tab,
            second_half * cosine + first_half * sine_tab,
            matrix[..., ROT:],
        ],
        axis=-1,
    )


def slot_layout(first_slot, count, block_row, length_row):
    slots = first_slot + jnp.arange(count, dtype=jnp.int32)
    chosen = (slots // BLK)[:, None] == jnp.arange(block_row.shape[0], dtype=jnp.int32)[None, :]
    source = jnp.sum(jnp.where(chosen, block_row[None, :], 0), axis=1)
    placed = source * BLK + slots % BLK
    seq_ends = jnp.cumsum(length_row)
    starts = seq_ends - length_row
    sequence = jnp.sum((placed[:, None] >= seq_ends[None, :]).astype(jnp.int32), axis=1)
    picked = sequence[:, None] == jnp.arange(length_row.shape[0], dtype=jnp.int32)[None, :]
    offset = jnp.sum(jnp.where(picked, starts[None, :], 0), axis=1)
    return (placed, sequence, placed - offset)


def orthogonalize(matrix):
    is_tall = matrix.shape[0] > matrix.shape[1]
    current = matrix.T if is_tall else matrix
    current = current / (jnp.sqrt(jnp.sum(current * current)) + 1e-07)
    for repeat in range(NS_STEPS):
        gram_mat = jnp.dot(current, current.T, precision=HIGHEST)
        poly_mat = NS_COEF[1] * gram_mat + NS_COEF[2] * jnp.dot(
            gram_mat, gram_mat, precision=HIGHEST
        )
        current = NS_COEF[0] * current + jnp.dot(poly_mat, current, precision=HIGHEST)
    return current.T if is_tall else current


def join_tp_rows(stacked, fsdp_count, tp_count):
    grid = stacked.reshape(fsdp_count, tp_count, stacked.shape[1], stacked.shape[2])
    return jnp.transpose(grid, (1, 2, 0, 3)).reshape(
        tp_count * stacked.shape[1], fsdp_count * stacked.shape[2]
    )


def join_fsdp_rows(stacked, fsdp_count, tp_count):
    grid = stacked.reshape(fsdp_count, tp_count, stacked.shape[1], stacked.shape[2])
    return jnp.transpose(grid, (0, 2, 1, 3)).reshape(
        fsdp_count * stacked.shape[1], tp_count * stacked.shape[2]
    )


def body(
    tokens,
    cotangent,
    w_qkv,
    w_attn,
    w_up,
    w_down,
    norm_vectors,
    qkv_bias,
    up_bias,
    qkv_moment,
    attn_moment,
    up_moment,
    down_moment,
    norm_moment,
    qbias_moment,
    ubias_moment,
    seq_lengths,
    block_source,
):
    row_count = tokens.shape[0]
    half_width = tokens.shape[1]
    tp_count = lax.axis_size("tp")
    fsdp_count = lax.axis_size("fsdp")
    ctx_count = lax.axis_size("ctx")
    tp_index = lax.axis_index("tp")
    fsdp_index = lax.axis_index("fsdp")
    ctx_index = lax.axis_index("ctx")
    width = half_width * tp_count
    heads_here = half_width // HD
    scale = HD ** (-0.5)
    block_row = block_source[0]
    length_row = seq_lengths[0]
    shaped = (row_count, heads_here, HD)
    full_tokens, full_cotangent = (
        lax.all_gather(tokens, "tp", axis=1, tiled=True),
        lax.all_gather(cotangent, "tp", axis=1, tiled=True),
    )
    qkv_full, attn_full, up_full, down_full = (
        lax.all_gather(w_qkv.astype(jnp.bfloat16), "fsdp", axis=0, tiled=True),
        lax.all_gather(w_attn.astype(jnp.bfloat16), "fsdp", axis=1, tiled=True),
        lax.all_gather(w_up.astype(jnp.bfloat16), "fsdp", axis=0, tiled=True),
        lax.all_gather(w_down.astype(jnp.bfloat16), "fsdp", axis=1, tiled=True),
    )
    inputs = full_tokens.astype(jnp.float32)
    row_mean = jnp.mean(inputs, axis=1, keepdims=True)
    centered = inputs - row_mean
    inv_std = lax.rsqrt(jnp.mean(centered * centered, axis=1, keepdims=True) + 1e-05)
    normed = centered * inv_std
    norm_out = (normed * norm_vectors[0] + norm_vectors[1]).astype(jnp.bfloat16)
    projected = (
        jnp.einsum("nd,dch->nch", norm_out, qkv_full, preferred_element_type=jnp.float32)
        + qkv_bias[None]
    )
    q_placed, q_sequence, q_places = slot_layout(
        ctx_index * row_count, row_count, block_row, length_row
    )
    cosine, sine_tab = rotary_tables(q_places)
    queries = rotate(projected[:, 0].reshape(shaped), cosine, sine_tab).astype(jnp.bfloat16)
    key_flat = (
        rotate(projected[:, 1].reshape(shaped), cosine, sine_tab)
        .astype(jnp.bfloat16)
        .reshape(row_count, half_width)
    )
    value_flat = projected[:, 2].astype(jnp.bfloat16)

    def masked_scores(key_block, key_placed, key_seq):
        scores = (
            jnp.einsum("qhd,khd->hqk", queries, key_block, preferred_element_type=jnp.float32)
            * scale
        )
        allowed = (
            (q_sequence[:, None] == key_seq[None, :]) & (key_placed[None, :] <= q_placed[:, None])
        )[None]
        return (jnp.where(allowed, scores, NEG_BIG), allowed)

    def grouped_keys(key_part, value_part, first_slot):
        count = key_part.shape[0]
        step_rows = math.gcd(count, 512)
        k_placed, k_sequence, unused = slot_layout(first_slot, count, block_row, length_row)
        return (
            key_part.reshape(count // step_rows, step_rows, heads_here, HD),
            value_part.reshape(count // step_rows, step_rows, heads_here, HD),
            k_placed.reshape(count // step_rows, step_rows),
            k_sequence.reshape(count // step_rows, step_rows),
        )

    start_state = (
        jnp.full((heads_here, row_count), NEG_BIG, jnp.float32),
        jnp.zeros((heads_here, row_count), jnp.float32),
        jnp.zeros((heads_here, row_count, HD), jnp.float32),
    )

    def one_block(inner, block_in):
        row_max, row_sum, out_acc = inner
        key_block, value_block, key_placed, key_seq = block_in
        scores, allowed = masked_scores(key_block, key_placed, key_seq)
        new_max = jnp.maximum(row_max, jnp.max(scores, axis=2))
        weights = jnp.where(allowed, jnp.exp(scores - new_max[:, :, None]), 0.0)
        fade = jnp.exp(row_max - new_max)
        row_sum = row_sum * fade + jnp.sum(weights, axis=2)
        out_acc = out_acc * fade[:, :, None] + jnp.einsum(
            "hqk,khd->hqd",
            weights.astype(jnp.bfloat16),
            value_block,
            preferred_element_type=jnp.float32,
        )
        return ((new_max, row_sum, out_acc), None)

    result, unused = lax.scan(
        one_block,
        start_state,
        grouped_keys(
            lax.all_gather(key_flat, "ctx", axis=0, tiled=True),
            lax.all_gather(value_flat, "ctx", axis=0, tiled=True),
            jnp.int32(0),
        ),
    )
    row_max, row_sum, out_acc = result
    attended = jnp.transpose(out_acc / row_sum[:, :, None], (1, 0, 2))
    log_sum = row_max + jnp.log(row_sum)
    attended_low = attended.reshape(row_count, half_width).astype(jnp.bfloat16)
    hidden = jnp.dot(norm_out, up_full, preferred_element_type=jnp.float32) + up_bias
    gelu_exact = partial(jax.nn.gelu, approximate=False)
    activated, gelu_pull = jax.vjp(gelu_exact, hidden)
    activated_low = activated.astype(jnp.bfloat16)
    partial_out = jnp.dot(attended_low, attn_full, preferred_element_type=jnp.float32) + jnp.dot(
        activated_low, down_full, preferred_element_type=jnp.float32
    )
    mixed_part = lax.psum_scatter(
        partial_out.astype(jnp.bfloat16), "tp", scatter_dimension=1, tiled=True
    ).astype(jnp.float32)
    out_bias = norm_vectors[2] + norm_vectors[3]
    mixed = (
        tokens.astype(jnp.float32)
        + mixed_part
        + lax.dynamic_slice_in_dim(out_bias, tp_index * half_width, half_width)
    ).astype(jnp.bfloat16)
    grad_attn = jnp.einsum(
        "nd,ne->de", attended_low, full_cotangent, preferred_element_type=jnp.float32
    )
    grad_down = jnp.einsum(
        "nf,ne->fe", activated_low, full_cotangent, preferred_element_type=jnp.float32
    )
    grad_outbias = jnp.sum(full_cotangent.astype(jnp.float32), axis=0)
    d_attended = (
        jnp.einsum("ne,de->nd", full_cotangent, attn_full, preferred_element_type=jnp.float32)
        .astype(jnp.bfloat16)
        .reshape(shaped)
    )
    d_activated = jnp.einsum(
        "ne,fe->nf", full_cotangent, down_full, preferred_element_type=jnp.float32
    )
    d_hidden = gelu_pull(d_activated)[0].astype(jnp.bfloat16)
    all_keys, all_values = (
        lax.all_gather(key_flat, "ctx", axis=0, tiled=True),
        lax.all_gather(value_flat, "ctx", axis=0, tiled=True),
    )
    total_keys = all_keys.shape[0]
    delta = jnp.einsum("qhd,qhd->hq", d_attended.astype(jnp.float32), attended)

    def score_grads(key_block, value_block, key_placed, key_seq):
        scores, allowed = masked_scores(key_block, key_placed, key_seq)
        probs_full = jnp.where(allowed, jnp.exp(scores - log_sum[:, :, None]), 0.0)
        grad_prob = jnp.einsum(
            "qhd,khd->hqk", d_attended, value_block, preferred_element_type=jnp.float32
        )
        grad_score = (probs_full * (grad_prob - delta[:, :, None])).astype(jnp.bfloat16)
        return (probs_full, grad_score)

    def back_block(grad_query, block_in):
        key_block, value_block, key_placed, key_seq = block_in
        probs_full, grad_score = score_grads(key_block, value_block, key_placed, key_seq)
        grad_query = (
            grad_query
            + jnp.einsum("hqk,khd->qhd", grad_score, key_block, preferred_element_type=jnp.float32)
            * scale
        )
        grad_key = (
            jnp.einsum("hqk,qhd->khd", grad_score, queries, preferred_element_type=jnp.float32)
            * scale
        )
        grad_value = jnp.einsum(
            "hqk,qhd->khd",
            probs_full.astype(jnp.bfloat16),
            d_attended,
            preferred_element_type=jnp.float32,
        )
        return (grad_query, (grad_key, grad_value))

    grad_query, key_terms = lax.scan(
        back_block, jnp.zeros(shaped, jnp.float32), grouped_keys(all_keys, all_values, 0)
    )
    grad_keys = key_terms[0].reshape(total_keys, half_width)
    grad_values = key_terms[1].reshape(total_keys, half_width)
    own_keys, own_values = (
        lax.psum_scatter(
            grad_keys.astype(jnp.bfloat16), "ctx", scatter_dimension=0, tiled=True
        ).astype(jnp.float32),
        lax.psum_scatter(
            grad_values.astype(jnp.bfloat16), "ctx", scatter_dimension=0, tiled=True
        ).astype(jnp.float32),
    )
    grad_q = rotate(grad_query, cosine, -sine_tab).astype(jnp.bfloat16)
    grad_k = rotate(own_keys.reshape(shaped), cosine, -sine_tab).astype(jnp.bfloat16)
    grad_v = own_values.astype(jnp.bfloat16).reshape(shaped)
    grad_proj = jnp.stack([grad_q, grad_k, grad_v], axis=1).reshape(row_count, 3, half_width)
    grad_qkv = jnp.einsum("nd,nch->dch", norm_out, grad_proj, preferred_element_type=jnp.float32)
    grad_qbias = jnp.sum(grad_proj.astype(jnp.float32), axis=0)
    grad_up = jnp.einsum("nd,nf->df", norm_out, d_hidden, preferred_element_type=jnp.float32)
    grad_ubias = jnp.sum(d_hidden.astype(jnp.float32), axis=0)
    norm_part = jnp.einsum(
        "nch,dch->nd", grad_proj, qkv_full, preferred_element_type=jnp.float32
    ) + jnp.einsum("nf,df->nd", d_hidden, up_full, preferred_element_type=jnp.float32)
    grad_norm = lax.psum(norm_part.astype(jnp.bfloat16), "tp").astype(jnp.float32)
    grad_gain = jnp.sum(grad_norm * normed, axis=0)
    grad_shift = jnp.sum(grad_norm, axis=0)
    scaled = grad_norm * norm_vectors[0]
    grad_inputs = full_cotangent.astype(jnp.float32) + inv_std * (
        scaled
        - jnp.mean(scaled, axis=1, keepdims=True)
        - normed * jnp.mean(scaled * normed, axis=1, keepdims=True)
    )
    grad_tokens = lax.dynamic_slice_in_dim(grad_inputs, tp_index * half_width, half_width, 1)
    part_qkv, part_attn, part_up, part_down = (
        lax.psum_scatter(
            grad_qkv.astype(jnp.bfloat16), "fsdp", scatter_dimension=0, tiled=True
        ).astype(jnp.float32),
        lax.psum_scatter(
            grad_attn.astype(jnp.bfloat16), "fsdp", scatter_dimension=1, tiled=True
        ).astype(jnp.float32),
        lax.psum_scatter(
            grad_up.astype(jnp.bfloat16), "fsdp", scatter_dimension=0, tiled=True
        ).astype(jnp.float32),
        lax.psum_scatter(
            grad_down.astype(jnp.bfloat16), "fsdp", scatter_dimension=1, tiled=True
        ).astype(jnp.float32),
    )
    sum_qkv, sum_attn, sum_up, sum_down = (
        lax.psum(part_qkv.astype(jnp.bfloat16), "ctx").astype(jnp.float32),
        lax.psum(part_attn.astype(jnp.bfloat16), "ctx").astype(jnp.float32),
        lax.psum(part_up.astype(jnp.bfloat16), "ctx").astype(jnp.float32),
        lax.psum(part_down.astype(jnp.bfloat16), "ctx").astype(jnp.float32),
    )
    grad_vectors = jnp.stack([grad_gain, grad_shift, grad_outbias, grad_outbias])
    sum_vectors, sum_qbias, sum_ubias = lax.psum(
        (grad_vectors, grad_qbias, grad_ubias), ("fsdp", "ctx")
    )
    fresh = (
        0.95 * qkv_moment + sum_qkv,
        0.95 * attn_moment + sum_attn,
        0.95 * up_moment + sum_up,
        0.95 * down_moment + sum_down,
    )
    stack_qkv, stack_attn, stack_up, stack_down = (
        lax.all_gather(
            fresh[0][None].astype(jnp.bfloat16), ("fsdp", "tp"), axis=0, tiled=True
        ).astype(jnp.float32),
        lax.all_gather(
            fresh[1][None].astype(jnp.bfloat16), ("fsdp", "tp"), axis=0, tiled=True
        ).astype(jnp.float32),
        lax.all_gather(
            fresh[2][None].astype(jnp.bfloat16), ("fsdp", "tp"), axis=0, tiled=True
        ).astype(jnp.float32),
        lax.all_gather(
            fresh[3][None].astype(jnp.bfloat16), ("fsdp", "tp"), axis=0, tiled=True
        ).astype(jnp.float32),
    )
    qkv_rows, qkv_cols = (fresh[0].shape[0], fresh[0].shape[2])
    qkv_grid = stack_qkv.reshape(fsdp_count, tp_count, qkv_rows, 3, qkv_cols)
    whole_qkv = jnp.transpose(qkv_grid, (0, 2, 3, 1, 4)).reshape(width, 3 * width)
    wholes = (
        whole_qkv,
        join_tp_rows(stack_attn, fsdp_count, tp_count),
        join_fsdp_rows(stack_up, fsdp_count, tp_count),
        join_tp_rows(stack_down, fsdp_count, tp_count),
    )
    fan_ins = (width, width // 64, width, up_full.shape[1] * tp_count)
    olds = (w_qkv, w_attn, w_up, w_down)
    updated = []
    for matrix_id in range(4):
        owner_index = matrix_id * ctx_count // 4
        orthogonal = lax.cond(
            ctx_index == owner_index, orthogonalize, jnp.zeros_like, wholes[matrix_id]
        )
        old_shape = olds[matrix_id].shape
        if matrix_id == 0:
            own_piece = lax.dynamic_slice(
                orthogonal.reshape(width, 3, width),
                (fsdp_index * old_shape[0], 0, tp_index * old_shape[2]),
                old_shape,
            )
        elif matrix_id == 2:
            own_piece = lax.dynamic_slice(
                orthogonal, (fsdp_index * old_shape[0], tp_index * old_shape[1]), old_shape
            )
        else:
            own_piece = lax.dynamic_slice(
                orthogonal, (tp_index * old_shape[0], fsdp_index * old_shape[1]), old_shape
            )
        own_piece = from_root(for_sending(own_piece), "ctx", owner_index).astype(own_piece.dtype)
        rate = 0.5 * math.sqrt(max(wholes[matrix_id].shape) / fan_ins[matrix_id])
        new_shard = olds[matrix_id] - rate * own_piece
        cut_dim = 0 if matrix_id in (0, 2) else 1
        slice_size = old_shape[cut_dim] // ctx_count
        updated.append(
            lax.dynamic_slice_in_dim(new_shard, ctx_index * slice_size, slice_size, cut_dim)
        )
    vector_rate = 0.3 / math.sqrt(row_count * fsdp_count * ctx_count)
    mom_norm = 0.9 * norm_moment + sum_vectors
    mom_qbias = 0.9 * qbias_moment + sum_qbias
    mom_ubias = 0.9 * ubias_moment + sum_ubias
    return (
        mixed,
        grad_tokens,
        fresh[0],
        updated[0],
        fresh[1],
        updated[1],
        fresh[2],
        updated[2],
        fresh[3],
        updated[3],
        mom_norm,
        norm_vectors - vector_rate * mom_norm,
        mom_qbias,
        qkv_bias - vector_rate * mom_qbias,
        mom_ubias,
        up_bias - vector_rate * mom_ubias,
    )


def solution(mesh):
    return jax.shard_map(
        body,
        mesh=mesh,
        in_specs=(
            P(("fsdp", "ctx"), "tp"),
            P(("fsdp", "ctx"), "tp"),
            P("fsdp", None, "tp"),
            P("tp", "fsdp"),
            P("fsdp", "tp"),
            P("tp", "fsdp"),
            P(),
            P(None, "tp"),
            P("tp"),
            P("fsdp", None, "tp"),
            P("tp", "fsdp"),
            P("fsdp", "tp"),
            P("tp", "fsdp"),
            P(),
            P(None, "tp"),
            P("tp"),
            P("fsdp", None),
            P("fsdp", None),
        ),
        out_specs=(
            P(("fsdp", "ctx"), "tp"),
            P(("fsdp", "ctx"), "tp"),
            P("fsdp", None, "tp"),
            P(("fsdp", "ctx"), None, "tp"),
            P("tp", "fsdp"),
            P("tp", ("fsdp", "ctx")),
            P("fsdp", "tp"),
            P(("fsdp", "ctx"), "tp"),
            P("tp", "fsdp"),
            P("tp", ("fsdp", "ctx")),
            P(),
            P(),
            P(None, "tp"),
            P(None, "tp"),
            P("tp"),
            P("tp"),
        ),
        check_vma=False,
    )
```

profile of v0, /device:TPU:0, one launch (start us, length us, event | category | flops | bytes accessed | tf_op | source)
XLA Modules:
  0.0 1480.9 jit_solution(16304708919996624268)
XLA Ops:
  14.8 27.5 %all-gather.15.cloned.1.call-done = bf16[768,3,384]{0,2,1:T(8,128)(2,1)} async-done(((bf16[384,3,384]{0,2,1:T(8,128)(2,1)}), bf16[768,3,384]{0,2,1:T(8,128)(2,1)}) %all-gather.15.cloned.1.call-update) | async-done | bytes 1769488 | tf_op jit(solution)/shard_map/all_gather | solution.py:133
  56.0 9.9 all_gather.42
  66.9 43.4 %all-gather.17.cloned.1.call-done = bf16[4096,384]{0,1:T(8,128)(2,1)} async-done(((bf16[512,384]{0,1:T(8,128)(2,1)}), bf16[4096,384]{0,1:T(8,128)(2,1)}) %all-gather.17.cloned.1.call-update) | async-done | bytes 3145744 | tf_op jit(solution)/shard_map/all_gather | solution.py:207
  116.4 57.8 %all-gather.23.cloned.1.call-done = bf16[4096,1,384]{0,2,1:T(8,128)(2,1)} async-done(((bf16[512,1,384]{0,2,1:T(8,128)(2,1)}), bf16[4096,1,384]{0,2,1:T(8,128)(2,1)}) %all-gather.23.cloned.1.call-update) | async-done | bytes 3145744 | tf_op jit(solution)/shard_map/all_gather | solution.py:208
  180.3 102.0 %while.30 = (s32[]{:T(128)}, f32[6,512]{1,0:T(8,128)S(1)}, f32[6,512]{1,0:T(8,128)S(1)}, f32[6,512,64]{1,2,0:T(8,128)S(1)}, s32[512]{0:T(512)S(1)}, /*index=5*/s...) while((s32[]{:T(128)}, f32[6,512]{1,0:T(8,128)S(1)}, ...), condition=%wide.region_11.12_spmd.clone, body=%wide.region_8.11_spmd.clone.sunk | while | flops 424492032 | bytes 48054456 | solution.py:203
  180.8 4.9 fusion.450
  185.7 4.4 fusion.451
  193.6 4.8 fusion.450
  198.4 4.4 fusion.451
  206.3 4.8 fusion.450
  211.2 4.4 fusion.451
  219.0 4.9 fusion.450
  223.9 4.4 fusion.451
  231.8 4.8 fusion.450
  236.6 4.4 fusion.451
  244.5 4.8 fusion.450
  249.4 4.4 fusion.451
  257.2 4.8 fusion.450
  262.1 4.4 fusion.451
  269.9 4.8 fusion.450
  274.8 4.4 fusion.451
  284.5 122.5 %while.31 = (s32[]{:T(128)}, f32[512,6,64]{0,2,1:T(8,128)}, bf16[8,512,6,64]{1,3,2,0:T(8,128)(2,1)}, bf16[8,512,6,64]{1,3,2,0:T(8,128)(2,1)}, bf16[8,512,6,64]{1...) while((s32[]{:T(128)}, f32[512,6,64]{0,2,1:T(8,128)}, ...), condition=%wide.region_14.15_spmd.clone, body=%wide.region_13.14_spmd.clone.sunk | while | flops 1027080192 | bytes 91034176 | solution.py:284
  332.6 4.1 fusion.465
  423.0 4.9 convolution_add_fusion
  427.9 11.9 convert_reduce_fusion
  444.5 4.3 copy.152
  451.4 4.4 convolution_convert_fusion.1
  457.0 30.7 %reduce-scatter.14.cloned.1.call-done = bf16[512,384]{0,1:T(8,128)(2,1)} async-done(((bf16[4096,384]{0,1:T(8,128)(2,1)}), bf16[512,384]{0,1:T(8,128)(2,1)}) %reduce-scatter.14.cloned.1.call-update) | async-done | bytes 393232 | tf_op jit(solution)/shard_map/reduce_scatter | solution.py:290
  490.3 74.6 %reduce-scatter.16.cloned.1.call-done = bf16[512,384]{1,0:T(8,128)(2,1)} async-done(((bf16[4096,384]{1,0:T(8,128)(2,1)}), bf16[512,384]{1,0:T(8,128)(2,1)}) %reduce-scatter.16.cloned.1.call-update) | async-done | bytes 393232 | tf_op jit(solution)/shard_map/reduce_scatter | solution.py:293
  568.6 32.9 %reduce-scatter.26.cloned.1.call-done = bf16[384,1536]{1,0:T(8,128)(2,1)} async-done(((bf16[768,1536]{1,0:T(8,128)(2,1)}), bf16[384,1536]{1,0:T(8,128)(2,1)}) %reduce-scatter.26.cloned.1.call-update) | async-done | bytes 1179664
  603.9 15.9 %reduce-scatter.24.cloned.1.call-done = bf16[384,384]{1,0:T(8,128)(2,1)} async-done(((bf16[768,384]{1,0:T(8,128)(2,1)}), bf16[384,384]{1,0:T(8,128)(2,1)}) %reduce-scatter.24.cloned.1.call-update) | async-done | bytes 294928
  621.6 35.6 %reduce-scatter.20.cloned.1.call-done = bf16[384,1536]{1,0:T(8,128)(2,1)} async-done(((bf16[768,1536]{1,0:T(8,128)(2,1)}), bf16[384,1536]{1,0:T(8,128)(2,1)}) %reduce-scatter.20.cloned.1.call-update) | async-done | bytes 1179664 | tf_op jit(solution)/shard_map/reduce_scatter | solution.py:325
  657.2 31.2 %reduce-scatter.18.cloned.1.call-done = bf16[384,3,384]{2,0,1:T(8,128)(2,1)} async-done(((bf16[768,3,384]{2,0,1:T(8,128)(2,1)}), bf16[384,3,384]{2,0,1:T(8,128)(2,1)}) %reduce-scatter.18.cloned.1.call-update) | async-done | bytes 884752 | tf_op jit(solution)/shard_map/reduce_scatter | solution.py:319
  688.5 145.4 %all-reduce.11.cloned.1.call-done = (bf16[384,3,384]{2,0,1:T(8,128)(2,1)}, bf16[384,384]{1,0:T(8,128)(2,1)}, bf16[384,1536]{1,0:T(8,128)(2,1)}, bf16[1536,384]{1,0:T(8,128)(2,1)}) async-done(((bf16[384,3,384]{2,0,1:T(8,128)(2,1)}, bf16[384,384]{1,0:T(8,128)(2,1)}, bf16[384,1536]{1,0:T(8,128)(2,1)}, bf16[1536,384]{1,0:T(8,128)(2,1)}), (bf16[384,3,384]{2,0,1:T(8,128)(2,1)}, bf16[384,384]{1,0:T(8,128)(2,1)}, ...) | async-done | bytes 3538960 | tf_op jit(solution)/shard_map/psum | solution.py:333
  839.5 4.4 fusion.266
  862.0 8.0 conditional.5
  870.8 14.0 all-gather.25.cloned.1.call-done
  884.8 8.6 copy.172
  893.3 255.8 %conditional.4 = (bf16[768,3,768]{2,0,1:T(8,128)(2,1)}) conditional(s32[]{:T(128)} %convert_element_type.261, () %tuple.44, f32[2,384,3,2,384]{4,3,2,1,0:T(2,128)} %bitcast.388), branch_computations={%region_22.23_spmd, %region_23.25_spmd} | conditional | flops 190287249408 | bytes 239468608 | solution.py:376
  893.3 11.9 multiply_reduce_fusion
  905.9 8.4 broadcast_divide_fusion
  914.3 10.0 div.69
  924.4 20.9 %fusion.270 = f32[768,768]{1,0:T(8,128)S(1)} fusion(f32[768,2304]{1,0:T(8,128)} %div.69), kind=kOutput, calls=%fused_computation.415 | convolution fusion | flops 16307453952 | bytes 9437184 | tf_op jit(solution)/shard_map/cond/branch_1_fun/dot_general | solution.py:72
  945.3 6.0 fusion.271
  951.3 18.1 %multiply_add_fusion.4 = f32[768,2304]{1,0:T(8,128)S(1)} fusion(f32[768,2304]{1,0:T(8,128)S(1)} %copy-done.16, f32[768,768]{1,0:T(8,128)S(1)} %fusion.271, f32[768,768]{1,0:T(8,128)S(1)} %fusion.270), kind=kOutput, calls=%fused_computation.4 | convolution fusion | flops 16312762368 | bytes 18874368 | tf_op jit(solution)/shard_map/cond/branch_1_fun/dot_general | solution.py:76
  969.3 18.4 %fusion.272 = f32[768,768]{1,0:T(8,128)S(1)} fusion(f32[768,2304]{1,0:T(8,128)S(1)} %multiply_add_fusion.4), kind=kOutput, calls=%fused_computation.417 | convolution fusion | flops 16307453952 | bytes 9437184 | tf_op jit(solution)/shard_map/cond/branch_1_fun/dot_general | solution.py:72
  987.8 6.0 fusion.273
  993.8 18.1 %multiply_add_fusion.3 = f32[768,2304]{1,0:T(8,128)S(1)} fusion(f32[768,2304]{1,0:T(8,128)S(1)} %multiply_add_fusion.4, f32[768,768]{1,0:T(8,128)S(1)} %fusion.273, f32[768,768]{1,0:T(8,128)S(1)} %fusion.272), kind=kOutput, calls=%fused_computation.3 | convolution fusion | flops 16312762368 | bytes 18874368 | tf_op jit(solution)/shard_map/cond/branch_1_fun/dot_general | solution.py:76
  1011.8 18.4 %fusion.274 = f32[768,768]{1,0:T(8,128)S(1)} fusion(f32[768,2304]{1,0:T(8,128)S(1)} %multiply_add_fusion.3), kind=kOutput, calls=%fused_computation.419 | convolution fusion | flops 16307453952 | bytes 9437184 | tf_op jit(solution)/shard_map/cond/branch_1_fun/dot_general | solution.py:72
  1030.3 6.0 fusion.275
  1036.3 18.1 %multiply_add_fusion.2 = f32[768,2304]{1,0:T(8,128)S(1)} fusion(f32[768,2304]{1,0:T(8,128)S(1)} %multiply_add_fusion.3, f32[768,768]{1,0:T(8,128)S(1)} %fusion.275, f32[768,768]{1,0:T(8,128)S(1)} %fusion.274), kind=kOutput, calls=%fused_computation.2 | convolution fusion | flops 16312762368 | bytes 18874368 | tf_op jit(solution)/shard_map/cond/branch_1_fun/dot_general | solution.py:76
  1054.3 18.2 %fusion.276 = f32[768,768]{1,0:T(8,128)S(1)} fusion(f32[768,2304]{1,0:T(8,128)S(1)} %multiply_add_fusion.2), kind=kOutput, calls=%fused_computation.421 | convolution fusion | flops 16307453952 | bytes 9437184 | tf_op jit(solution)/shard_map/cond/branch_1_fun/dot_general | solution.py:72
  1072.6 6.0 fusion.277
  1078.6 18.3 %multiply_add_fusion.1 = f32[768,2304]{1,0:T(8,128)S(1)} fusion(f32[768,2304]{1,0:T(8,128)S(1)} %multiply_add_fusion.2, f32[768,768]{1,0:T(8,128)S(1)} %fusion.277, f32[768,768]{1,0:T(8,128)S(1)} %fusion.276), kind=kOutput, calls=%fused_computation.1 | convolution fusion | flops 16312762368 | bytes 18874368 | tf_op jit(solution)/shard_map/cond/branch_1_fun/dot_general | solution.py:76
  1096.9 18.2 %fusion.278 = f32[768,768]{1,0:T(8,128)S(1)} fusion(f32[768,2304]{1,0:T(8,128)S(1)} %multiply_add_fusion.1), kind=kOutput, calls=%fused_computation.423 | convolution fusion | flops 16307453952 | bytes 9437184 | tf_op jit(solution)/shard_map/cond/branch_1_fun/dot_general | solution.py:72
  1115.1 6.0 fusion.279
  1121.1 19.4 %multiply_add_fusion = bf16[768,2304]{1,0:T(8,128)(2,1)} fusion(f32[768,2304]{1,0:T(8,128)S(1)} %multiply_add_fusion.1, f32[768,768]{1,0:T(8,128)S(1)} %fusion.279, f32[768,768]{1,0:T(8,128)S(1)} %fusion.278), kind=kOutput, calls=%fused_computation | convolution fusion | flops 16314531840 | bytes 15335424 | tf_op jit(solution)/shard_map/cond/branch_1_fun/dot_general | solution.py:76
  1140.4 4.5 copy.107
  1151.4 10.3 copy.171
  1161.7 13.2 copy.131
  1174.9 7.3 conditional.6
  1182.3 11.4 conditional.7
  1215.5 201.2 %all-reduce = (f32[4,768]{1,0:T(4,128)S(1)}, f32[3,384]{1,0:T(4,128)S(1)}, f32[1536]{0:T(1024)S(1)}) all-reduce(f32[4,768]{1,0:T(4,128)S(1)} %pad_maximum_fusion.5, f32[3,384]{1,0:T(4,128)S(1)} %convert_reduce_fusion.2, f32[1536]{0:T(1024)S(1)} %copy-done.67), channel_id=1, replica_groups=mesh['fsdp'=2,'ctx'=8,'tp'=2] {'fsdp','ctx'}, use_global_device_ids=true, to_apply=%region_47.48 | all-reduce | flops 5760 | bytes 46080 | tf_op jit(solution)/shard_map/psum | solution.py:339
  1421.1 46.2 %all-reduce.9.cloned.1.call-done = (bf16[384,3,384]{2,0,1:T(8,128)(2,1)}, bf16[384,384]{0,1:T(8,128)(2,1)}, bf16[384,1536]{1,0:T(8,128)(2,1)}, bf16[1536,384]{0,1:T(8,128)(2,1)}) async-done(((bf16[384,3,384]{2,0,1:T(8,128)(2,1)}, bf16[384,384]{0,1:T(8,128)(2,1)}, bf16[384,1536]{1,0:T(8,128)(2,1)}, bf16[1536,384]{0,1:T(8,128)(2,1)}), (bf16[384,3,384]{2,0,1:T(8,128)(2,1)}, bf16[384,384]{0,1:T(8,128)(2,1)}, ...) | async-done | bytes 3538960 | tf_op jit(solution)/shard_map/psum | solution.py:30
  (602 shorter events, 283.1 us)
Async XLA Ops:
  7.2 35.1 %all-gather.15.cloned.1.call-start = ((), (), s32[]{:S(2)}) async-start(), calls=%async_computation.7 | async-start | bytes 2654208 | tf_op jit(solution)/shard_map/all_gather | solution.py:133
  9.8 32.5 %copy-start.69 = (f32[3,384]{1,0:T(4,128)S(1)}, f32[3,384]{1,0:T(4,128)}, u32[]{:S(2)}) copy-start(f32[3,384]{1,0:T(4,128)} %param.37) | copy-start | bytes 13828
  9.8 100.5 %all-gather.17.cloned.1.call-start = ((), (), s32[]{:S(2)}) async-start(), calls=%async_computation.8 | async-start | bytes 3538944 | tf_op jit(solution)/shard_map/all_gather | solution.py:207
  10.2 34.9 %copy-start.76 = (s32[3,1]{0,1:T(1,128)}, s32[3,1]{0,1:T(1,128)S(1)}, u32[]{:S(2)}) copy-start(s32[3,1]{0,1:T(1,128)S(1)} %reduce-window.4) | copy-start | bytes 40
  12.8 32.3 %copy-start.13 = (bf16[512,768]{1,0:T(8,128)(2,1)}, bf16[512,768]{1,0:T(8,128)(2,1)S(1)}, u32[]{:S(2)}) copy-start(bf16[512,768]{1,0:T(8,128)(2,1)S(1)} %all_gather.38) | copy-start | bytes 2359300
  13.0 551.9 %copy-start.55 = (f32[512]{0:T(512)}, f32[512]{0:T(512)S(1)}, u32[]{:S(2)}) copy-start(f32[512]{0:T(512)S(1)} %broadcast_multiply_fusion.4) | copy-start | bytes 6148
  13.4 551.5 %copy-start.53 = (f32[512]{0:T(512)}, f32[512]{0:T(512)S(1)}, u32[]{:S(2)}) copy-start(f32[512]{0:T(512)S(1)} %add_rsqrt_fusion) | copy-start | bytes 6148
  14.0 31.1 %copy-start.60 = (f32[768]{0:T(1024)}, f32[768]{0:T(1024)S(1)}, u32[]{:S(2)}) copy-start(f32[768]{0:T(1024)S(1)} %get-tuple-element.363) | copy-start | bytes 9220
  14.0 31.1 %copy-start.72 = (f32[768]{0:T(1024)}, f32[768]{0:T(1024)S(1)}, u32[]{:S(2)}) copy-start(f32[768]{0:T(1024)S(1)} %get-tuple-element.364) | copy-start | bytes 9220
  14.8 30.5 %copy-start.44 = (f32[512,8]{0,1:T(8,128)}, f32[512,8]{0,1:T(8,128)S(1)}, u32[]{:S(2)}) copy-start(f32[512,8]{0,1:T(8,128)S(1)} %get-tuple-element.479) | copy-start | bytes 49156
  47.1 127.1 %all-gather.23.cloned.1.call-start = ((), (), s32[]{:S(2)}) async-start(), calls=%async_computation.16 | async-start | bytes 3538944 | tf_op jit(solution)/shard_map/all_gather | solution.py:208
  49.1 372.9 %all-gather.19.cloned.1.call-start = ((), (), s32[]{:S(2)}) async-start(), calls=%async_computation.9 | async-start | bytes 3538944 | tf_op jit(solution)/shard_map/all_gather | solution.py:135
  52.1 375.7 %all-gather.21.cloned.1.call-start = ((), (), s32[]{:S(2)}) async-start(), calls=%async_computation.10 | async-start | bytes 3538944 | tf_op jit(solution)/shard_map/all_gather | solution.py:136
  53.3 12.6 copy-start.75
  53.3 12.7 copy-start.77
  53.4 434.3 %reduce-scatter.14.cloned.1.call-start = ((), (), s32[]{:S(2)}) async-start(), calls=%async_computation.11 | async-start | bytes 3538944 | tf_op jit(solution)/shard_map/reduce_scatter | solution.py:290
  56.0 10.9 copy-start.10
  56.0 10.8 copy-start.42
  56.0 10.8 copy-start.43
  65.9 47.7 %copy-start.23 = (bf16[384,768]{1,0:T(8,128)(2,1)}, bf16[384,768]{1,0:T(8,128)(2,1)S(1)}, u32[]{:S(2)}) copy-start(bf16[384,768]{1,0:T(8,128)(2,1)S(1)} %all_gather.42) | copy-start | bytes 1769476
  236.6 4.6 copy-start
  262.1 4.6 copy-start
  306.2 4.8 copy-start.3
  321.5 4.8 copy-start.3
  336.7 4.8 copy-start.3
  352.1 4.8 copy-start.3
  367.4 4.8 copy-start.3
  382.7 4.8 copy-start.3
  398.0 4.8 copy-start.3
  413.9 151.0 %reduce-scatter.16.cloned.1.call-start = ((), (), s32[]{:S(2)}) async-start(), calls=%async_computation.12 | async-start | bytes 3538944 | tf_op jit(solution)/shard_map/reduce_scatter | solution.py:293
  421.9 6.0 copy-start.11
  421.9 179.6 %reduce-scatter.26.cloned.1.call-start = ((), (), s32[]{:S(2)}) async-start(), calls=%async_computation.23 | async-start | bytes 3538944
  427.9 11.9 copy-start.22
  448.8 171.0 %reduce-scatter.24.cloned.1.call-start = ((), (), s32[]{:S(2)}) async-start(), calls=%async_computation.22 | async-start | bytes 884736
  451.3 205.9 %reduce-scatter.20.cloned.1.call-start = ((), (), s32[]{:S(2)}) async-start(), calls=%async_computation.15 | async-start | bytes 3538944 | tf_op jit(solution)/shard_map/reduce_scatter | solution.py:325
  455.8 33.0 %copy-start.45 = (f32[512,8]{0,1:T(8,128)S(1)}, f32[512,8]{0,1:T(8,128)}, u32[]{:S(2)}) copy-start(f32[512,8]{0,1:T(8,128)} %copy-done.44) | copy-start | bytes 49156
  455.8 33.0 %copy-start.50 = (f32[512,8]{0,1:T(8,128)S(1)}, f32[512,8]{0,1:T(8,128)}, u32[]{:S(2)}) copy-start(f32[512,8]{0,1:T(8,128)} %get-tuple-element.477) | copy-start | bytes 49156
  455.8 232.6 %reduce-scatter.18.cloned.1.call-start = ((), (), s32[]{:S(2)}) async-start(), calls=%async_computation.14 | async-start | bytes 2654208 | tf_op jit(solution)/shard_map/reduce_scatter | solution.py:319
  490.1 367.0 %copy-start.26 = (bf16[512,1,384]{2,0,1:T(8,128)(2,1)}, bf16[512,1,384]{2,0,1:T(8,128)(2,1)S(1)}, u32[]{:S(2)}) copy-start(bf16[512,1,384]{2,0,1:T(8,128)(2,1)S(1)} %copy.122) | copy-start | bytes 1179652
  490.3 366.8 %copy-start.28 = (bf16[512,1,384]{2,0,1:T(8,128)(2,1)}, bf16[512,1,384]{2,0,1:T(8,128)(2,1)S(1)}, u32[]{:S(2)}) copy-start(bf16[512,1,384]{2,0,1:T(8,128)(2,1)S(1)} %copy.121) | copy-start | bytes 1179652
  568.5 265.3 %all-reduce.11.cloned.1.call-start = ((), (), s32[]{:S(2)}) async-start(), calls=%async_computation.25 | async-start | bytes 7077888 | tf_op jit(solution)/shard_map/psum | solution.py:333
  603.9 230.0 %copy-start.36 = (f32[384,384]{1,0:T(8,128)S(1)}, f32[384,384]{1,0:T(8,128)}, u32[]{:S(2)}) copy-start(f32[384,384]{1,0:T(8,128)} %param.40) | copy-start | bytes 1769476
  688.4 171.0 %all-gather.27.cloned.1.call-start = ((), (), s32[]{:S(2)}) async-start(), calls=%async_computation.18 | async-start | bytes 1474560 | tf_op jit(solution)/shard_map/all_gather | solution.py:352
  835.9 48.9 %all-gather.25.cloned.1.call-start = ((), (), s32[]{:S(2)}) async-start(), calls=%async_computation.17 | async-start | bytes 4423680 | tf_op jit(solution)/shard_map/all_gather | solution.py:349
  839.2 312.2 %all-gather.29.cloned.1.call-start = ((), (), s32[]{:S(2)}) async-start(), calls=%async_computation.19 | async-start | bytes 5898240 | tf_op jit(solution)/shard_map/all_gather | solution.py:355
  844.0 317.8 %all-gather.31.cloned.1.call-start = ((), (), s32[]{:S(2)}) async-start(), calls=%async_computation.20 | async-start | bytes 5898240 | tf_op jit(solution)/shard_map/all_gather | solution.py:358
  847.9 359.5 %reduce-scatter.22.cloned.1.call-start = ((), (), s32[]{:S(2)}) async-start(), calls=%async_computation.21 | async-start | bytes 1179648
  853.4 358.5 %all-reduce.7.cloned.1.call-start = ((), (), s32[]{:S(2)}) async-start(), calls=%async_computation.13 | async-start | bytes 1572864 | tf_op jit(solution)/shard_map/psum | solution.py:308
  859.3 608.0 %all-reduce.9.cloned.1.call-start = ((), (), s32[]{:S(2)}) async-start(), calls=%async_computation.24 | async-start | bytes 7077888 | tf_op jit(solution)/shard_map/psum | solution.py:30
  945.3 6.0 copy-start.16
  1199.9 6.8 copy-start.68
  1201.7 8.8 copy-start.27
  1204.4 7.6 copy-start.15
  1204.4 7.6 copy-start.54
  1204.4 7.6 copy-start.56
  1204.4 7.6 copy-start.62
  1211.8 204.9 %copy-start.70 = (f32[3,384]{1,0:T(4,128)S(1)}, f32[3,384]{1,0:T(4,128)}, u32[]{:S(2)}) copy-start(f32[3,384]{1,0:T(4,128)} %param.37) | copy-start | bytes 13828
  1211.8 204.9 %copy-start.71 = (f32[3,384]{1,0:T(4,128)S(1)}, f32[3,384]{1,0:T(4,128)}, u32[]{:S(2)}) copy-start(f32[3,384]{1,0:T(4,128)} %param.44) | copy-start | bytes 13828
  1211.8 205.5 %copy-start.65 = (f32[1536]{0:T(1024)S(1)}, f32[1536]{0:T(1024)}, u32[]{:S(2)}) copy-start(f32[1536]{0:T(1024)} %param.38) | copy-start | bytes 18436
  1211.9 205.5 %copy-start.66 = (f32[1536]{0:T(1024)S(1)}, f32[1536]{0:T(1024)}, u32[]{:S(2)}) copy-start(f32[1536]{0:T(1024)} %param.45) | copy-start | bytes 18436
  1211.9 206.1 %copy-start.52 = (f32[4,768]{1,0:T(4,128)S(1)}, f32[4,768]{1,0:T(4,128)}, u32[]{:S(2)}) copy-start(f32[4,768]{1,0:T(4,128)} %param.36) | copy-start | bytes 36868
  1211.9 206.1 %copy-start.63 = (f32[4,768]{1,0:T(4,128)S(1)}, f32[4,768]{1,0:T(4,128)}, u32[]{:S(2)}) copy-start(f32[4,768]{1,0:T(4,128)} %param.43) | copy-start | bytes 36868
  1215.4 255.3 %copy-start.41 = (f32[384,48]{0,1:T(8,128)S(1)}, f32[384,48]{0,1:T(8,128)}, u32[]{:S(2)}) copy-start(f32[384,48]{0,1:T(8,128)} %copy.158) | copy-start | bytes 221188
  1418.0 54.2 %copy-start.32 = (f32[1536,48]{0,1:T(8,128)S(1)}, f32[1536,48]{0,1:T(8,128)}, u32[]{:S(2)}) copy-start(f32[1536,48]{0,1:T(8,128)} %copy.159) | copy-start | bytes 884740
  (127 other events, 371.0 us)
Sparse Core Ops, SparseCore 0:
  10.2 32.1 all-gather.14
  47.2 63.0 all-gather.16
  112.9 61.2 all-gather.22
  176.2 34.2 all-gather.18
  212.4 36.0 all-gather.20
  414.0 73.6 reduce-scatter.13
  491.2 73.6 reduce-scatter.15
  567.7 33.7 reduce-scatter.25
  604.5 15.2 reduce-scatter.23
  622.5 34.7 reduce-scatter.19
  660.1 28.2 reduce-scatter.17
  693.4 140.4 all-reduce.10
  836.1 16.3 all-gather.26
  854.0 30.7 all-gather.24
  886.3 37.4 all-gather.28
  925.3 37.4 all-gather.30
  964.9 8.2 reduce-scatter.21
  975.4 20.3 all-reduce.6
  1198.8 268.4 all-reduce.8
where the time goes:
time: 1490 us; the launch traced here: 1480 us
  waiting for transfers between devices  556 us (37%)
  matrix products  437 us (29%)
  blocking collectives  216 us (14%)
  local copies, waits for them, and re-layouts  118 us (8%)
  other arithmetic  113 us (8%)
  loops' own time  24.8 us (2%)
  between operations  15.4 us (1%)
    psum x1, blocking collectives, body(): lax.psum((grad_vectors, grad_qbias, grad_ubias), ('fsdp', 'ctx'))  201 us
    psum x1, waiting for transfers between devices, body(): lax.psum(part_qkv.astype(jnp.bfloat16), 'ctx').astype(jnp.float32)  145 us
    dot_general x5, matrix products, orthogonalize(): gram_mat = jnp.dot(current, current.T, precision=HIGHEST)  94.2 us
    dot_general x5, matrix products, orthogonalize(): jnp.dot(poly_mat, current, precision=HIGHEST)  91.9 us
    reduce_scatter x1, waiting for transfers between devices, body(): lax.psum_scatter(grad_values.astype(jnp.bfloat16), 'ctx', scatter_dimensi...  74.6 us
    all_gather x1, waiting for transfers between devices, body(): lax.all_gather(value_flat, 'ctx', axis=0, tiled=True)  57.8 us
    dot_general x16, matrix products, masked_scores(): jnp.einsum('qhd,khd->hqk', queries, key_block, preferred_element_type=jnp...  56.2 us
    unnamed x22, waiting for transfers between devices  49.2 us
  transfers between devices with their start and end apart: 19, of which 12 were waited for; matrix products, arithmetic and copies ran while one was open for 43% of the time, Pallas kernels for 0%

commit v1 on v0

v1 whole, which is shorter than its diff:
```python
from functools import partial
import math

import jax
import jax.numpy as jnp
from jax import lax
from jax.experimental import pallas as pl
from jax.experimental.pallas import tpu as pltpu
from jax.sharding import PartitionSpec as P

HD = 64
ROT = 16
BLK = 128
NS_STEPS = 5
CHUNK = 512
MAX_LEN = 2048
SPAN = (MAX_LEN + BLK) // CHUNK + 2
OWNERS = 4
NS_COEF = (3.4445, -4.775, 2.0315)
NEG_BIG = -1e30
SCALE = HD**-0.5
LOW = jnp.bfloat16
WIDE = jnp.float32
NT = (((1,), (1,)), ((), ()))
VMEM_ASK = 56 * 1024 * 1024


def dot_nn(left, right):
    return jnp.dot(left, right, preferred_element_type=WIDE)


def dot_nt(left, right):
    return lax.dot_general(left, right, NT, preferred_element_type=WIDE)


def partner(value, axis, step):
    size = lax.axis_size(axis)
    return lax.ppermute(value, axis, [(i, i ^ step) for i in range(size)])


def sum_scatter(pieces, axis, stride, index):
    count = pieces.shape[0]
    total = lax.dynamic_index_in_dim(pieces, index, 0, keepdims=False)
    for step in range(1, count):
        piece = lax.dynamic_index_in_dim(pieces, index ^ step, 0, keepdims=False)
        total = total + partner(piece.astype(LOW), axis, step * stride).astype(WIDE)
    return total


def gather_axis(shard, axis, dim):
    if lax.axis_size(axis) != 2:
        return lax.all_gather(shard, axis, axis=dim, tiled=True)
    other = partner(shard, axis, 1)
    first = lax.axis_index(axis) == 0
    return jnp.concatenate(
        [jnp.where(first, shard, other), jnp.where(first, other, shard)], axis=dim
    )


def sum_everywhere(value, axes):
    for axis in axes:
        step = 1
        while step < lax.axis_size(axis):
            value = value + partner(value, axis, step)
            step *= 2
    return value


def turned(block, cosine, sine, lane):
    half = ROT // 2
    swapped = jnp.where(
        lane % HD < half, pltpu.roll(block, BLK - half, 1), pltpu.roll(block, half, 1)
    )
    return block * cosine + swapped * sine


def two_heads(block, lane):
    zero = jnp.zeros_like(block)
    return jnp.concatenate(
        [jnp.where(lane < HD, block, zero), jnp.where(lane < HD, zero, block)], axis=0
    )


def one_of_two(stacked, lane):
    return jnp.where(lane < HD, stacked[:BLK], stacked[BLK:])


def project_kernel(count, inv_ref, *refs):
    x_own, x_far = refs[:count], refs[count : 2 * count]
    g_own, g_far = refs[2 * count : 3 * count], refs[3 * count : 4 * count]
    (
        w_own,
        w_far,
        bias,
        vec_own,
        vec_far,
        a_own,
        a_far,
        cos_ref,
        sin_ref,
        q_out,
        k_out,
        v_out,
        d_out,
    ) = refs[4 * count :]

    def whole(parts):
        return jnp.concatenate([part[...] for part in parts], axis=0)

    own, far = whole(x_own).astype(WIDE), whole(x_far).astype(WIDE)
    half = own.shape[1]
    width = 2 * half
    mean = (
        jnp.sum(own, axis=1, keepdims=True) + jnp.sum(far, axis=1, keepdims=True)
    ) / width
    own, far = own - mean, far - mean
    var = (
        jnp.sum(own * own, axis=1, keepdims=True) + jnp.sum(far * far, axis=1, keepdims=True)
    ) / width
    inv_std = lax.rsqrt(var + 1e-5)
    own = (own * inv_std * vec_own[0:1] + vec_own[1:2]).astype(LOW)
    far = (far * inv_std * vec_far[0:1] + vec_far[1:2]).astype(LOW)
    rows = own.shape[0]
    lane = lax.broadcasted_iota(jnp.int32, (rows, BLK), 1)
    cosine, sine = cos_ref[...], sin_ref[...]
    for part, out in enumerate((q_out, k_out, v_out)):
        cut = slice(part * half, (part + 1) * half)
        made = dot_nn(own, w_own[:, cut]) + dot_nn(far, w_far[:, cut]) + bias[:, cut]
        for pair in range(half // BLK):
            lanes = slice(pair * BLK, (pair + 1) * BLK)
            block = made[:, lanes]
            if part < 2:
                block = turned(block, cosine, sine, lane)
            out[:, lanes] = block.astype(LOW)
    d_out[...] = (dot_nt(whole(g_own), a_own[...]) + dot_nt(whole(g_far), a_far[...])).astype(LOW)


def project_all(inverse, x_own, x_far, g_own, g_far, weights, cosine, sine):
    rows, half = x_own.shape
    count = CHUNK // BLK

    def picked(place):
        return pl.BlockSpec((BLK, half), lambda i, inv: (inv[i * count + place], 0))

    def fixed(array):
        return pl.BlockSpec(array.shape, lambda i, inv: (0,) * array.ndim)

    def chunk(width):
        return pl.BlockSpec((CHUNK, width), lambda i, inv: (i, 0))

    return pl.pallas_call(
        partial(project_kernel, count),
        grid_spec=pltpu.PrefetchScalarGridSpec(
            num_scalar_prefetch=1,
            grid=(rows // CHUNK,),
            in_specs=[picked(i) for i in range(count)] * 4
            + [fixed(w) for w in weights]
            + [chunk(BLK)] * 2,
            out_specs=[chunk(half)] * 4,
        ),
        out_shape=[jax.ShapeDtypeStruct((rows, half), LOW)] * 4,
        compiler_params=pltpu.CompilerParams(vmem_limit_bytes=VMEM_ASK),
        cost_estimate=pl.CostEstimate(
            flops=16 * rows * half * half, bytes_accessed=20 * rows * half, transcendentals=0
        ),
        name="project_all",
    )(
        inverse,
        *([x_own] * count),
        *([x_far] * count),
        *([g_own] * count),
        *([g_far] * count),
        *weights,
        cosine,
        sine,
    )


def lane_tiles(array, combine):
    total = array[:, :BLK]
    for i in range(1, array.shape[1] // BLK):
        total = combine(total, array[:, i * BLK : (i + 1) * BLK])
    return total


def query_kernel(
    blocks,
    first,
    last,
    q_ref,
    k_ref,
    v_ref,
    d_ref,
    cos_ref,
    sin_ref,
    start_ref,
    att_out,
    dq_out,
    stat_out,
    s_scr,
    p_scr,
    q_scr,
    d_scr,
    m_scr,
    l_scr,
    e_scr,
    o_scr,
):
    pairs = q_ref.shape[1] // BLK
    own = att_out.shape[0] // BLK
    lane = lax.broadcasted_iota(jnp.int32, (BLK, BLK), 1)

    def lanes(pair):
        return slice(pair * BLK, (pair + 1) * BLK)

    @pl.loop(0, own)
    def _(j):
        row0 = pl.multiple_of(blocks[j] * BLK, BLK)
        out0 = pl.multiple_of(j * BLK, BLK)
        lo = first[j]
        hi = last[j]
        for g in range(pairs):
            q_scr[g] = two_heads(q_ref[pl.ds(row0, BLK), lanes(g)].astype(WIDE), lane).astype(
                LOW
            ) * LOW(SCALE)
            d_scr[g] = two_heads(d_ref[pl.ds(row0, BLK), lanes(g)].astype(WIDE), lane).astype(LOW)
        m_scr[...] = jnp.full(m_scr.shape, NEG_BIG, WIDE)
        l_scr[...] = jnp.zeros(l_scr.shape, WIDE)
        e_scr[...] = jnp.zeros(e_scr.shape, WIDE)
        o_scr[...] = jnp.zeros(o_scr.shape, WIDE)
        starts = start_ref[pl.ds(out0, BLK), :]
        places = row0 + lax.broadcasted_iota(jnp.int32, (BLK, 1), 0)
        starts = jnp.concatenate([starts, starts], axis=0)
        places = jnp.concatenate([places, places], axis=0)

        @pl.loop(lo, hi)
        def _(c):
            key0 = pl.multiple_of(c * CHUNK, CHUNK)
            key_place = key0 + lax.broadcasted_iota(jnp.int32, (2 * BLK, CHUNK), 1)
            allowed = (key_place >= starts) & (key_place <= places)
            for g in range(pairs):
                scores = dot_nt(q_scr[g], k_ref[pl.ds(key0, CHUNK), lanes(g)])
                scores = jnp.where(allowed, scores, NEG_BIG)
                s_scr[g, c - lo] = scores
                m_scr[g] = jnp.maximum(m_scr[g], lane_tiles(scores, jnp.maximum))

        for g in range(pairs):
            m_scr[g] = jnp.broadcast_to(
                jnp.max(m_scr[g], axis=1, keepdims=True), (2 * BLK, BLK)
            )

        @pl.loop(lo, hi)
        def _(c):
            key0 = pl.multiple_of(c * CHUNK, CHUNK)
            for g in range(pairs):
                values = v_ref[pl.ds(key0, CHUNK), lanes(g)]
                top = m_scr[g]
                weights = jnp.exp(s_scr[g, c - lo] - jnp.concatenate([top] * (CHUNK // BLK), 1))
                l_scr[g] += lane_tiles(weights, jnp.add)
                o_scr[g] += dot_nn(weights.astype(LOW), values)
                grad_prob = dot_nt(d_scr[g], values)
                e_scr[g] += lane_tiles(weights * grad_prob, jnp.add)
                s_scr[g, c - lo] = weights
                p_scr[g, c - lo] = grad_prob

        for g in range(pairs):
            total = jnp.sum(l_scr[g], axis=1, keepdims=True)
            inverse = 1.0 / total
            delta = jnp.sum(e_scr[g], axis=1, keepdims=True) * inverse
            att_out[pl.ds(out0, BLK), lanes(g)] = one_of_two(o_scr[g] * inverse, lane).astype(LOW)
            log_sum = m_scr[g] + jnp.log(total)
            stat_out[j, 2 * g : 2 * g + 1, :] = log_sum[:BLK].T[0:1]
            stat_out[j, 2 * g + 1 : 2 * g + 2, :] = log_sum[BLK:].T[0:1]
            wide = jnp.broadcast_to(delta, (2 * BLK, BLK))
            base = stat_out.shape[1] // 2 + 2 * g
            stat_out[j, base : base + 1, :] = wide[:BLK].T[0:1]
            stat_out[j, base + 1 : base + 2, :] = wide[BLK:].T[0:1]
            l_scr[g] = jnp.broadcast_to(inverse, (2 * BLK, BLK))
            e_scr[g] = wide
        o_scr[...] = jnp.zeros(o_scr.shape, WIDE)

        @pl.loop(lo, hi)
        def _(c):
            key0 = pl.multiple_of(c * CHUNK, CHUNK)
            for g in range(pairs):
                wide = jnp.concatenate([e_scr[g]] * (CHUNK // BLK), 1)
                grad_score = s_scr[g, c - lo] * (p_scr[g, c - lo] - wide)
                o_scr[g] += dot_nn(grad_score.astype(LOW), k_ref[pl.ds(key0, CHUNK), lanes(g)])

        cosine = cos_ref[pl.ds(row0, BLK), :]
        sine = sin_ref[pl.ds(row0, BLK), :]
        for g in range(pairs):
            grad = one_of_two(o_scr[g] * l_scr[g], lane) * SCALE
            dq_out[pl.ds(out0, BLK), lanes(g)] = turned(grad, cosine, -sine, lane).astype(LOW)


def smem():
    return pl.BlockSpec(memory_space=pltpu.SMEM)


def vmem():
    return pl.BlockSpec(memory_space=pltpu.VMEM)


def query_side(blocks, first, last, queries, keys, values, grads, cosine, sine, starts):
    own = blocks.shape[0]
    width = queries.shape[1]
    pairs = width // BLK
    stat_rows = 16 * ((2 * pairs + 7) // 8)
    work = 2 * BLK * CHUNK
    return pl.pallas_call(
        query_kernel,
        in_specs=[smem()] * 3 + [vmem()] * 7,
        out_specs=[vmem()] * 3,
        out_shape=[
            jax.ShapeDtypeStruct((own * BLK, width), LOW),
            jax.ShapeDtypeStruct((own * BLK, width), LOW),
            jax.ShapeDtypeStruct((own, stat_rows, BLK), WIDE),
        ],
        scratch_shapes=[
            pltpu.VMEM((pairs, SPAN, 2 * BLK, CHUNK), WIDE),
            pltpu.VMEM((pairs, SPAN, 2 * BLK, CHUNK), WIDE),
            pltpu.VMEM((pairs, 2 * BLK, BLK), LOW),
            pltpu.VMEM((pairs, 2 * BLK, BLK), LOW),
            pltpu.VMEM((pairs, 2 * BLK, BLK), WIDE),
            pltpu.VMEM((pairs, 2 * BLK, BLK), WIDE),
            pltpu.VMEM((pairs, 2 * BLK, BLK), WIDE),
            pltpu.VMEM((pairs, 2 * BLK, BLK), WIDE),
        ],
        compiler_params=pltpu.CompilerParams(vmem_limit_bytes=VMEM_ASK),
        cost_estimate=pl.CostEstimate(
            flops=own * pairs * 4 * 4 * 2 * work * BLK,
            bytes_accessed=4 * keys.shape[0] * width * 2,
            transcendentals=own * pairs * 4 * work,
        ),
        name="query_side",
    )(blocks, first, last, queries, keys, values, grads, cosine, sine, starts)


def key_kernel(
    blocks,
    first,
    last,
    inverse,
    q_ref,
    k_ref,
    v_ref,
    d_ref,
    cos_ref,
    sin_ref,
    end_ref,
    stat_ref,
    dk_out,
    dv_out,
    k_scr,
    v_scr,
    dk_scr,
    dv_scr,
):
    pairs = q_ref.shape[1] // BLK
    own = dk_out.shape[0] // BLK
    half_stat = stat_ref.shape[1] // 2
    lane = lax.broadcasted_iota(jnp.int32, (BLK, BLK), 1)

    def lanes(pair):
        return slice(pair * BLK, (pair + 1) * BLK)

    @pl.loop(0, own)
    def _(j):
        row0 = pl.multiple_of(blocks[j] * BLK, BLK)
        out0 = pl.multiple_of(j * BLK, BLK)
        for g in range(pairs):
            k_scr[g] = two_heads(k_ref[pl.ds(row0, BLK), lanes(g)].astype(WIDE), lane).astype(
                LOW
            ) * LOW(SCALE)
            v_scr[g] = two_heads(v_ref[pl.ds(row0, BLK), lanes(g)].astype(WIDE), lane).astype(LOW)
        dk_scr[...] = jnp.zeros(dk_scr.shape, WIDE)
        dv_scr[...] = jnp.zeros(dv_scr.shape, WIDE)
        ends = end_ref[pl.ds(out0, BLK), :]
        places = row0 + lax.broadcasted_iota(jnp.int32, (BLK, 1), 0)

        @pl.loop(first[j], last[j])
        def _(c):
            query0 = pl.multiple_of(c * CHUNK, CHUNK)
            query_place = query0 + lax.broadcasted_iota(jnp.int32, (BLK, CHUNK), 1)
            allowed = (query_place >= places) & (query_place < ends)
            count = CHUNK // BLK
            slots = [inverse[c * count + i] for i in range(count)]

            def stat(row):
                return jnp.concatenate([stat_ref[slot, row : row + 1, :] for slot in slots], 1)

            for g in range(pairs):
                queries = q_ref[pl.ds(query0, CHUNK), lanes(g)]
                grads = d_ref[pl.ds(query0, CHUNK), lanes(g)]
                scores = dot_nt(k_scr[g], queries)
                grad_prob = dot_nt(v_scr[g], grads)
                probs, grad_scores = [], []
                for h in range(2):
                    rows = slice(h * BLK, (h + 1) * BLK)
                    shifted = jnp.where(allowed, scores[rows] - stat(2 * g + h), NEG_BIG)
                    prob = jnp.exp(shifted)
                    probs.append(prob.astype(LOW))
                    grad_scores.append(
                        (prob * (grad_prob[rows] - stat(half_stat + 2 * g + h))).astype(LOW)
                    )
                dv_scr[g] += dot_nn(jnp.concatenate(probs, 0), grads)
                dk_scr[g] += dot_nn(jnp.concatenate(grad_scores, 0), queries)

        cosine = cos_ref[pl.ds(row0, BLK), :]
        sine = sin_ref[pl.ds(row0, BLK), :]
        for g in range(pairs):
            grad = one_of_two(dk_scr[g], lane) * SCALE
            dk_out[pl.ds(out0, BLK), lanes(g)] = turned(grad, cosine, -sine, lane).astype(LOW)
            dv_out[pl.ds(out0, BLK), lanes(g)] = one_of_two(dv_scr[g], lane).astype(LOW)


def key_side(
    blocks, first, last, inverse, queries, keys, values, grads, cosine, sine, ends, stats
):
    own = blocks.shape[0]
    width = queries.shape[1]
    pairs = width // BLK
    work = 2 * BLK * CHUNK
    return pl.pallas_call(
        key_kernel,
        in_specs=[smem()] * 4 + [vmem()] * 8,
        out_specs=[vmem()] * 2,
        out_shape=[jax.ShapeDtypeStruct((own * BLK, width), LOW)] * 2,
        scratch_shapes=[
            pltpu.VMEM((pairs, 2 * BLK, BLK), LOW),
            pltpu.VMEM((pairs, 2 * BLK, BLK), LOW),
            pltpu.VMEM((pairs, 2 * BLK, BLK), WIDE),
            pltpu.VMEM((pairs, 2 * BLK, BLK), WIDE),
        ],
        compiler_params=pltpu.CompilerParams(vmem_limit_bytes=VMEM_ASK),
        cost_estimate=pl.CostEstimate(
            flops=own * pairs * 4 * 4 * 2 * work * BLK,
            bytes_accessed=4 * keys.shape[0] * width * 2,
            transcendentals=own * pairs * 4 * work,
        ),
        name="key_side",
    )(blocks, first, last, inverse, queries, keys, values, grads, cosine, sine, ends, stats)


TILE = 256


def symmetric_product(out_ref, left, right):
    size = out_ref.shape[0]
    for i in range(0, size, TILE):
        out_ref[i : i + TILE, i:] = dot_nt(left[i : i + TILE, :], right[i:, :])
    for i in range(0, size, TILE):
        for j in range(i + TILE, size, TILE):
            out_ref[j : j + TILE, i : i + TILE] = out_ref[i : i + TILE, j : j + TILE].T


def ns_kernel(near_ref, far_ref, out_ref, wide_scr, low_scr, gram_scr, poly_scr):
    size, half = near_ref.shape
    span = 2 * half
    step = 768
    cuts = [slice(i, i + step) for i in range(0, span, step)]
    total = jnp.zeros((1, 1), WIDE)
    for source, base in ((near_ref, 0), (far_ref, half)):
        for i in range(0, half, step):
            part = source[:, i : i + step].astype(WIDE)
            wide_scr[:, base + i : base + i + step] = part
            total = total + jnp.sum(part * part)
    factor = 1.0 / (jnp.sqrt(total) + 1e-7)
    for cut in cuts:
        part = wide_scr[:, cut] * factor
        wide_scr[:, cut] = part
        low_scr[:, cut] = part.astype(LOW)

    def polynomial():
        symmetric_product(gram_scr, low_scr, low_scr)
        poly_scr[...] = gram_scr[...].astype(LOW)
        first = gram_scr[...] * NS_COEF[1]
        symmetric_product(gram_scr, poly_scr, poly_scr)
        poly_scr[...] = (first + NS_COEF[2] * gram_scr[...]).astype(LOW)

    @pl.loop(0, NS_STEPS - 1)
    def _(_):
        polynomial()
        for cut in cuts:
            part = NS_COEF[0] * wide_scr[:, cut] + dot_nn(poly_scr[...], low_scr[:, cut])
            wide_scr[:, cut] = part
            low_scr[:, cut] = part.astype(LOW)

    polynomial()
    rows = out_ref.shape[0]
    for i in range(0, half, step):
        cut = slice(i, i + step)
        out_ref[:, cut] = (
            NS_COEF[0] * wide_scr[:rows, cut] + dot_nn(poly_scr[:rows, :], low_scr[:, cut])
        ).astype(LOW)


def orthogonal_rows(near, far, rows):
    size, half = near.shape
    kept = rows if rows % 16 == 0 else size
    out = pl.pallas_call(
        ns_kernel,
        in_specs=[vmem()] * 2,
        out_specs=vmem(),
        out_shape=jax.ShapeDtypeStruct((kept, half), LOW),
        scratch_shapes=[
            pltpu.VMEM((size, 2 * half), WIDE),
            pltpu.VMEM((size, 2 * half), LOW),
            pltpu.VMEM((size, size), WIDE),
            pltpu.VMEM((size, size), LOW),
        ],
        compiler_params=pltpu.CompilerParams(vmem_limit_bytes=VMEM_ASK),
        cost_estimate=pl.CostEstimate(
            flops=NS_STEPS * 7 * size * size * half, bytes_accessed=4 * size * half, transcendentals=0
        ),
        name="orthogonal_rows",
    )(near, far)
    return out[:rows]


def rotary_tables(places):
    half = ROT // 2
    exponent = jnp.arange(0, ROT, 2, dtype=WIDE) / ROT
    frequency = 1.0 / 10000.0**exponent
    angles = frequency[:, None] * places.astype(WIDE)[None, :]
    lane = jnp.arange(BLK) % HD
    picked = ((lane % half)[None, :] == jnp.arange(half)[:, None]) & (lane < ROT)[None, :]
    sign = jnp.where(lane < half, -1.0, 1.0)[None, :]
    spread = partial(
        jnp.einsum, "fn,fl->nl", precision=lax.Precision.HIGHEST, preferred_element_type=WIDE
    )
    cosine = spread(jnp.cos(angles), picked.astype(WIDE)) + (lane >= ROT)[None, :].astype(WIDE)
    return cosine, spread(jnp.sin(angles), picked * sign)


def body(
    tokens,
    cotangent,
    w_qkv,
    w_attn,
    w_up,
    w_down,
    norm_vectors,
    qkv_bias,
    up_bias,
    qkv_moment,
    attn_moment,
    up_moment,
    down_moment,
    norm_moment,
    qbias_moment,
    ubias_moment,
    seq_lengths,
    block_source,
):
    row_count, half = tokens.shape
    fsdp_count = lax.axis_size("fsdp")
    ctx_count = lax.axis_size("ctx")
    tp_index = lax.axis_index("tp")
    fsdp_index = lax.axis_index("fsdp")
    ctx_index = lax.axis_index("ctx")
    low_count = ctx_count // OWNERS
    ctx_low = ctx_index % low_count
    ctx_high = ctx_index // low_count
    width = 2 * half
    own_blocks = row_count // BLK
    pack = ctx_count * row_count
    first_tp = tp_index == 0
    block_row = block_source[0]
    length_row = seq_lengths[0]

    def both_halves(mine, other, dim):
        return jnp.concatenate(
            [jnp.where(first_tp, mine, other), jnp.where(first_tp, other, mine)], axis=dim
        )

    tokens_far = partner(tokens, "tp", 1)
    cotangent_far = partner(cotangent, "tp", 1)
    full_cotangent = both_halves(cotangent, cotangent_far, 1)

    up_full = gather_axis(w_up.astype(LOW), "fsdp", 0)
    down_full = gather_axis(w_down.astype(LOW), "fsdp", 1)
    qkv_full = gather_axis(w_qkv.astype(LOW).reshape(w_qkv.shape[0], 3 * half), "fsdp", 0)
    attn_full = gather_axis(w_attn.astype(LOW), "fsdp", 1)

    def group_rows(own, own_far):
        near = [own] + [partner(own, "ctx", s * low_count) for s in range(1, OWNERS)]
        shards = [jnp.concatenate(near, axis=0)]
        for s in range(1, low_count):
            shards.append(jnp.concatenate([partner(part, "ctx", s) for part in near], axis=0))
        near_rest = jnp.concatenate(near[1:], axis=0)
        far = [own_far, partner(near_rest, "tp", 1)]
        far += [partner(shard, "tp", 1) for shard in shards[1:]]
        return jnp.concatenate(shards, axis=0), jnp.concatenate(far, axis=0)

    x_near, x_far = group_rows(tokens, tokens_far)
    g_near, g_far = group_rows(cotangent, cotangent_far)

    def group_place(ctx):
        differs = ctx ^ ctx_index
        return (differs % low_count) * OWNERS + differs // low_count

    slot_blocks = jnp.arange(block_row.shape[0], dtype=jnp.int32)
    slot_places = group_place(slot_blocks // own_blocks) * own_blocks + slot_blocks % own_blocks
    inverse = jnp.sum(
        jnp.where(block_row[None, :] == slot_blocks[:, None], slot_places[None, :], 0), axis=1
    ).astype(jnp.int32)
    my_blocks = lax.dynamic_slice_in_dim(block_row, ctx_index * own_blocks, own_blocks)

    seq_ends = jnp.cumsum(length_row).astype(jnp.int32)
    seq_starts = seq_ends - length_row

    def bounds(packed):
        inside = (packed[:, None] >= seq_starts[None, :]) & (packed[:, None] < seq_ends[None, :])
        return (
            jnp.sum(jnp.where(inside, seq_starts[None, :], 0), axis=1).astype(jnp.int32),
            jnp.sum(jnp.where(inside, seq_ends[None, :], 0), axis=1).astype(jnp.int32),
        )

    packed = jnp.arange(pack, dtype=jnp.int32)
    cosine, sine = rotary_tables(packed - bounds(packed)[0])
    my_packed = (
        my_blocks[:, None] * BLK + jnp.arange(BLK, dtype=jnp.int32)[None, :]
    ).reshape(-1)
    my_starts, my_ends = bounds(my_packed)
    key_first = bounds(my_blocks * BLK)[0] // CHUNK
    key_last = (my_blocks * BLK + BLK - 1) // CHUNK + 1
    query_first = my_blocks * BLK // CHUNK
    query_last = (bounds(my_blocks * BLK + BLK - 1)[1] + CHUNK - 1) // CHUNK

    def own_first(array, dim):
        left, right = jnp.split(array, 2, axis=dim)
        return jnp.where(first_tp, left, right), jnp.where(first_tp, right, left)

    queries, keys, values, d_attended = project_all(
        inverse,
        x_near,
        x_far,
        g_near,
        g_far,
        (
            *own_first(qkv_full, 0),
            qkv_bias.reshape(1, 3 * half),
            *own_first(norm_vectors, 1),
            *own_first(attn_full, 1),
        ),
        cosine,
        sine,
    )

    inputs = both_halves(tokens, tokens_far, 1).astype(WIDE)
    centered = inputs - jnp.mean(inputs, axis=1, keepdims=True)
    inv_std = lax.rsqrt(jnp.mean(centered * centered, axis=1, keepdims=True) + 1e-05)
    normed = centered * inv_std
    norm_out = (normed * norm_vectors[0] + norm_vectors[1]).astype(LOW)
    hidden = dot_nn(norm_out, up_full) + up_bias
    activated, gelu_pull = jax.vjp(partial(jax.nn.gelu, approximate=False), hidden)
    activated_low = activated.astype(LOW)
    d_hidden = gelu_pull(dot_nt(full_cotangent, down_full))[0].astype(LOW)

    def outer(left, right):
        return jnp.einsum("na,nb->ab", left, right, preferred_element_type=WIDE)

    def reduced(gradient):
        rows = gradient.shape[0] // fsdp_count
        part = sum_scatter(
            gradient.reshape(fsdp_count, rows, gradient.shape[1]), "fsdp", 1, fsdp_index
        )
        piece = rows // ctx_count
        part = part.reshape(OWNERS, low_count, piece, gradient.shape[1])
        part = sum_scatter(jnp.swapaxes(part, 0, 1), "ctx", 1, ctx_low)
        return sum_scatter(part, "ctx", low_count, ctx_high)

    sum_up = reduced(outer(norm_out, d_hidden))
    sum_down = reduced(outer(full_cotangent, activated_low))
    grad_ubias = jnp.sum(d_hidden.astype(WIDE), axis=0)
    grad_outbias = jnp.sum(cotangent.astype(WIDE), axis=0)

    attended, grad_q, stats = query_side(
        my_blocks,
        key_first,
        key_last,
        queries,
        keys,
        values,
        d_attended,
        cosine,
        sine,
        my_starts[:, None],
    )
    near = [stats] + [partner(stats, "ctx", s * low_count) for s in range(1, OWNERS)]
    all_stats = list(near)
    for s in range(1, low_count):
        all_stats += [partner(part, "ctx", s) for part in near]
    grad_k, grad_v = key_side(
        my_blocks,
        query_first,
        query_last,
        inverse,
        queries,
        keys,
        values,
        d_attended,
        cosine,
        sine,
        my_ends[:, None],
        jnp.concatenate(all_stats, axis=0),
    )
    grad_proj = jnp.concatenate([grad_q, grad_k, grad_v], axis=1)
    sum_joint = reduced(
        jnp.concatenate(
            [outer(norm_out, grad_proj), outer(full_cotangent, attended)], axis=1
        )
    )
    grad_qbias = jnp.sum(grad_proj.astype(WIDE), axis=0)

    partial_out = dot_nn(attended, attn_full) + dot_nn(activated_low, down_full)

    def own_half(array):
        return jnp.where(first_tp, array[:, :half], array[:, half:])

    def far_half(array):
        return jnp.where(first_tp, array[:, half:], array[:, :half])

    def sum_halves(array):
        return own_half(array) + partner(far_half(array).astype(LOW), "tp", 1).astype(WIDE)

    out_bias = own_half((norm_vectors[2] + norm_vectors[3])[None, :])
    mixed = (tokens.astype(WIDE) + sum_halves(partial_out) + out_bias).astype(LOW)

    grad_norm = sum_halves(dot_nt(grad_proj, qkv_full) + dot_nt(d_hidden, up_full))
    my_normed = own_half(normed)
    scaled = grad_norm * own_half(norm_vectors[0:1])
    row_sums = jnp.stack([jnp.sum(scaled, axis=1), jnp.sum(scaled * my_normed, axis=1)])
    row_means = (row_sums + partner(row_sums, "tp", 1)) / width
    grad_tokens = cotangent.astype(WIDE) + inv_std * (
        scaled - row_means[0][:, None] - my_normed * row_means[1][:, None]
    )

    vector_parts = jnp.stack(
        [jnp.sum(grad_norm * my_normed, axis=0), jnp.sum(grad_norm, axis=0), grad_outbias]
    )
    small = jnp.concatenate([vector_parts.reshape(-1), grad_qbias, grad_ubias])
    small = sum_everywhere(small, ("ctx", "fsdp"))
    mine = small[: 3 * half].reshape(3, half)
    vectors = both_halves(mine, partner(mine, "tp", 1), 1)
    sum_vectors = jnp.concatenate([vectors, vectors[2:3]], axis=0)
    sum_qbias = small[3 * half : 6 * half].reshape(3, half)
    sum_ubias = small[6 * half :]

    joint = jnp.concatenate([sum_up, sum_down, sum_joint], axis=1)
    hidden_here = up_bias.shape[0]
    gathered = lax.all_gather(joint.astype(LOW), "ctx", axis=0, tiled=True).astype(WIDE)
    cut_down, cut_qkv, cut_attn = hidden_here, 2 * hidden_here, 2 * hidden_here + 3 * half
    fresh_up = 0.95 * up_moment + gathered[:, :cut_down]
    fresh_down = 0.95 * down_moment + gathered[:, cut_down:cut_qkv].T
    fresh_qkv = 0.95 * qkv_moment + gathered[:, cut_qkv:cut_attn].reshape(qkv_moment.shape)
    fresh_attn = 0.95 * attn_moment + gathered[:, cut_attn:].T

    piece = joint.shape[0]

    def my_rows(array, dim):
        return lax.dynamic_slice_in_dim(array, ctx_index * piece, piece, dim)

    def as_rows(up, down, qkv, attn):
        return (
            my_rows(up, 0),
            my_rows(down, 1).T,
            my_rows(qkv, 0).reshape(piece, 3 * half),
            my_rows(attn, 1).T,
        )

    moments = as_rows(up_moment, down_moment, qkv_moment, attn_moment)
    sums = (sum_up, sum_down, sum_joint[:, : 3 * half], sum_joint[:, 3 * half :])
    pieces = jnp.stack(
        [
            jnp.pad(
                (0.95 * moment + total).astype(LOW), ((0, 0), (0, hidden_here - total.shape[1]))
            )
            for moment, total in zip(moments, sums)
        ]
    )

    def to_owner(array, step):
        if step == 0:
            return lax.dynamic_index_in_dim(array, ctx_high, 0, keepdims=False)
        picked = lax.dynamic_index_in_dim(array, ctx_high ^ step, 0, keepdims=False)
        return partner(picked, "ctx", step * low_count)

    matrix = jnp.concatenate([to_owner(pieces, s) for s in range(OWNERS)], axis=0)
    parts = [matrix] + [partner(matrix, "ctx", s) for s in range(1, low_count)]
    for s in range(1, fsdp_count):
        parts += [partner(part, "fsdp", s) for part in parts[:low_count]]
    near_cols = jnp.concatenate(parts, axis=0)
    far_cols = jnp.concatenate([partner(part, "tp", 1) for part in parts], axis=0)
    rows_out = orthogonal_rows(near_cols, far_cols, OWNERS * piece).reshape(
        OWNERS, piece, hidden_here
    )
    returned = jnp.stack(
        [rows_out[0]]
        + [partner(rows_out[s], "ctx", s * low_count) for s in range(1, OWNERS)]
    )
    orthogonal = [
        lax.dynamic_index_in_dim(returned, ctx_high ^ m, 0, keepdims=False).astype(WIDE)
        for m in range(OWNERS)
    ]
    full_hidden = hidden_here * 2
    olds = as_rows(w_up, w_down, w_qkv, w_attn)
    rates = (
        0.5 * math.sqrt(full_hidden / width),
        0.5 * math.sqrt(full_hidden / full_hidden),
        0.5 * math.sqrt(3 * width / width),
        0.5 * math.sqrt(width / (width // HD)),
    )
    new_up, new_down, new_qkv, new_attn = (
        old - rate * made[:, : old.shape[1]] for old, rate, made in zip(olds, rates, orthogonal)
    )

    vector_rate = 0.3 / math.sqrt(row_count * fsdp_count * ctx_count)
    mom_norm = 0.9 * norm_moment + sum_vectors
    mom_qbias = 0.9 * qbias_moment + sum_qbias
    mom_ubias = 0.9 * ubias_moment + sum_ubias
    return (
        mixed,
        grad_tokens,
        fresh_qkv,
        new_qkv.reshape(piece, 3, half),
        fresh_attn,
        new_attn.T,
        fresh_up,
        new_up,
        fresh_down,
        new_down.T,
        mom_norm,
        norm_vectors - vector_rate * mom_norm,
        mom_qbias,
        qkv_bias - vector_rate * mom_qbias,
        mom_ubias,
        up_bias - vector_rate * mom_ubias,
    )


def solution(mesh):
    return jax.shard_map(
        body,
        mesh=mesh,
        in_specs=(
            P(("fsdp", "ctx"), "tp"),
            P(("fsdp", "ctx"), "tp"),
            P("fsdp", None, "tp"),
            P("tp", "fsdp"),
            P("fsdp", "tp"),
            P("tp", "fsdp"),
            P(),
            P(None, "tp"),
            P("tp"),
            P("fsdp", None, "tp"),
            P("tp", "fsdp"),
            P("fsdp", "tp"),
            P("tp", "fsdp"),
            P(),
            P(None, "tp"),
            P("tp"),
            P("fsdp", None),
            P("fsdp", None),
        ),
        out_specs=(
            P(("fsdp", "ctx"), "tp"),
            P(("fsdp", "ctx"), "tp"),
            P("fsdp", None, "tp"),
            P(("fsdp", "ctx"), None, "tp"),
            P("tp", "fsdp"),
            P("tp", ("fsdp", "ctx")),
            P("fsdp", "tp"),
            P(("fsdp", "ctx"), "tp"),
            P("tp", "fsdp"),
            P("tp", ("fsdp", "ctx")),
            P(),
            P(),
            P(None, "tp"),
            P(None, "tp"),
            P("tp"),
            P("tp"),
        ),
        check_vma=False,
    )
```

time: 1490 us -> 545 us (0.37)
  waiting for transfers between devices: 556 us -> 165 us
  matrix products: 437 us -> 49.1 us
  blocking collectives: 216 us -> 0 us
  Pallas kernels: 0 us -> 103 us
  starting transfers between devices: 1 us -> 80.4 us
  local copies, waits for them, and re-layouts: 118 us -> 59.5 us
  other arithmetic: 113 us -> 65 us
  loops' own time: 24.8 us -> 0 us
    dot_general x83 -> x12, matrix products: 437 us -> 49.1 us  [the longest x3 25.2 us: dot_nn(): return jnp.dot(left, right, preferred_element_type=WIDE)]
    psum x1 -> x0, blocking collectives: 201 us -> none  [body(): lax.psum((grad_vectors, grad_qbias, grad_ubias), ('fsdp', 'ctx'))]
    psum x3 -> x0, waiting for transfers between devices: 192 us -> none  [the longest x1 145 us: body(): lax.psum(part_qkv.astype(jnp.bfloat16), 'ctx').astype(jnp.float32)]
    reduce_scatter x4 -> x0, waiting for transfers between devices: 172 us -> none  [the longest x1 74.6 us: body(): lax.psum_scatter(grad_values.astype(jnp.bfloat16), 'ctx', scatter_dimensi...]
    ppermute x0 -> x67, waiting for transfers between devices: none -> 165 us  [partner(): return lax.ppermute(value, axis, [(i, i ^ step) for i in range(size)])]
    all_gather x9 -> x1, waiting for transfers between devices: 143 us -> 0.01 us  [body(): lax.all_gather(joint.astype(LOW), 'ctx', axis=0, tiled=True).astype(WIDE)]
    pallas_call x0 -> x4, Pallas kernels: none -> 103 us  [the longest x1 38.6 us: orthogonal_rows(): pl.pallas_call(ns_kernel, in_specs=[vmem()] * 2, out_specs=vmem(), out_sh...]
    ppermute x0 -> x67, starting transfers between devices: none -> 80.3 us  [partner(): return lax.ppermute(value, axis, [(i, i ^ step) for i in range(size)])]
  transfers between devices with their start and end apart: 19 -> 68, of which waited for: 12 -> 27; matrix products, arithmetic and copies ran while one was open for 43% -> 28% of each run, Pallas kernels for 0% -> 19%
where the time goes in v1:
time: 545 us; the launch traced here: 538 us
  waiting for transfers between devices  165 us (30%)
  Pallas kernels  103 us (19%)
  starting transfers between devices  80.4 us (15%)
  other arithmetic  65 us (12%)
  local copies, waits for them, and re-layouts  59.5 us (11%)
  matrix products  49.1 us (9%)
  between operations  15.2 us (3%)
    ppermute x67, waiting for transfers between devices, partner(): return lax.ppermute(value, axis, [(i, i ^ step) for i in range(size)])  165 us
    ppermute x67, starting transfers between devices, partner(): return lax.ppermute(value, axis, [(i, i ^ step) for i in range(size)])  80.3 us
    pallas_call x1, Pallas kernels, orthogonal_rows(): pl.pallas_call(ns_kernel, in_specs=[vmem()] * 2, out_specs=vmem(), out_sh...  38.6 us
    unnamed x158, local copies, waits for them, and re-layouts  35.5 us
    pallas_call x1, Pallas kernels, project_all(): pl.pallas_call(partial(project_kernel, count), grid_spec=pltpu.PrefetchSc...  26.1 us
    dot_general x3, matrix products, dot_nn(): return jnp.dot(left, right, preferred_element_type=WIDE)  25.2 us
    pallas_call x1, Pallas kernels, query_side(): pl.pallas_call(query_kernel, in_specs=[smem()] * 3 + [vmem()] * 7, out_sp...  21.4 us
    pallas_call x1, Pallas kernels, key_side(): pl.pallas_call(key_kernel, in_specs=[smem()] * 4 + [vmem()] * 8, out_spec...  17.1 us
  transfers between devices with their start and end apart: 68, of which 27 were waited for; matrix products, arithmetic and copies ran while one was open for 28% of the time, Pallas kernels for 19%

profile of v1, /device:TPU:0, one launch (start us, length us, event | category | flops | bytes accessed | tf_op | source)
XLA Modules:
  0.0 537.9 jit_solution(10303645146856812255)
XLA Ops:
  7.8 2.7 collective-permute-start
  10.4 2.6 collective-permute-start.1
  13.0 1.8 convert_element_type.244
  27.9 2.6 constant_dynamic-slice_fusion.1
  32.1 3.4 convolution_add_fusion.refs_23_.cos_ref
  35.5 2.7 copy.91
  39.3 3.0 copy.97
  47.4 3.5 copy.103
  55.1 5.0 fusion.52.refs_24_.sin_ref
  66.9 3.1 collective-permute-start.11
  76.3 9.5 %collective-permute-done.10 = bf16[512,384]{1,0:T(8,128)(2,1)S(1)} collective-permute-done((bf16[512,384]{1,0:T(8,128)(2,1)S(1)}, bf16[512,384]{1,0:T(8,128)(2,1)S(1)}, u32[]{:S(2)}, u32[]{:S(2)}) %collective-permute-start.10) | collective-permute-done | bytes 393248 | tf_op jit(solution)/shard_map/ppermute | solution.py:38
  86.4 10.4 %collective-permute-done.11 = bf16[512,384]{1,0:T(8,128)(2,1)S(1)} collective-permute-done((bf16[512,384]{1,0:T(8,128)(2,1)S(1)}, bf16[512,384]{1,0:T(8,128)(2,1)S(1)}, u32[]{:S(2)}, u32[]{:S(2)}) %collective-permute-start.11) | collective-permute-done | bytes 393248 | tf_op jit(solution)/shard_map/ppermute | solution.py:38
  102.6 6.5 %collective-permute-done.4 = bf16[512,384]{1,0:T(8,128)(2,1)S(1)} collective-permute-done((bf16[512,384]{1,0:T(8,128)(2,1)}, bf16[512,384]{1,0:T(8,128)(2,1)S(1)}, u32[]{:S(2)}, u32[]{:S(2)}) %collective-permute-start.4) | collective-permute-done | bytes 393248 | tf_op jit(solution)/shard_map/ppermute | solution.py:38
  109.7 7.9 %collective-permute-done.5 = bf16[512,384]{1,0:T(8,128)(2,1)S(1)} collective-permute-done((bf16[512,384]{1,0:T(8,128)(2,1)}, bf16[512,384]{1,0:T(8,128)(2,1)S(1)}, u32[]{:S(2)}, u32[]{:S(2)}) %collective-permute-start.5) | collective-permute-done | bytes 393248 | tf_op jit(solution)/shard_map/ppermute | solution.py:38
  118.1 7.9 %collective-permute-done.6 = bf16[512,384]{1,0:T(8,128)(2,1)S(1)} collective-permute-done((bf16[512,384]{1,0:T(8,128)(2,1)}, bf16[512,384]{1,0:T(8,128)(2,1)S(1)}, u32[]{:S(2)}, u32[]{:S(2)}) %collective-permute-start.6) | collective-permute-done | bytes 393248 | tf_op jit(solution)/shard_map/ppermute | solution.py:38
  126.6 7.8 %collective-permute-done.14 = bf16[512,384]{1,0:T(8,128)(2,1)S(1)} collective-permute-done((bf16[512,384]{1,0:T(8,128)(2,1)S(1)}, bf16[512,384]{1,0:T(8,128)(2,1)S(1)}, u32[]{:S(2)}, u32[]{:S(2)}) %collective-permute-start.14) | collective-permute-done | bytes 393248 | tf_op jit(solution)/shard_map/ppermute | solution.py:38
  135.0 6.0 %collective-permute-done.15 = bf16[512,384]{1,0:T(8,128)(2,1)S(1)} collective-permute-done((bf16[512,384]{1,0:T(8,128)(2,1)S(1)}, bf16[512,384]{1,0:T(8,128)(2,1)S(1)}, u32[]{:S(2)}, u32[]{:S(2)}) %collective-permute-start.15) | collective-permute-done | bytes 393248 | tf_op jit(solution)/shard_map/ppermute | solution.py:38
  141.1 4.1 collective-permute-done.16
  150.7 3.9 collective-permute-done.22
  154.9 22.1 %multiply_convert_fusion = (bf16[512,1536]{1,0:T(8,128)(2,1)S(1)}, f32[512,1536]{1,0:T(8,128)S(1)}, f32[512,1536]{1,0:T(8,128)S(1)}) fusion(f32[1536]{0:T(1024)S(1)} %copy-done.56, bf16[384,1536]{1,0:T(8,128)(2,1)S(1)} %get-tuple-element.133, bf16[384,1536]{1,0:T(8,128)(2,1)S(1)} %get-tuple-element.132, f32[768]{0:T(1024)S(1)} %get-tuple-element.103, ...), kind=kOutput, calls=%fused_computation.9 | convolution fusion | flops 1268121600 | bytes 11026432 | tf_op jit(solution)/shard_map/dot_general | solution.py:29
  177.3 2.4 convert_reduce_fusion
  181.3 2.6 fusion.16
  188.3 2.6 fusion.15
  192.3 3.0 pad_maximum_fusion.1.refs_4_.refs_5_.refs_6_.refs_7_
  195.4 2.0 pad_maximum_fusion.2.refs_12_.refs_13_.refs_14_.refs_15_
  197.4 26.1 %project_all.1 = (bf16[4096,384]{1,0:T(8,128)(2,1)}, bf16[4096,384]{1,0:T(8,128)(2,1)}, bf16[4096,384]{1,0:T(8,128)(2,1)}, bf16[4096,384]{1,0:T(8,128)(2,1)}) custom-call(s32[32]{0:T(128)} %select_reduce_fusion.1.inv_ref.inverse, bf16[4096,384]{1,0:T(8,128)(2,1)} %copy-done, bf16[4096,384]{1,0:T(8,128)(2,1)} %copy-done, bf16[4096,384]{1,0:T(8,128)(2,1)} %copy-done, ...), custom_call_target="tpu_custom_call" | custom-call | flops 9663676416 | bytes 31457280 | tf_op jit(solution)/shard_map/project_all/pallas_call | solution.py:151
  223.6 21.4 %query_side.1 = (bf16[512,384]{1,0:T(8,128)(2,1)}, bf16[512,384]{1,0:T(8,128)(2,1)}, f32[4,16,128]{2,1,0:T(8,128)}) custom-call(s32[4]{0:T(128)} %copy-done.58, s32[4]{0:T(128)} %and_select_fusion.9.first, s32[4]{0:T(128)} %get-tuple-element.175.last, bf16[4096,384]{1,0:T(8,128)(2,1)} %get-tuple-element.25.q_ref, bf16[4096,384]{1,0:T(8,128)(2,1)} %get-tuple-element.26.k_ref, ...), custom_call_target="tpu_custom_call" | custom-call | flops 6442450944 | bytes 12582912 | tf_op jit(solution)/shard_map/query_side/pallas_call | solution.py:311
  245.0 2.9 collective-permute-start.25
  250.3 1.8 constant_dynamic-update-slice_fusion.26
  253.0 2.3 bitcast_add_fusion.2
  265.6 19.7 %collective-permute-done.29 = f32[4,16,128]{2,1,0:T(8,128)S(1)} collective-permute-done((f32[4,16,128]{2,1,0:T(8,128)S(1)}, f32[4,16,128]{2,1,0:T(8,128)S(1)}, u32[]{:S(2)}, u32[]{:S(2)}) %collective-permute-start.29) | collective-permute-done | bytes 32800 | tf_op jit(solution)/shard_map/ppermute | solution.py:38
  286.7 17.1 %key_side.1 = (bf16[512,384]{1,0:T(8,128)(2,1)}, bf16[512,384]{1,0:T(8,128)(2,1)}) custom-call(s32[4]{0:T(128)} %copy-done.58, s32[4]{0:T(128)} %get-tuple-element.120.first, s32[4]{0:T(128)} %and_select_fusion.last, s32[32]{0:T(128)} %select_reduce_fusion.1.inv_ref.inverse, bf16[4096,384]{1,0:T(8,128)(2,1)} %get-tuple-element.25.q_ref, ...), custom_call_target="tpu_custom_call" | custom-call | flops 6442450944 | bytes 12582912 | tf_op jit(solution)/shard_map/key_side/pallas_call | solution.py:425
  305.9 3.1 fusion.17
  315.3 4.3 collective-permute-start.62
  319.5 2.7 fusion.93
  323.7 2.3 collective-permute-done.63
  326.2 2.6 collective-permute-start.44
  328.8 1.9 collective-permute-done.64
  330.7 1.9 collective-permute-start.65
  332.6 2.1 add_convert_fusion.2
  334.7 18.8 %collective-permute-done.65 = f32[3840]{0:T(1024)S(1)} collective-permute-done((f32[3840]{0:T(1024)S(1)}, f32[3840]{0:T(1024)S(1)}, u32[]{:S(2)}, u32[]{:S(2)}) %collective-permute-start.65) | collective-permute-done | bytes 15392 | tf_op jit(solution)/shard_map/ppermute | solution.py:38
  370.7 6.2 %collective-permute-done.37 = bf16[48,1536]{1,0:T(8,128)(2,1)S(1)} collective-permute-done((bf16[48,1536]{1,0:T(8,128)(2,1)S(1)}, bf16[48,1536]{1,0:T(8,128)(2,1)S(1)}, u32[]{:S(2)}, u32[]{:S(2)}) %collective-permute-start.37) | collective-permute-done | bytes 147488 | tf_op jit(solution)/shard_map/ppermute | solution.py:38
  376.9 2.0 collective-permute-start.43
  380.1 3.9 collective-permute-done.45
  384.2 5.3 collective-permute-start.46
  389.9 2.0 collective-permute-start.48
  393.9 8.5 %collective-permute-done.47 = bf16[48,1536]{1,0:T(8,128)(2,1)S(1)} collective-permute-done((bf16[48,1536]{1,0:T(8,128)(2,1)S(1)}, bf16[48,1536]{1,0:T(8,128)(2,1)S(1)}, u32[]{:S(2)}, u32[]{:S(2)}) %collective-permute-start.47) | collective-permute-done | bytes 147488 | tf_op jit(solution)/shard_map/ppermute | solution.py:38
  402.7 2.9 collective-permute-start.49
  410.0 8.8 %collective-permute-done.50 = bf16[48,1536]{1,0:T(8,128)(2,1)S(1)} collective-permute-done((bf16[48,1536]{1,0:T(8,128)(2,1)S(1)}, bf16[48,1536]{1,0:T(8,128)(2,1)S(1)}, u32[]{:S(2)}, u32[]{:S(2)}) %collective-permute-start.50) | collective-permute-done | bytes 147488 | tf_op jit(solution)/shard_map/ppermute | solution.py:38
  422.1 1.8 collective-permute-start.53
  423.9 6.9 %collective-permute-done.52 = bf16[192,1536]{1,0:T(8,128)(2,1)} collective-permute-done((bf16[192,1536]{1,0:T(8,128)(2,1)}, bf16[192,1536]{1,0:T(8,128)(2,1)}, u32[]{:S(2)}, u32[]{:S(2)}) %collective-permute-start.52) | collective-permute-done | bytes 589856 | tf_op jit(solution)/shard_map/ppermute | solution.py:38
  430.8 2.7 collective-permute-start.54
  436.3 9.6 %collective-permute-done.54 = bf16[192,1536]{1,0:T(8,128)(2,1)S(1)} collective-permute-done((bf16[192,1536]{1,0:T(8,128)(2,1)}, bf16[192,1536]{1,0:T(8,128)(2,1)S(1)}, u32[]{:S(2)}, u32[]{:S(2)}) %collective-permute-start.54) | collective-permute-done | bytes 589856 | tf_op jit(solution)/shard_map/ppermute | solution.py:38
  445.9 1.9 constant_dynamic-update-slice_fusion.29
  451.2 38.6 %orthogonal_rows.1 = bf16[192,1536]{1,0:T(8,128)(2,1)} custom-call(bf16[768,1536]{1,0:T(8,128)(2,1)} %constant_dynamic-update-slice_fusion.27.near_ref, bf16[768,1536]{1,0:T(8,128)(2,1)} %pad_maximum_fusion.5.far_ref), custom_call_target="tpu_custom_call" | custom-call | flops 31708938240 | bytes 4718592 | tf_op jit(solution)/shard_map/orthogonal_rows/pallas_call | solution.py:502
  491.0 5.9 %collective-permute-start.59 = (bf16[48,1536]{1,0:T(8,128)(2,1)S(1)}, bf16[48,1536]{1,0:T(8,128)(2,1)S(1)}, u32[]{:S(2)}, u32[]{:S(2)}) collective-permute-start(bf16[48,1536]{1,0:T(8,128)(2,1)S(1)} %get-tuple-element.158), channel_id=1, source_target_pairs={{0,4},{2,6},{4,0},{6,2},{8,12},{10,14},{12,8},{14,10},{1,5},{3,7},... | collective-permute-start | bytes 442376 | tf_op jit(solution)/shard_map/ppermute | solution.py:38
  496.9 2.4 collective-permute-start.61
  500.0 3.1 collective-permute-done.59
  503.0 7.8 %collective-permute-done.60 = bf16[48,1536]{1,0:T(8,128)(2,1)S(1)} collective-permute-done((bf16[48,1536]{1,0:T(8,128)(2,1)S(1)}, bf16[48,1536]{1,0:T(8,128)(2,1)S(1)}, u32[]{:S(2)}, u32[]{:S(2)}) %collective-permute-start.60) | collective-permute-done | bytes 147488 | tf_op jit(solution)/shard_map/ppermute | solution.py:38
  513.3 3.0 convert_element_type.304
  516.3 1.8 fusion.6
  518.6 1.8 slice_add_fusion
  521.3 1.9 copy.113
  528.0 1.8 copy.110
  (371 shorter events, 131.5 us)
Async XLA Ops:
  7.2 506.1 %all-gather.2.cloned.1.call-start = ((), (), s32[]{:S(2)}) async-start(), calls=%async_computation | async-start | bytes 3981312 | tf_op jit(solution)/shard_map/all_gather | solution.py:754
  7.2 57.0 %collective-permute-start.7 = (bf16[512,384]{1,0:T(8,128)(2,1)}, bf16[512,384]{1,0:T(8,128)(2,1)}, u32[]{:S(2)}, u32[]{:S(2)}) collective-permute-start(bf16[512,384]{1,0:T(8,128)(2,1)} %param.18), channel_id=1, source_target_pairs={{0,1},{1,0},{2,3},{3,2},{4,5},{5,4},{6,7},{7,6},{8,9},{9,8},{10,11... | collective-permute-start | bytes 1179656 | tf_op jit(solution)/shard_map/ppermute | solution.py:38
  7.8 58.4 %collective-permute-start = (bf16[512,384]{1,0:T(8,128)(2,1)}, bf16[512,384]{1,0:T(8,128)(2,1)}, u32[]{:S(2)}, u32[]{:S(2)}) collective-permute-start(bf16[512,384]{1,0:T(8,128)(2,1)} %param.18), channel_id=1, source_target_pairs={{0,4},{2,6},{4,0},{6,2},{8,12},{10,14},{12,8},{14,10},{1,5},{3,7},... | collective-permute-start | bytes 1179656 | tf_op jit(solution)/shard_map/ppermute | solution.py:38
  10.4 56.5 %collective-permute-start.1 = (bf16[512,384]{1,0:T(8,128)(2,1)}, bf16[512,384]{1,0:T(8,128)(2,1)}, u32[]{:S(2)}, u32[]{:S(2)}) collective-permute-start(bf16[512,384]{1,0:T(8,128)(2,1)} %param.18), channel_id=1, source_target_pairs={{0,8},{2,10},{4,12},{6,14},{8,0},{10,2},{12,4},{14,6},{1,9},{3,11}... | collective-permute-start | bytes 1179656 | tf_op jit(solution)/shard_map/ppermute | solution.py:38
  13.0 57.0 %collective-permute-start.2 = (bf16[512,384]{1,0:T(8,128)(2,1)}, bf16[512,384]{1,0:T(8,128)(2,1)}, u32[]{:S(2)}, u32[]{:S(2)}) collective-permute-start(bf16[512,384]{1,0:T(8,128)(2,1)} %param.18), channel_id=1, source_target_pairs={{0,12},{2,14},{4,8},{6,10},{8,4},{10,6},{12,0},{14,2},{1,13},{3,15... | collective-permute-start | bytes 1179656 | tf_op jit(solution)/shard_map/ppermute | solution.py:38
  14.8 45.4 %collective-permute-start.21 = (bf16[384,384]{1,0:T(8,128)(2,1)}, bf16[384,384]{1,0:T(8,128)(2,1)}, u32[]{:S(2)}, u32[]{:S(2)}) collective-permute-start(bf16[384,384]{1,0:T(8,128)(2,1)} %convert_element_type.244), channel_id=1, source_target_pairs={{0,16},{16,0},{1,17},{17,1},{2,18},{18,2},{3,19},{19,3},{4,20},{20... | collective-permute-start | bytes 884744 | tf_op jit(solution)/shard_map/ppermute | solution.py:38
  60.2 40.1 %collective-permute-start.3 = (bf16[512,384]{1,0:T(8,128)(2,1)}, bf16[512,384]{1,0:T(8,128)(2,1)S(1)}, u32[]{:S(2)}, u32[]{:S(2)}) collective-permute-start(bf16[512,384]{1,0:T(8,128)(2,1)} %param.18), channel_id=1, source_target_pairs={{0,2},{2,0},{4,6},{6,4},{8,10},{10,8},{12,14},{14,12},{1,3},{3,1},... | collective-permute-start | bytes 1179656 | tf_op jit(solution)/shard_map/ppermute | solution.py:38
  64.3 11.3 %collective-permute-start.17 = (bf16[512,384]{1,0:T(8,128)(2,1)S(1)}, bf16[512,384]{1,0:T(8,128)(2,1)S(1)}, u32[]{:S(2)}, u32[]{:S(2)}) collective-permute-start(bf16[512,384]{1,0:T(8,128)(2,1)S(1)} %copy-done.32), channel_id=1, source_target_pairs={{0,1},{1,0},{2,3},{3,2},{4,5},{5,4},{6,7},{7,6},{8,9},{9,8},{10,11... | collective-permute-start | bytes 1179656 | tf_op jit(solution)/shard_map/ppermute | solution.py:38
  66.2 19.7 %collective-permute-start.10 = (bf16[512,384]{1,0:T(8,128)(2,1)S(1)}, bf16[512,384]{1,0:T(8,128)(2,1)S(1)}, u32[]{:S(2)}, u32[]{:S(2)}) collective-permute-start(bf16[512,384]{1,0:T(8,128)(2,1)S(1)} %copy-done.32), channel_id=1, source_target_pairs={{0,4},{2,6},{4,0},{6,2},{8,12},{10,14},{12,8},{14,10},{1,5},{3,7},... | collective-permute-start | bytes 1179656 | tf_op jit(solution)/shard_map/ppermute | solution.py:38
  66.9 29.9 %collective-permute-start.11 = (bf16[512,384]{1,0:T(8,128)(2,1)S(1)}, bf16[512,384]{1,0:T(8,128)(2,1)S(1)}, u32[]{:S(2)}, u32[]{:S(2)}) collective-permute-start(bf16[512,384]{1,0:T(8,128)(2,1)S(1)} %copy-done.32), channel_id=1, source_target_pairs={{0,8},{2,10},{4,12},{6,14},{8,0},{10,2},{12,4},{14,6},{1,9},{3,11}... | collective-permute-start | bytes 1179656 | tf_op jit(solution)/shard_map/ppermute | solution.py:38
  70.0 27.3 %collective-permute-start.12 = (bf16[512,384]{1,0:T(8,128)(2,1)S(1)}, bf16[512,384]{1,0:T(8,128)(2,1)S(1)}, u32[]{:S(2)}, u32[]{:S(2)}) collective-permute-start(bf16[512,384]{1,0:T(8,128)(2,1)S(1)} %copy-done.32), channel_id=1, source_target_pairs={{0,12},{2,14},{4,8},{6,10},{8,4},{10,6},{12,0},{14,2},{1,13},{3,15... | collective-permute-start | bytes 1179656 | tf_op jit(solution)/shard_map/ppermute | solution.py:38
  75.6 25.4 %collective-permute-start.13 = (bf16[512,384]{1,0:T(8,128)(2,1)S(1)}, bf16[512,384]{1,0:T(8,128)(2,1)S(1)}, u32[]{:S(2)}, u32[]{:S(2)}) collective-permute-start(bf16[512,384]{1,0:T(8,128)(2,1)S(1)} %copy-done.32), channel_id=1, source_target_pairs={{0,2},{2,0},{4,6},{6,4},{8,10},{10,8},{12,14},{14,12},{1,3},{3,1},... | collective-permute-start | bytes 1179656 | tf_op jit(solution)/shard_map/ppermute | solution.py:38
  85.9 61.1 %collective-permute-start.20 = (bf16[384,1152]{1,0:T(8,128)(2,1)S(1)}, bf16[384,1152]{1,0:T(8,128)(2,1)S(1)}, u32[]{:S(2)}, u32[]{:S(2)}) collective-permute-start(bf16[384,1152]{1,0:T(8,128)(2,1)S(1)} %copy-done.16), channel_id=1, source_target_pairs={{0,16},{16,0},{1,17},{17,1},{2,18},{18,2},{3,19},{19,3},{4,20},{20... | collective-permute-start | bytes 2654216 | tf_op jit(solution)/shard_map/ppermute | solution.py:38
  96.8 12.3 %collective-permute-start.4 = (bf16[512,384]{1,0:T(8,128)(2,1)}, bf16[512,384]{1,0:T(8,128)(2,1)S(1)}, u32[]{:S(2)}, u32[]{:S(2)}) collective-permute-start(bf16[512,384]{1,0:T(8,128)(2,1)} %collective-permute-done), channel_id=1, source_target_pairs={{0,2},{2,0},{4,6},{6,4},{8,10},{10,8},{12,14},{14,12},{1,3},{3,1},... | collective-permute-start | bytes 1179656 | tf_op jit(solution)/shard_map/ppermute | solution.py:38
  97.3 20.2 %collective-permute-start.5 = (bf16[512,384]{1,0:T(8,128)(2,1)}, bf16[512,384]{1,0:T(8,128)(2,1)S(1)}, u32[]{:S(2)}, u32[]{:S(2)}) collective-permute-start(bf16[512,384]{1,0:T(8,128)(2,1)} %collective-permute-done.1), channel_id=1, source_target_pairs={{0,2},{2,0},{4,6},{6,4},{8,10},{10,8},{12,14},{14,12},{1,3},{3,1},... | collective-permute-start | bytes 1179656 | tf_op jit(solution)/shard_map/ppermute | solution.py:38
  100.3 25.6 %collective-permute-start.6 = (bf16[512,384]{1,0:T(8,128)(2,1)}, bf16[512,384]{1,0:T(8,128)(2,1)S(1)}, u32[]{:S(2)}, u32[]{:S(2)}) collective-permute-start(bf16[512,384]{1,0:T(8,128)(2,1)} %collective-permute-done.2), channel_id=1, source_target_pairs={{0,2},{2,0},{4,6},{6,4},{8,10},{10,8},{12,14},{14,12},{1,3},{3,1},... | collective-permute-start | bytes 1179656 | tf_op jit(solution)/shard_map/ppermute | solution.py:38
  100.9 33.4 %collective-permute-start.14 = (bf16[512,384]{1,0:T(8,128)(2,1)S(1)}, bf16[512,384]{1,0:T(8,128)(2,1)S(1)}, u32[]{:S(2)}, u32[]{:S(2)}) collective-permute-start(bf16[512,384]{1,0:T(8,128)(2,1)S(1)} %collective-permute-done.10), channel_id=1, source_target_pairs={{0,2},{2,0},{4,6},{6,4},{8,10},{10,8},{12,14},{14,12},{1,3},{3,1},... | collective-permute-start | bytes 1179656 | tf_op jit(solution)/shard_map/ppermute | solution.py:38
  109.1 31.9 %collective-permute-start.15 = (bf16[512,384]{1,0:T(8,128)(2,1)S(1)}, bf16[512,384]{1,0:T(8,128)(2,1)S(1)}, u32[]{:S(2)}, u32[]{:S(2)}) collective-permute-start(bf16[512,384]{1,0:T(8,128)(2,1)S(1)} %collective-permute-done.11), channel_id=1, source_target_pairs={{0,2},{2,0},{4,6},{6,4},{8,10},{10,8},{12,14},{14,12},{1,3},{3,1},... | collective-permute-start | bytes 1179656 | tf_op jit(solution)/shard_map/ppermute | solution.py:38
  117.5 27.7 %collective-permute-start.16 = (bf16[512,384]{1,0:T(8,128)(2,1)S(1)}, bf16[512,384]{1,0:T(8,128)(2,1)S(1)}, u32[]{:S(2)}, u32[]{:S(2)}) collective-permute-start(bf16[512,384]{1,0:T(8,128)(2,1)S(1)} %collective-permute-done.12), channel_id=1, source_target_pairs={{0,2},{2,0},{4,6},{6,4},{8,10},{10,8},{12,14},{14,12},{1,3},{3,1},... | collective-permute-start | bytes 1179656 | tf_op jit(solution)/shard_map/ppermute | solution.py:38
  125.9 28.6 %collective-permute-start.22 = (bf16[384,1536]{1,0:T(8,128)(2,1)S(1)}, bf16[384,1536]{1,0:T(8,128)(2,1)S(1)}, u32[]{:S(2)}, u32[]{:S(2)}) collective-permute-start(bf16[384,1536]{1,0:T(8,128)(2,1)S(1)} %copy-done.41), channel_id=1, source_target_pairs={{0,16},{16,0},{1,17},{17,1},{2,18},{18,2},{3,19},{19,3},{4,20},{20... | collective-permute-start | bytes 3538952 | tf_op jit(solution)/shard_map/ppermute | solution.py:38
  134.4 42.6 %collective-permute-start.23 = (bf16[1536,384]{1,0:T(8,128)(2,1)S(1)}, bf16[1536,384]{1,0:T(8,128)(2,1)S(1)}, u32[]{:S(2)}, u32[]{:S(2)}) collective-permute-start(bf16[1536,384]{1,0:T(8,128)(2,1)S(1)} %copy-done.40), channel_id=1, source_target_pairs={{0,16},{16,0},{1,17},{17,1},{2,18},{18,2},{3,19},{19,3},{4,20},{20... | collective-permute-start | bytes 3538952 | tf_op jit(solution)/shard_map/ppermute | solution.py:38
  141.0 49.8 %collective-permute-start.8 = (bf16[1536,384]{1,0:T(8,128)(2,1)S(1)}, bf16[1536,384]{1,0:T(8,128)(2,1)S(1)}, u32[]{:S(2)}, u32[]{:S(2)}) collective-permute-start(bf16[1536,384]{1,0:T(8,128)(2,1)S(1)} %pad_maximum_fusion.14), channel_id=1, source_target_pairs={{0,1},{1,0},{2,3},{3,2},{4,5},{5,4},{6,7},{7,6},{8,9},{9,8},{10,11... | collective-permute-start | bytes 3538952 | tf_op jit(solution)/shard_map/ppermute | solution.py:38
  145.2 50.1 %collective-permute-start.18 = (bf16[1536,384]{1,0:T(8,128)(2,1)S(1)}, bf16[1536,384]{1,0:T(8,128)(2,1)S(1)}, u32[]{:S(2)}, u32[]{:S(2)}) collective-permute-start(bf16[1536,384]{1,0:T(8,128)(2,1)S(1)} %pad_maximum_fusion.15), channel_id=1, source_target_pairs={{0,1},{1,0},{2,3},{3,2},{4,5},{5,4},{6,7},{7,6},{8,9},{9,8},{10,11... | collective-permute-start | bytes 3538952 | tf_op jit(solution)/shard_map/ppermute | solution.py:38
  147.0 45.4 %collective-permute-start.9 = (bf16[2048,384]{1,0:T(8,128)(2,1)S(1)}, bf16[2048,384]{1,0:T(8,128)(2,1)S(1)}, u32[]{:S(2)}, u32[]{:S(2)}) collective-permute-start(bf16[2048,384]{1,0:T(8,128)(2,1)S(1)} %pad_maximum_fusion.6), channel_id=1, source_target_pairs={{0,1},{1,0},{2,3},{3,2},{4,5},{5,4},{6,7},{7,6},{8,9},{9,8},{10,11... | collective-permute-start | bytes 4718600 | tf_op jit(solution)/shard_map/ppermute | solution.py:38
  154.6 40.8 %collective-permute-start.19 = (bf16[2048,384]{1,0:T(8,128)(2,1)S(1)}, bf16[2048,384]{1,0:T(8,128)(2,1)S(1)}, u32[]{:S(2)}, u32[]{:S(2)}) collective-permute-start(bf16[2048,384]{1,0:T(8,128)(2,1)S(1)} %pad_maximum_fusion.7), channel_id=1, source_target_pairs={{0,1},{1,0},{2,3},{3,2},{4,5},{5,4},{6,7},{7,6},{8,9},{9,8},{10,11... | collective-permute-start | bytes 4718600 | tf_op jit(solution)/shard_map/ppermute | solution.py:38
  185.2 67.0 %collective-permute-start.34 = (bf16[384,1536]{1,0:T(8,128)(2,1)}, bf16[384,1536]{1,0:T(8,128)(2,1)}, u32[]{:S(2)}, u32[]{:S(2)}) collective-permute-start(bf16[384,1536]{1,0:T(8,128)(2,1)} %fusion.20), channel_id=1, source_target_pairs={{0,16},{16,0},{1,17},{17,1},{2,18},{18,2},{3,19},{19,3},{4,20},{20... | collective-permute-start | bytes 3538952 | tf_op jit(solution)/shard_map/ppermute | solution.py:38
  190.8 65.6 %collective-permute-start.39 = (bf16[384,1536]{1,0:T(8,128)(2,1)}, bf16[384,1536]{1,0:T(8,128)(2,1)}, u32[]{:S(2)}, u32[]{:S(2)}) collective-permute-start(bf16[384,1536]{1,0:T(8,128)(2,1)} %fusion.21), channel_id=1, source_target_pairs={{0,16},{16,0},{1,17},{17,1},{2,18},{18,2},{3,19},{19,3},{4,20},{20... | collective-permute-start | bytes 3538952 | tf_op jit(solution)/shard_map/ppermute | solution.py:38
  245.0 16.5 %collective-permute-start.25 = (f32[4,16,128]{2,1,0:T(8,128)}, f32[4,16,128]{2,1,0:T(8,128)S(1)}, u32[]{:S(2)}, u32[]{:S(2)}) collective-permute-start(f32[4,16,128]{2,1,0:T(8,128)} %get-tuple-element.31), channel_id=1, source_target_pairs={{0,4},{2,6},{4,0},{6,2},{8,12},{10,14},{12,8},{14,10},{1,5},{3,7},... | collective-permute-start | bytes 98312 | tf_op jit(solution)/shard_map/ppermute | solution.py:38
  247.8 14.6 %collective-permute-start.26 = (f32[4,16,128]{2,1,0:T(8,128)}, f32[4,16,128]{2,1,0:T(8,128)S(1)}, u32[]{:S(2)}, u32[]{:S(2)}) collective-permute-start(f32[4,16,128]{2,1,0:T(8,128)} %get-tuple-element.31), channel_id=1, source_target_pairs={{0,8},{2,10},{4,12},{6,14},{8,0},{10,2},{12,4},{14,6},{1,9},{3,11}... | collective-permute-start | bytes 98312 | tf_op jit(solution)/shard_map/ppermute | solution.py:38
  249.0 14.6 %collective-permute-start.27 = (f32[4,16,128]{2,1,0:T(8,128)}, f32[4,16,128]{2,1,0:T(8,128)S(1)}, u32[]{:S(2)}, u32[]{:S(2)}) collective-permute-start(f32[4,16,128]{2,1,0:T(8,128)} %get-tuple-element.31), channel_id=1, source_target_pairs={{0,12},{2,14},{4,8},{6,10},{8,4},{10,6},{12,0},{14,2},{1,13},{3,15... | collective-permute-start | bytes 98312 | tf_op jit(solution)/shard_map/ppermute | solution.py:38
  252.1 12.3 %collective-permute-start.28 = (f32[4,16,128]{2,1,0:T(8,128)}, f32[4,16,128]{2,1,0:T(8,128)S(1)}, u32[]{:S(2)}, u32[]{:S(2)}) collective-permute-start(f32[4,16,128]{2,1,0:T(8,128)} %get-tuple-element.31), channel_id=1, source_target_pairs={{0,2},{2,0},{4,6},{6,4},{8,10},{10,8},{12,14},{14,12},{1,3},{3,1},... | collective-permute-start | bytes 98312 | tf_op jit(solution)/shard_map/ppermute | solution.py:38
  257.0 102.4 %collective-permute-start.35 = (bf16[4,48,1536]{2,1,0:T(8,128)(2,1)}, bf16[4,48,1536]{2,1,0:T(8,128)(2,1)}, u32[]{:S(2)}, u32[]{:S(2)}) collective-permute-start(bf16[4,48,1536]{2,1,0:T(8,128)(2,1)} %fusion.23), channel_id=1, source_target_pairs={{0,2},{2,0},{4,6},{6,4},{8,10},{10,8},{12,14},{14,12},{1,3},{3,1},... | collective-permute-start | bytes 1769480 | tf_op jit(solution)/shard_map/ppermute | solution.py:38
  261.4 103.2 %collective-permute-start.40 = (bf16[4,48,1536]{2,1,0:T(8,128)(2,1)}, bf16[4,48,1536]{2,1,0:T(8,128)(2,1)}, u32[]{:S(2)}, u32[]{:S(2)}) collective-permute-start(bf16[4,48,1536]{2,1,0:T(8,128)(2,1)} %fusion.24), channel_id=1, source_target_pairs={{0,2},{2,0},{4,6},{6,4},{8,10},{10,8},{12,14},{14,12},{1,3},{3,1},... | collective-permute-start | bytes 1769480 | tf_op jit(solution)/shard_map/ppermute | solution.py:38
  262.4 22.9 %collective-permute-start.29 = (f32[4,16,128]{2,1,0:T(8,128)S(1)}, f32[4,16,128]{2,1,0:T(8,128)S(1)}, u32[]{:S(2)}, u32[]{:S(2)}) collective-permute-start(f32[4,16,128]{2,1,0:T(8,128)S(1)} %collective-permute-done.25), channel_id=1, source_target_pairs={{0,2},{2,0},{4,6},{6,4},{8,10},{10,8},{12,14},{14,12},{1,3},{3,1},... | collective-permute-start | bytes 98312 | tf_op jit(solution)/shard_map/ppermute | solution.py:38
  263.6 22.1 %collective-permute-start.30 = (f32[4,16,128]{2,1,0:T(8,128)S(1)}, f32[4,16,128]{2,1,0:T(8,128)S(1)}, u32[]{:S(2)}, u32[]{:S(2)}) collective-permute-start(f32[4,16,128]{2,1,0:T(8,128)S(1)} %collective-permute-done.26), channel_id=1, source_target_pairs={{0,2},{2,0},{4,6},{6,4},{8,10},{10,8},{12,14},{14,12},{1,3},{3,1},... | collective-permute-start | bytes 98312 | tf_op jit(solution)/shard_map/ppermute | solution.py:38
  264.4 21.5 %collective-permute-start.31 = (f32[4,16,128]{2,1,0:T(8,128)S(1)}, f32[4,16,128]{2,1,0:T(8,128)S(1)}, u32[]{:S(2)}, u32[]{:S(2)}) collective-permute-start(f32[4,16,128]{2,1,0:T(8,128)S(1)} %collective-permute-done.27), channel_id=1, source_target_pairs={{0,2},{2,0},{4,6},{6,4},{8,10},{10,8},{12,14},{14,12},{1,3},{3,1},... | collective-permute-start | bytes 98312 | tf_op jit(solution)/shard_map/ppermute | solution.py:38
  310.0 22.6 %collective-permute-start.24 = (bf16[512,384]{1,0:T(8,128)(2,1)}, bf16[512,384]{1,0:T(8,128)(2,1)}, u32[]{:S(2)}, u32[]{:S(2)}) collective-permute-start(bf16[512,384]{1,0:T(8,128)(2,1)} %select_convert_fusion.1), channel_id=1, source_target_pairs={{0,1},{1,0},{2,3},{3,2},{4,5},{5,4},{6,7},{7,6},{8,9},{9,8},{10,11... | collective-permute-start | bytes 1179656 | tf_op jit(solution)/shard_map/ppermute | solution.py:38
  315.3 6.9 %collective-permute-start.62 = (f32[3840]{0:T(1024)S(1)}, f32[3840]{0:T(1024)S(1)}, u32[]{:S(2)}, u32[]{:S(2)}) collective-permute-start(f32[3840]{0:T(1024)S(1)} %pad_maximum_fusion.25), channel_id=1, source_target_pairs={{0,2},{2,0},{4,6},{6,4},{8,10},{10,8},{12,14},{14,12},{1,3},{3,1},... | collective-permute-start | bytes 46088 | tf_op jit(solution)/shard_map/ppermute | solution.py:38
  326.0 4.6 collective-permute-start.64
  326.2 41.0 %collective-permute-start.44 = (bf16[384,1536]{1,0:T(8,128)(2,1)S(1)}, bf16[384,1536]{1,0:T(8,128)(2,1)}, u32[]{:S(2)}, u32[]{:S(2)}) collective-permute-start(bf16[384,1536]{1,0:T(8,128)(2,1)S(1)} %fusion.22), channel_id=1, source_target_pairs={{0,16},{16,0},{1,17},{17,1},{2,18},{18,2},{3,19},{19,3},{4,20},{20... | collective-permute-start | bytes 3538952 | tf_op jit(solution)/shard_map/ppermute | solution.py:38
  330.7 22.8 %collective-permute-start.65 = (f32[3840]{0:T(1024)S(1)}, f32[3840]{0:T(1024)S(1)}, u32[]{:S(2)}, u32[]{:S(2)}) collective-permute-start(f32[3840]{0:T(1024)S(1)} %add.421), channel_id=1, source_target_pairs={{0,16},{16,0},{1,17},{17,1},{2,18},{18,2},{3,19},{19,3},{4,20},{20... | collective-permute-start | bytes 46088 | tf_op jit(solution)/shard_map/ppermute | solution.py:38
  355.4 65.2 %collective-permute-start.66 = (f32[3,384]{1,0:T(4,128)}, f32[3,384]{1,0:T(4,128)}, u32[]{:S(2)}, u32[]{:S(2)}) collective-permute-start(f32[3,384]{1,0:T(4,128)} %slice.167), channel_id=1, source_target_pairs={{0,1},{1,0},{2,3},{3,2},{4,5},{5,4},{6,7},{7,6},{8,9},{9,8},{10,11... | collective-permute-start | bytes 13832 | tf_op jit(solution)/shard_map/ppermute | solution.py:38
  361.1 9.1 %collective-permute-start.36 = (bf16[48,1536]{1,0:T(8,128)(2,1)S(1)}, bf16[48,1536]{1,0:T(8,128)(2,1)S(1)}, u32[]{:S(2)}, u32[]{:S(2)}) collective-permute-start(bf16[48,1536]{1,0:T(8,128)(2,1)S(1)} %get-tuple-element.138), channel_id=1, source_target_pairs={{0,4},{2,6},{4,0},{6,2},{8,12},{10,14},{12,8},{14,10},{1,5},{3,7},... | collective-permute-start | bytes 442376 | tf_op jit(solution)/shard_map/ppermute | solution.py:38
  362.9 14.0 %collective-permute-start.37 = (bf16[48,1536]{1,0:T(8,128)(2,1)S(1)}, bf16[48,1536]{1,0:T(8,128)(2,1)S(1)}, u32[]{:S(2)}, u32[]{:S(2)}) collective-permute-start(bf16[48,1536]{1,0:T(8,128)(2,1)S(1)} %get-tuple-element.140), channel_id=1, source_target_pairs={{0,8},{2,10},{4,12},{6,14},{8,0},{10,2},{12,4},{14,6},{1,9},{3,11}... | collective-permute-start | bytes 442376 | tf_op jit(solution)/shard_map/ppermute | solution.py:38
  364.7 12.3 %collective-permute-start.38 = (bf16[48,1536]{1,0:T(8,128)(2,1)S(1)}, bf16[48,1536]{1,0:T(8,128)(2,1)S(1)}, u32[]{:S(2)}, u32[]{:S(2)}) collective-permute-start(bf16[48,1536]{1,0:T(8,128)(2,1)S(1)} %get-tuple-element.139), channel_id=1, source_target_pairs={{0,12},{2,14},{4,8},{6,10},{8,4},{10,6},{12,0},{14,2},{1,13},{3,15... | collective-permute-start | bytes 442376 | tf_op jit(solution)/shard_map/ppermute | solution.py:38
  368.9 15.0 %collective-permute-start.45 = (bf16[4,48,1536]{2,1,0:T(8,128)(2,1)S(1)}, bf16[4,48,1536]{2,1,0:T(8,128)(2,1)S(1)}, u32[]{:S(2)}, u32[]{:S(2)}) collective-permute-start(bf16[4,48,1536]{2,1,0:T(8,128)(2,1)S(1)} %fusion.25), channel_id=1, source_target_pairs={{0,2},{2,0},{4,6},{6,4},{8,10},{10,8},{12,14},{14,12},{1,3},{3,1},... | collective-permute-start | bytes 1769480 | tf_op jit(solution)/shard_map/ppermute | solution.py:38
  370.3 19.2 %collective-permute-start.41 = (bf16[48,1536]{1,0:T(8,128)(2,1)S(1)}, bf16[48,1536]{1,0:T(8,128)(2,1)S(1)}, u32[]{:S(2)}, u32[]{:S(2)}) collective-permute-start(bf16[48,1536]{1,0:T(8,128)(2,1)S(1)} %get-tuple-element.141), channel_id=1, source_target_pairs={{0,4},{2,6},{4,0},{6,2},{8,12},{10,14},{12,8},{14,10},{1,5},{3,7},... | collective-permute-start | bytes 442376 | tf_op jit(solution)/shard_map/ppermute | solution.py:38
  376.9 13.0 %collective-permute-start.42 = (bf16[48,1536]{1,0:T(8,128)(2,1)S(1)}, bf16[48,1536]{1,0:T(8,128)(2,1)S(1)}, u32[]{:S(2)}, u32[]{:S(2)}) collective-permute-start(bf16[48,1536]{1,0:T(8,128)(2,1)S(1)} %get-tuple-element.143), channel_id=1, source_target_pairs={{0,8},{2,10},{4,12},{6,14},{8,0},{10,2},{12,4},{14,6},{1,9},{3,11}... | collective-permute-start | bytes 442376 | tf_op jit(solution)/shard_map/ppermute | solution.py:38
  376.9 15.0 %collective-permute-start.43 = (bf16[48,1536]{1,0:T(8,128)(2,1)S(1)}, bf16[48,1536]{1,0:T(8,128)(2,1)S(1)}, u32[]{:S(2)}, u32[]{:S(2)}) collective-permute-start(bf16[48,1536]{1,0:T(8,128)(2,1)S(1)} %get-tuple-element.142), channel_id=1, source_target_pairs={{0,12},{2,14},{4,8},{6,10},{8,4},{10,6},{12,0},{14,2},{1,13},{3,15... | collective-permute-start | bytes 442376 | tf_op jit(solution)/shard_map/ppermute | solution.py:38
  384.2 9.7 %collective-permute-start.46 = (bf16[48,1536]{1,0:T(8,128)(2,1)S(1)}, bf16[48,1536]{1,0:T(8,128)(2,1)S(1)}, u32[]{:S(2)}, u32[]{:S(2)}) collective-permute-start(bf16[48,1536]{1,0:T(8,128)(2,1)S(1)} %get-tuple-element.144), channel_id=1, source_target_pairs={{0,4},{2,6},{4,0},{6,2},{8,12},{10,14},{12,8},{14,10},{1,5},{3,7},... | collective-permute-start | bytes 442376 | tf_op jit(solution)/shard_map/ppermute | solution.py:38
  389.5 12.9 %collective-permute-start.47 = (bf16[48,1536]{1,0:T(8,128)(2,1)S(1)}, bf16[48,1536]{1,0:T(8,128)(2,1)S(1)}, u32[]{:S(2)}, u32[]{:S(2)}) collective-permute-start(bf16[48,1536]{1,0:T(8,128)(2,1)S(1)} %get-tuple-element.146), channel_id=1, source_target_pairs={{0,8},{2,10},{4,12},{6,14},{8,0},{10,2},{12,4},{14,6},{1,9},{3,11}... | collective-permute-start | bytes 442376 | tf_op jit(solution)/shard_map/ppermute | solution.py:38
  389.9 12.5 %collective-permute-start.48 = (bf16[48,1536]{1,0:T(8,128)(2,1)S(1)}, bf16[48,1536]{1,0:T(8,128)(2,1)S(1)}, u32[]{:S(2)}, u32[]{:S(2)}) collective-permute-start(bf16[48,1536]{1,0:T(8,128)(2,1)S(1)} %get-tuple-element.145), channel_id=1, source_target_pairs={{0,12},{2,14},{4,8},{6,10},{8,4},{10,6},{12,0},{14,2},{1,13},{3,15... | collective-permute-start | bytes 442376 | tf_op jit(solution)/shard_map/ppermute | solution.py:38
  402.7 7.2 %collective-permute-start.49 = (bf16[48,1536]{1,0:T(8,128)(2,1)S(1)}, bf16[48,1536]{1,0:T(8,128)(2,1)S(1)}, u32[]{:S(2)}, u32[]{:S(2)}) collective-permute-start(bf16[48,1536]{1,0:T(8,128)(2,1)S(1)} %get-tuple-element.161), channel_id=1, source_target_pairs={{0,4},{2,6},{4,0},{6,2},{8,12},{10,14},{12,8},{14,10},{1,5},{3,7},... | collective-permute-start | bytes 442376 | tf_op jit(solution)/shard_map/ppermute | solution.py:38
  405.7 13.1 %collective-permute-start.50 = (bf16[48,1536]{1,0:T(8,128)(2,1)S(1)}, bf16[48,1536]{1,0:T(8,128)(2,1)S(1)}, u32[]{:S(2)}, u32[]{:S(2)}) collective-permute-start(bf16[48,1536]{1,0:T(8,128)(2,1)S(1)} %get-tuple-element.160), channel_id=1, source_target_pairs={{0,8},{2,10},{4,12},{6,14},{8,0},{10,2},{12,4},{14,6},{1,9},{3,11}... | collective-permute-start | bytes 442376 | tf_op jit(solution)/shard_map/ppermute | solution.py:38
  406.3 12.4 %collective-permute-start.51 = (bf16[48,1536]{1,0:T(8,128)(2,1)S(1)}, bf16[48,1536]{1,0:T(8,128)(2,1)S(1)}, u32[]{:S(2)}, u32[]{:S(2)}) collective-permute-start(bf16[48,1536]{1,0:T(8,128)(2,1)S(1)} %get-tuple-element.159), channel_id=1, source_target_pairs={{0,12},{2,14},{4,8},{6,10},{8,4},{10,6},{12,0},{14,2},{1,13},{3,15... | collective-permute-start | bytes 442376 | tf_op jit(solution)/shard_map/ppermute | solution.py:38
  419.6 11.2 %collective-permute-start.52 = (bf16[192,1536]{1,0:T(8,128)(2,1)}, bf16[192,1536]{1,0:T(8,128)(2,1)}, u32[]{:S(2)}, u32[]{:S(2)}) collective-permute-start(bf16[192,1536]{1,0:T(8,128)(2,1)} %pad_maximum_fusion.19), channel_id=1, source_target_pairs={{0,2},{2,0},{4,6},{6,4},{8,10},{10,8},{12,14},{14,12},{1,3},{3,1},... | collective-permute-start | bytes 1769480 | tf_op jit(solution)/shard_map/ppermute | solution.py:38
  422.1 14.3 %collective-permute-start.53 = (bf16[192,1536]{1,0:T(8,128)(2,1)}, bf16[192,1536]{1,0:T(8,128)(2,1)S(1)}, u32[]{:S(2)}, u32[]{:S(2)}) collective-permute-start(bf16[192,1536]{1,0:T(8,128)(2,1)} %pad_maximum_fusion.19), channel_id=1, source_target_pairs={{0,16},{16,0},{1,17},{17,1},{2,18},{18,2},{3,19},{19,3},{4,20},{20... | collective-permute-start | bytes 1769480 | tf_op jit(solution)/shard_map/ppermute | solution.py:38
  423.9 25.7 %collective-permute-start.55 = (bf16[192,1536]{1,0:T(8,128)(2,1)}, bf16[192,1536]{1,0:T(8,128)(2,1)S(1)}, u32[]{:S(2)}, u32[]{:S(2)}) collective-permute-start(bf16[192,1536]{1,0:T(8,128)(2,1)} %pad_maximum_fusion.19), channel_id=1, source_target_pairs={{0,1},{1,0},{2,3},{3,2},{4,5},{5,4},{6,7},{7,6},{8,9},{9,8},{10,11... | collective-permute-start | bytes 1769480 | tf_op jit(solution)/shard_map/ppermute | solution.py:38
  430.8 15.1 %collective-permute-start.54 = (bf16[192,1536]{1,0:T(8,128)(2,1)}, bf16[192,1536]{1,0:T(8,128)(2,1)S(1)}, u32[]{:S(2)}, u32[]{:S(2)}) collective-permute-start(bf16[192,1536]{1,0:T(8,128)(2,1)} %collective-permute-done.52), channel_id=1, source_target_pairs={{0,16},{16,0},{1,17},{17,1},{2,18},{18,2},{3,19},{19,3},{4,20},{20... | collective-permute-start | bytes 1769480 | tf_op jit(solution)/shard_map/ppermute | solution.py:38
  435.5 14.0 %collective-permute-start.56 = (bf16[192,1536]{1,0:T(8,128)(2,1)}, bf16[192,1536]{1,0:T(8,128)(2,1)S(1)}, u32[]{:S(2)}, u32[]{:S(2)}) collective-permute-start(bf16[192,1536]{1,0:T(8,128)(2,1)} %collective-permute-done.52), channel_id=1, source_target_pairs={{0,1},{1,0},{2,3},{3,2},{4,5},{5,4},{6,7},{7,6},{8,9},{9,8},{10,11... | collective-permute-start | bytes 1769480 | tf_op jit(solution)/shard_map/ppermute | solution.py:38
  436.3 13.2 %collective-permute-start.57 = (bf16[192,1536]{1,0:T(8,128)(2,1)S(1)}, bf16[192,1536]{1,0:T(8,128)(2,1)S(1)}, u32[]{:S(2)}, u32[]{:S(2)}) collective-permute-start(bf16[192,1536]{1,0:T(8,128)(2,1)S(1)} %collective-permute-done.53), channel_id=1, source_target_pairs={{0,1},{1,0},{2,3},{3,2},{4,5},{5,4},{6,7},{7,6},{8,9},{9,8},{10,11... | collective-permute-start | bytes 1769480 | tf_op jit(solution)/shard_map/ppermute | solution.py:38
  491.0 12.0 %collective-permute-start.59 = (bf16[48,1536]{1,0:T(8,128)(2,1)S(1)}, bf16[48,1536]{1,0:T(8,128)(2,1)S(1)}, u32[]{:S(2)}, u32[]{:S(2)}) collective-permute-start(bf16[48,1536]{1,0:T(8,128)(2,1)S(1)} %get-tuple-element.158), channel_id=1, source_target_pairs={{0,4},{2,6},{4,0},{6,2},{8,12},{10,14},{12,8},{14,10},{1,5},{3,7},... | collective-permute-start | bytes 442376 | tf_op jit(solution)/shard_map/ppermute | solution.py:38
  496.9 13.9 %collective-permute-start.60 = (bf16[48,1536]{1,0:T(8,128)(2,1)S(1)}, bf16[48,1536]{1,0:T(8,128)(2,1)S(1)}, u32[]{:S(2)}, u32[]{:S(2)}) collective-permute-start(bf16[48,1536]{1,0:T(8,128)(2,1)S(1)} %get-tuple-element.157), channel_id=1, source_target_pairs={{0,8},{2,10},{4,12},{6,14},{8,0},{10,2},{12,4},{14,6},{1,9},{3,11}... | collective-permute-start | bytes 442376 | tf_op jit(solution)/shard_map/ppermute | solution.py:38
  496.9 13.9 %collective-permute-start.61 = (bf16[48,1536]{1,0:T(8,128)(2,1)S(1)}, bf16[48,1536]{1,0:T(8,128)(2,1)S(1)}, u32[]{:S(2)}, u32[]{:S(2)}) collective-permute-start(bf16[48,1536]{1,0:T(8,128)(2,1)S(1)} %get-tuple-element.156), channel_id=1, source_target_pairs={{0,12},{2,14},{4,8},{6,10},{8,4},{10,6},{12,0},{14,2},{1,13},{3,15... | collective-permute-start | bytes 442376 | tf_op jit(solution)/shard_map/ppermute | solution.py:38
  (64 other events, 862.9 us)
Sparse Core Ops, SparseCore 0:
  422.2 65.7 all-gather.1

commit v2 on v1

v2 whole, which is shorter than its diff:
```python
from functools import partial
import math

import jax
import jax.numpy as jnp
from jax import lax
from jax.experimental import pallas as pl
from jax.experimental.pallas import tpu as pltpu
from jax.sharding import PartitionSpec as P

HD = 64
ROT = 16
BLK = 128
NS_STEPS = 5
CHUNK = 512
MAX_LEN = 2048
SPAN = (MAX_LEN + BLK) // CHUNK + 2
OWNERS = 4
NS_COEF = (3.4445, -4.775, 2.0315)
NEG_BIG = -1e30
SCALE = HD**-0.5
LOW = jnp.bfloat16
WIDE = jnp.float32
NT = (((1,), (1,)), ((), ()))
VMEM_ASK = 56 * 1024 * 1024


def dot_nn(left, right):
    return jnp.dot(left, right, preferred_element_type=WIDE)


def dot_nt(left, right):
    return lax.dot_general(left, right, NT, preferred_element_type=WIDE)


def partner(value, axis, step):
    size = lax.axis_size(axis)
    return lax.ppermute(value, axis, [(i, i ^ step) for i in range(size)])


def partner_among(value, axes, strides, wanted):
    sizes = [lax.axis_size(axis) for axis in axes]
    pairs = []
    for flat in range(math.prod(sizes)):
        index, rest = [], flat
        for size in reversed(sizes):
            index.insert(0, rest % size)
            rest //= size
        if wanted(index):
            source = 0
            for size, i, stride in zip(sizes, index, strides):
                source = source * size + (i ^ stride)
            pairs.append((source, flat))
    return lax.ppermute(value, tuple(axes), pairs)


def sum_scatter(pieces, axis, stride, index):
    count = pieces.shape[0]
    total = lax.dynamic_index_in_dim(pieces, index, 0, keepdims=False).astype(WIDE)
    for step in range(1, count):
        piece = lax.dynamic_index_in_dim(pieces, index ^ step, 0, keepdims=False)
        total = total + partner(piece.astype(LOW), axis, step * stride).astype(WIDE)
    return total


def gather_axis(shard, axis, dim):
    if lax.axis_size(axis) != 2:
        return lax.all_gather(shard, axis, axis=dim, tiled=True)
    other = partner(shard, axis, 1)
    first = lax.axis_index(axis) == 0
    return jnp.concatenate(
        [jnp.where(first, shard, other), jnp.where(first, other, shard)], axis=dim
    )


def sum_everywhere(value, axes):
    for axis in axes:
        step = 1
        while step < lax.axis_size(axis):
            value = value + partner(value, axis, step)
            step *= 2
    return value


def turned(block, cosine, sine, lane):
    half = ROT // 2
    swapped = jnp.where(
        lane % HD < half, pltpu.roll(block, BLK - half, 1), pltpu.roll(block, half, 1)
    )
    return block * cosine + swapped * sine


def two_heads(block, lane):
    zero = jnp.zeros_like(block)
    return jnp.concatenate(
        [jnp.where(lane < HD, block, zero), jnp.where(lane < HD, zero, block)], axis=0
    )


def one_of_two(stacked, lane):
    return jnp.where(lane < HD, stacked[:BLK], stacked[BLK:])


def project_kernel(
    near, far, w_near, w_far, bias, vec_near, vec_far, cos_ref, sin_ref, *outs
):
    outs = outs[-4:]
    half = outs[0].shape[1]
    width = 2 * half
    own, other = near[:, :half].astype(WIDE), far[:, :half].astype(WIDE)
    mean = (
        jnp.sum(own, axis=1, keepdims=True) + jnp.sum(other, axis=1, keepdims=True)
    ) / width
    own, other = own - mean, other - mean
    var = (
        jnp.sum(own * own, axis=1, keepdims=True) + jnp.sum(other * other, axis=1, keepdims=True)
    ) / width
    inv_std = lax.rsqrt(var + 1e-5)
    own = (own * inv_std * vec_near[0:1] + vec_near[1:2]).astype(LOW)
    other = (other * inv_std * vec_far[0:1] + vec_far[1:2]).astype(LOW)
    lane = lax.broadcasted_iota(jnp.int32, (own.shape[0], BLK), 1)
    cosine, sine = cos_ref[...], sin_ref[...]
    for part, out in enumerate(outs[:3]):
        span = slice(part * half, (part + 1) * half)
        made = dot_nn(own, w_near[:, span]) + dot_nn(other, w_far[:, span]) + bias[:, span]
        for pair in range(half // BLK):
            lanes = slice(pair * BLK, (pair + 1) * BLK)
            block = made[:, lanes]
            if part < 2:
                block = turned(block, cosine, sine, lane)
            out[:, lanes] = block.astype(LOW)
    span = slice(3 * half, 4 * half)
    outs[3][...] = (
        dot_nn(near[:, half:], w_near[:, span]) + dot_nn(far[:, half:], w_far[:, span])
    ).astype(LOW)


def project_rows(part, pack, near, far, weights, cosine, sine, made):
    rows = near.shape[0]
    half = near.shape[1] // 2
    base = part * (rows // CHUNK)

    def fixed(array):
        return pl.BlockSpec(array.shape, lambda i: (0,) * array.ndim)

    def placed(width):
        return pl.BlockSpec((CHUNK, width), lambda i: (i + base, 0))

    here = pl.BlockSpec((CHUNK, 2 * half), lambda i: (i, 0))
    before = 4 + len(weights)
    return pl.pallas_call(
        project_kernel,
        grid=(rows // CHUNK,),
        in_specs=[here] * 2
        + [fixed(w) for w in weights]
        + [placed(BLK)] * 2
        + [pl.BlockSpec(memory_space=pl.ANY)] * len(made),
        out_specs=[placed(half)] * 4,
        out_shape=[jax.ShapeDtypeStruct((pack, half), LOW)] * 4,
        input_output_aliases={before + i: i for i in range(len(made))},
        compiler_params=pltpu.CompilerParams(vmem_limit_bytes=VMEM_ASK),
        cost_estimate=pl.CostEstimate(
            flops=48 * rows * half * half, bytes_accessed=20 * rows * half, transcendentals=0
        ),
        name="project_rows",
    )(near, far, *weights, cosine, sine, *made)


def feed_kernel(
    x_ref,
    xt_ref,
    g_ref,
    gt_ref,
    up_ref,
    down_ref,
    bias_ref,
    out_ref,
    dx_ref,
    dup_ref,
    ddown_ref,
    dbias_ref,
):
    hidden = dot_nn(x_ref[...], up_ref[...]) + bias_ref[...]
    grad = dot_nn(g_ref[...], down_ref[...])
    below = 0.5 + 0.5 * lax.erf(hidden * math.sqrt(0.5))
    density = jnp.exp(-0.5 * hidden * hidden) * (1.0 / math.sqrt(2.0 * math.pi))
    active = (hidden * below).astype(LOW)
    grad = (grad * (below + hidden * density)).astype(LOW)
    dbias_ref[...] = jnp.sum(grad.astype(WIDE), axis=0, keepdims=True)
    out = dot_nt(active, down_ref[...])
    dx = dot_nt(grad, up_ref[...])

    @pl.when(pl.program_id(0) == 0)
    def _():
        out_ref[...] = out
        dx_ref[...] = dx

    @pl.when(pl.program_id(0) != 0)
    def _():
        out_ref[...] += out
        dx_ref[...] += dx

    dup_ref[...] = dot_nn(xt_ref[...], grad).astype(LOW)
    ddown_ref[...] = dot_nn(gt_ref[...], active).astype(LOW)


def feed_forward(x, g, up_down, bias):
    rows, width = x.shape
    hidden = bias.shape[1]
    step = 512
    steps = hidden // step

    def whole(shape):
        return pl.BlockSpec(shape, lambda i: (0, 0))

    column = pl.BlockSpec((width, step), lambda i: (0, i))
    return pl.pallas_call(
        feed_kernel,
        grid=(steps,),
        in_specs=[
            whole((rows, width)),
            whole((width, rows)),
            whole((rows, width)),
            whole((width, rows)),
            column,
            pl.BlockSpec((width, step), lambda i: (0, i + steps)),
            pl.BlockSpec((1, step), lambda i: (0, i)),
        ],
        out_specs=[
            whole((rows, width)),
            whole((rows, width)),
            column,
            column,
            pl.BlockSpec((1, step), lambda i: (0, i)),
        ],
        out_shape=[
            jax.ShapeDtypeStruct((rows, width), WIDE),
            jax.ShapeDtypeStruct((rows, width), WIDE),
            jax.ShapeDtypeStruct((width, hidden), LOW),
            jax.ShapeDtypeStruct((width, hidden), LOW),
            jax.ShapeDtypeStruct((1, hidden), WIDE),
        ],
        compiler_params=pltpu.CompilerParams(vmem_limit_bytes=VMEM_ASK),
        cost_estimate=pl.CostEstimate(
            flops=20 * rows * width * hidden, bytes_accessed=12 * width * hidden, transcendentals=0
        ),
        name="feed_forward",
    )(x, x.T, g, g.T, up_down, up_down, bias)


def lane_tiles(array, combine):
    total = array[:, :BLK]
    for i in range(1, array.shape[1] // BLK):
        total = combine(total, array[:, i * BLK : (i + 1) * BLK])
    return total


def gathered_blocks(ref, inverse, chunk, lanes):
    count = CHUNK // BLK
    return jnp.concatenate(
        [
            ref[pl.ds(pl.multiple_of(inverse[chunk * count + i] * BLK, BLK), BLK), lanes]
            for i in range(count)
        ],
        axis=0,
    )


def query_kernel(
    blocks,
    first,
    last,
    inverse,
    q_ref,
    k_ref,
    v_ref,
    d_ref,
    cos_ref,
    sin_ref,
    start_ref,
    att_out,
    dq_out,
    stat_out,
    s_scr,
    p_scr,
    q_scr,
    d_scr,
    m_scr,
    l_scr,
    e_scr,
    o_scr,
):
    pairs = q_ref.shape[1] // BLK
    own = att_out.shape[0] // BLK
    lane = lax.broadcasted_iota(jnp.int32, (BLK, BLK), 1)

    def lanes(pair):
        return slice(pair * BLK, (pair + 1) * BLK)

    @pl.loop(0, own)
    def _(j):
        row0 = pl.multiple_of(blocks[j] * BLK, BLK)
        out0 = pl.multiple_of(j * BLK, BLK)
        lo = first[j]
        hi = last[j]
        for g in range(pairs):
            q_scr[g] = two_heads(q_ref[pl.ds(out0, BLK), lanes(g)].astype(WIDE), lane).astype(
                LOW
            ) * LOW(SCALE)
            d_scr[g] = two_heads(d_ref[pl.ds(out0, BLK), lanes(g)].astype(WIDE), lane).astype(LOW)
        m_scr[...] = jnp.full(m_scr.shape, NEG_BIG, WIDE)
        l_scr[...] = jnp.zeros(l_scr.shape, WIDE)
        e_scr[...] = jnp.zeros(e_scr.shape, WIDE)
        o_scr[...] = jnp.zeros(o_scr.shape, WIDE)
        starts = start_ref[pl.ds(out0, BLK), :]
        places = row0 + lax.broadcasted_iota(jnp.int32, (BLK, 1), 0)
        starts = jnp.concatenate([starts, starts], axis=0)
        places = jnp.concatenate([places, places], axis=0)

        @pl.loop(lo, hi)
        def _(c):
            key0 = pl.multiple_of(c * CHUNK, CHUNK)
            key_place = key0 + lax.broadcasted_iota(jnp.int32, (2 * BLK, CHUNK), 1)
            allowed = (key_place >= starts) & (key_place <= places)
            for g in range(pairs):
                scores = dot_nt(q_scr[g], gathered_blocks(k_ref, inverse, c, lanes(g)))
                scores = jnp.where(allowed, scores, NEG_BIG)
                s_scr[g, c - lo] = scores
                m_scr[g] = jnp.maximum(m_scr[g], lane_tiles(scores, jnp.maximum))

        for g in range(pairs):
            m_scr[g] = jnp.broadcast_to(
                jnp.max(m_scr[g], axis=1, keepdims=True), (2 * BLK, BLK)
            )

        @pl.loop(lo, hi)
        def _(c):
            for g in range(pairs):
                values = gathered_blocks(v_ref, inverse, c, lanes(g))
                top = m_scr[g]
                weights = jnp.exp(s_scr[g, c - lo] - jnp.concatenate([top] * (CHUNK // BLK), 1))
                l_scr[g] += lane_tiles(weights, jnp.add)
                o_scr[g] += dot_nn(weights.astype(LOW), values)
                grad_prob = dot_nt(d_scr[g], values)
                e_scr[g] += lane_tiles(weights * grad_prob, jnp.add)
                s_scr[g, c - lo] = weights
                p_scr[g, c - lo] = grad_prob

        for g in range(pairs):
            total = jnp.sum(l_scr[g], axis=1, keepdims=True)
            share = 1.0 / total
            delta = jnp.sum(e_scr[g], axis=1, keepdims=True) * share
            att_out[pl.ds(out0, BLK), lanes(g)] = one_of_two(o_scr[g] * share, lane).astype(LOW)
            log_sum = m_scr[g] + jnp.log(total)
            stat_out[j, 2 * g : 2 * g + 1, :] = log_sum[:BLK].T[0:1]
            stat_out[j, 2 * g + 1 : 2 * g + 2, :] = log_sum[BLK:].T[0:1]
            wide = jnp.broadcast_to(delta, (2 * BLK, BLK))
            base = stat_out.shape[1] // 2 + 2 * g
            stat_out[j, base : base + 1, :] = wide[:BLK].T[0:1]
            stat_out[j, base + 1 : base + 2, :] = wide[BLK:].T[0:1]
            l_scr[g] = jnp.broadcast_to(share, (2 * BLK, BLK))
            e_scr[g] = wide
        o_scr[...] = jnp.zeros(o_scr.shape, WIDE)

        @pl.loop(lo, hi)
        def _(c):
            for g in range(pairs):
                wide = jnp.concatenate([e_scr[g]] * (CHUNK // BLK), 1)
                grad_score = s_scr[g, c - lo] * (p_scr[g, c - lo] - wide)
                o_scr[g] += dot_nn(
                    grad_score.astype(LOW), gathered_blocks(k_ref, inverse, c, lanes(g))
                )

        cosine = cos_ref[pl.ds(out0, BLK), :]
        sine = sin_ref[pl.ds(out0, BLK), :]
        for g in range(pairs):
            grad = one_of_two(o_scr[g] * l_scr[g], lane) * SCALE
            dq_out[pl.ds(out0, BLK), lanes(g)] = turned(grad, cosine, -sine, lane).astype(LOW)


def smem():
    return pl.BlockSpec(memory_space=pltpu.SMEM)


def vmem():
    return pl.BlockSpec(memory_space=pltpu.VMEM)


def query_side(blocks, first, last, inverse, queries, keys, values, grads, cosine, sine, starts):
    own = blocks.shape[0]
    width = queries.shape[1]
    pairs = width // BLK
    stat_rows = 16 * ((2 * pairs + 7) // 8)
    work = 2 * BLK * CHUNK
    return pl.pallas_call(
        query_kernel,
        in_specs=[smem()] * 4 + [vmem()] * 7,
        out_specs=[vmem()] * 3,
        out_shape=[
            jax.ShapeDtypeStruct((own * BLK, width), LOW),
            jax.ShapeDtypeStruct((own * BLK, width), LOW),
            jax.ShapeDtypeStruct((own, stat_rows, BLK), WIDE),
        ],
        scratch_shapes=[
            pltpu.VMEM((pairs, SPAN, 2 * BLK, CHUNK), WIDE),
            pltpu.VMEM((pairs, SPAN, 2 * BLK, CHUNK), WIDE),
            pltpu.VMEM((pairs, 2 * BLK, BLK), LOW),
            pltpu.VMEM((pairs, 2 * BLK, BLK), LOW),
            pltpu.VMEM((pairs, 2 * BLK, BLK), WIDE),
            pltpu.VMEM((pairs, 2 * BLK, BLK), WIDE),
            pltpu.VMEM((pairs, 2 * BLK, BLK), WIDE),
            pltpu.VMEM((pairs, 2 * BLK, BLK), WIDE),
        ],
        compiler_params=pltpu.CompilerParams(vmem_limit_bytes=VMEM_ASK),
        cost_estimate=pl.CostEstimate(
            flops=own * pairs * 12 * 4 * 2 * work * BLK,
            bytes_accessed=4 * keys.shape[0] * width * 2,
            transcendentals=own * pairs * 4 * work,
        ),
        name="query_side",
    )(blocks, first, last, inverse, queries, keys, values, grads, cosine, sine, starts)


def key_kernel(
    blocks,
    first,
    last,
    inverse,
    q_ref,
    k_ref,
    v_ref,
    d_ref,
    cos_ref,
    sin_ref,
    end_ref,
    stat_ref,
    dk_out,
    dv_out,
    k_scr,
    v_scr,
    dk_scr,
    dv_scr,
):
    pairs = q_ref.shape[1] // BLK
    own = dk_out.shape[0] // BLK
    half_stat = stat_ref.shape[1] // 2
    lane = lax.broadcasted_iota(jnp.int32, (BLK, BLK), 1)

    def lanes(pair):
        return slice(pair * BLK, (pair + 1) * BLK)

    @pl.loop(0, own)
    def _(j):
        row0 = pl.multiple_of(blocks[j] * BLK, BLK)
        out0 = pl.multiple_of(j * BLK, BLK)
        for g in range(pairs):
            k_scr[g] = two_heads(k_ref[pl.ds(out0, BLK), lanes(g)].astype(WIDE), lane).astype(
                LOW
            ) * LOW(SCALE)
            v_scr[g] = two_heads(v_ref[pl.ds(out0, BLK), lanes(g)].astype(WIDE), lane).astype(LOW)
        dk_scr[...] = jnp.zeros(dk_scr.shape, WIDE)
        dv_scr[...] = jnp.zeros(dv_scr.shape, WIDE)
        ends = end_ref[pl.ds(out0, BLK), :]
        places = row0 + lax.broadcasted_iota(jnp.int32, (BLK, 1), 0)

        @pl.loop(first[j], last[j])
        def _(c):
            query0 = pl.multiple_of(c * CHUNK, CHUNK)
            query_place = query0 + lax.broadcasted_iota(jnp.int32, (BLK, CHUNK), 1)
            allowed = (query_place >= places) & (query_place < ends)
            count = CHUNK // BLK
            slots = [inverse[c * count + i] for i in range(count)]

            def stat(row):
                return jnp.concatenate([stat_ref[slot, row : row + 1, :] for slot in slots], 1)

            for g in range(pairs):
                queries = gathered_blocks(q_ref, inverse, c, lanes(g))
                grads = gathered_blocks(d_ref, inverse, c, lanes(g))
                scores = dot_nt(k_scr[g], queries)
                grad_prob = dot_nt(v_scr[g], grads)
                probs, grad_scores = [], []
                for h in range(2):
                    rows = slice(h * BLK, (h + 1) * BLK)
                    shifted = jnp.where(allowed, scores[rows] - stat(2 * g + h), NEG_BIG)
                    prob = jnp.exp(shifted)
                    probs.append(prob.astype(LOW))
                    grad_scores.append(
                        (prob * (grad_prob[rows] - stat(half_stat + 2 * g + h))).astype(LOW)
                    )
                dv_scr[g] += dot_nn(jnp.concatenate(probs, 0), grads)
                dk_scr[g] += dot_nn(jnp.concatenate(grad_scores, 0), queries)

        cosine = cos_ref[pl.ds(out0, BLK), :]
        sine = sin_ref[pl.ds(out0, BLK), :]
        for g in range(pairs):
            grad = one_of_two(dk_scr[g], lane) * SCALE
            dk_out[pl.ds(out0, BLK), lanes(g)] = turned(grad, cosine, -sine, lane).astype(LOW)
            dv_out[pl.ds(out0, BLK), lanes(g)] = one_of_two(dv_scr[g], lane).astype(LOW)


def key_side(
    blocks, first, last, inverse, queries, keys, values, grads, cosine, sine, ends, stats
):
    own = blocks.shape[0]
    width = queries.shape[1]
    pairs = width // BLK
    work = 2 * BLK * CHUNK
    return pl.pallas_call(
        key_kernel,
        in_specs=[smem()] * 4 + [vmem()] * 8,
        out_specs=[vmem()] * 2,
        out_shape=[jax.ShapeDtypeStruct((own * BLK, width), LOW)] * 2,
        scratch_shapes=[
            pltpu.VMEM((pairs, 2 * BLK, BLK), LOW),
            pltpu.VMEM((pairs, 2 * BLK, BLK), LOW),
            pltpu.VMEM((pairs, 2 * BLK, BLK), WIDE),
            pltpu.VMEM((pairs, 2 * BLK, BLK), WIDE),
        ],
        compiler_params=pltpu.CompilerParams(vmem_limit_bytes=VMEM_ASK),
        cost_estimate=pl.CostEstimate(
            flops=own * pairs * 12 * 4 * 2 * work * BLK,
            bytes_accessed=4 * keys.shape[0] * width * 2,
            transcendentals=own * pairs * 4 * work,
        ),
        name="key_side",
    )(blocks, first, last, inverse, queries, keys, values, grads, cosine, sine, ends, stats)


TILE = 256


def symmetric_product(out_ref, left, right, depth):
    size = out_ref.shape[0]
    for i in range(0, size, TILE):
        out_ref[i : i + TILE, i:] = dot_nt(left[i : i + TILE, :depth], right[i:, :depth])
    for i in range(0, size, TILE):
        for j in range(i + TILE, size, TILE):
            out_ref[j : j + TILE, i : i + TILE] = out_ref[i : i + TILE, j : j + TILE].T


def ns_matrix(span, near, far, out_ref, wide_scr, low_scr, gram_scr, poly_scr):
    half = span // 2
    step = 768
    cuts = [slice(i, i + step) for i in range(0, span, step)]
    total = jnp.zeros((1, 1), WIDE)
    for source, base in ((near, 0), (far, half)):
        for i in range(0, half, 384):
            part = source[:, i : i + 384].astype(WIDE)
            wide_scr[:, base + i : base + i + 384] = part
            total = total + jnp.sum(part * part)
    factor = 1.0 / (jnp.sqrt(total) + 1e-7)
    for cut in cuts:
        part = wide_scr[:, cut] * factor
        wide_scr[:, cut] = part
        low_scr[:, cut] = part.astype(LOW)

    def polynomial():
        symmetric_product(gram_scr, low_scr, low_scr, span)
        poly_scr[...] = gram_scr[...].astype(LOW)
        first = gram_scr[...] * NS_COEF[1]
        symmetric_product(gram_scr, poly_scr, poly_scr, poly_scr.shape[1])
        poly_scr[...] = (first + NS_COEF[2] * gram_scr[...]).astype(LOW)

    @pl.loop(0, NS_STEPS - 1)
    def _(_):
        polynomial()
        for cut in cuts:
            part = NS_COEF[0] * wide_scr[:, cut] + dot_nn(poly_scr[...], low_scr[:, cut])
            wide_scr[:, cut] = part
            low_scr[:, cut] = part.astype(LOW)

    polynomial()
    rows = out_ref.shape[0]
    for i in range(0, half, 384):
        cut = slice(i, i + 384)
        out_ref[:, cut] = (
            NS_COEF[0] * wide_scr[:rows, cut] + dot_nn(poly_scr[:rows, :], low_scr[:, cut])
        ).astype(LOW)


def ns_kernel(spans, high, near_a, far_a, near_b, far_b, out_ref, *scratch):
    out_ref[...] = jnp.zeros(out_ref.shape, LOW)
    widest = max(spans)
    for span in sorted(set(spans)):
        wanted = jnp.bool_(False)
        for owner, own_span in enumerate(spans):
            if own_span == span:
                wanted = wanted | (high[0] == owner)

        @pl.when(wanted)
        def _():
            near, far = (near_a, far_a) if span == widest else (near_b, far_b)
            ns_matrix(span, near, far, out_ref, *scratch)


def orthogonal_rows(spans, high, wide_pair, short_pair, rows):
    size, half = wide_pair[0].shape
    kept = rows if rows % 16 == 0 else size
    out = pl.pallas_call(
        partial(ns_kernel, spans),
        in_specs=[smem()] + [vmem()] * 4,
        out_specs=vmem(),
        out_shape=jax.ShapeDtypeStruct((kept, half), LOW),
        scratch_shapes=[
            pltpu.VMEM((size, 2 * half), WIDE),
            pltpu.VMEM((size, 2 * half), LOW),
            pltpu.VMEM((size, size), WIDE),
            pltpu.VMEM((size, size), LOW),
        ],
        compiler_params=pltpu.CompilerParams(vmem_limit_bytes=VMEM_ASK),
        cost_estimate=pl.CostEstimate(
            flops=NS_STEPS * 10 * size * size * half,
            bytes_accessed=8 * size * half,
            transcendentals=0,
        ),
        name="orthogonal_rows",
    )(high, *wide_pair, *short_pair)
    return out[:rows]


def rotary_tables(places):
    half = ROT // 2
    exponent = jnp.arange(0, ROT, 2, dtype=WIDE) / ROT
    frequency = 1.0 / 10000.0**exponent
    angles = frequency[:, None] * places.astype(WIDE)[None, :]
    lane = jnp.arange(BLK) % HD
    picked = ((lane % half)[None, :] == jnp.arange(half)[:, None]) & (lane < ROT)[None, :]
    sign = jnp.where(lane < half, -1.0, 1.0)[None, :]
    spread = partial(
        jnp.einsum, "fn,fl->nl", precision=lax.Precision.HIGHEST, preferred_element_type=WIDE
    )
    cosine = spread(jnp.cos(angles), picked.astype(WIDE)) + (lane >= ROT)[None, :].astype(WIDE)
    return cosine, spread(jnp.sin(angles), picked * sign)


def body(
    tokens,
    cotangent,
    w_qkv,
    w_attn,
    w_up,
    w_down,
    norm_vectors,
    qkv_bias,
    up_bias,
    qkv_moment,
    attn_moment,
    up_moment,
    down_moment,
    norm_moment,
    qbias_moment,
    ubias_moment,
    seq_lengths,
    block_source,
):
    row_count, half = tokens.shape
    fsdp_count = lax.axis_size("fsdp")
    ctx_count = lax.axis_size("ctx")
    tp_index = lax.axis_index("tp")
    fsdp_index = lax.axis_index("fsdp")
    ctx_index = lax.axis_index("ctx")
    low_count = ctx_count // OWNERS
    ctx_low = ctx_index % low_count
    ctx_high = ctx_index // low_count
    width = 2 * half
    own_blocks = row_count // BLK
    pack = ctx_count * row_count
    first_tp = tp_index == 0
    block_row = block_source[0]
    length_row = seq_lengths[0]

    def both_halves(mine, other, dim):
        return jnp.concatenate(
            [jnp.where(first_tp, mine, other), jnp.where(first_tp, other, mine)], axis=dim
        )

    def own_half(array):
        return jnp.where(first_tp, array[:, :half], array[:, half:])

    def far_half(array):
        return jnp.where(first_tp, array[:, half:], array[:, :half])

    own_pair = jnp.concatenate([tokens, cotangent], axis=1)
    far_pair = partner(own_pair, "tp", 1)
    inputs_low = both_halves(tokens, far_pair[:, :half], 1)
    full_cotangent = both_halves(cotangent, far_pair[:, half:], 1)

    near = [own_pair] + [partner(own_pair, "ctx", s * low_count) for s in range(1, OWNERS)]
    near_parts = [jnp.concatenate(near, axis=0)]
    for s in range(1, low_count):
        near_parts.append(jnp.concatenate([partner(part, "ctx", s) for part in near], axis=0))
    far_parts = [partner(part, "tp", 1) for part in near_parts]

    joint_full = gather_axis(
        jnp.concatenate(
            [w_qkv.astype(LOW).reshape(w_qkv.shape[0], 3 * half), w_attn.astype(LOW).T], axis=1
        ),
        "fsdp",
        0,
    )
    up_down = lax.all_gather(
        jnp.concatenate([w_up.astype(LOW), w_down.astype(LOW).T], axis=1),
        "fsdp",
        axis=0,
        tiled=True,
    )

    def group_place(ctx):
        differs = ctx ^ ctx_index
        return (differs % low_count) * OWNERS + differs // low_count

    slot_blocks = jnp.arange(block_row.shape[0], dtype=jnp.int32)
    slot_places = group_place(slot_blocks // own_blocks) * own_blocks + slot_blocks % own_blocks
    inverse = jnp.sum(
        jnp.where(block_row[None, :] == slot_blocks[:, None], slot_places[None, :], 0), axis=1
    ).astype(jnp.int32)
    my_blocks = lax.dynamic_slice_in_dim(block_row, ctx_index * own_blocks, own_blocks)

    seq_ends = jnp.cumsum(length_row).astype(jnp.int32)
    seq_starts = seq_ends - length_row

    def bounds(packed):
        inside = (packed[:, None] >= seq_starts[None, :]) & (packed[:, None] < seq_ends[None, :])
        return (
            jnp.sum(jnp.where(inside, seq_starts[None, :], 0), axis=1).astype(jnp.int32),
            jnp.sum(jnp.where(inside, seq_ends[None, :], 0), axis=1).astype(jnp.int32),
        )

    group_blocks = jnp.sum(
        jnp.where(slot_places[None, :] == slot_blocks[:, None], block_row[None, :], 0), axis=1
    )
    offsets = jnp.arange(BLK, dtype=jnp.int32)
    packed = (group_blocks[:, None] * BLK + offsets[None, :]).reshape(-1)
    cosine, sine = rotary_tables(packed - bounds(packed)[0])
    my_starts, my_ends = bounds(
        (my_blocks[:, None] * BLK + offsets[None, :]).reshape(-1)
    )
    key_first = bounds(my_blocks * BLK)[0] // CHUNK
    key_last = (my_blocks * BLK + BLK - 1) // CHUNK + 1
    query_first = my_blocks * BLK // CHUNK
    query_last = (bounds(my_blocks * BLK + BLK - 1)[1] + CHUNK - 1) // CHUNK

    def own_first(array, dim):
        left, right = jnp.split(array, 2, axis=dim)
        return jnp.where(first_tp, left, right), jnp.where(first_tp, right, left)

    projections = (
        *own_first(joint_full, 0),
        qkv_bias.reshape(1, 3 * half),
        *own_first(norm_vectors, 1),
    )
    made = ()
    for part, (near_part, far_part) in enumerate(zip(near_parts, far_parts)):
        made = project_rows(
            part, pack, near_part, far_part, projections, cosine, sine, made
        )
    queries, keys, values, d_attended = made

    inputs = inputs_low.astype(WIDE)
    centered = inputs - jnp.mean(inputs, axis=1, keepdims=True)
    inv_std = lax.rsqrt(jnp.mean(centered * centered, axis=1, keepdims=True) + 1e-05)
    normed = centered * inv_std
    norm_out = (normed * norm_vectors[0] + norm_vectors[1]).astype(LOW)
    hidden_here = up_bias.shape[0]
    feed_out, feed_dx, grad_up, grad_down, grad_ubias = feed_forward(
        norm_out, full_cotangent, up_down, up_bias.reshape(1, hidden_here)
    )

    def outer(left, right):
        return jnp.einsum("na,nb->ab", left, right, preferred_element_type=WIDE).astype(LOW)

    def reduced_first(gradient):
        rows = gradient.shape[0] // fsdp_count
        return sum_scatter(
            gradient.reshape(fsdp_count, rows, gradient.shape[1]), "fsdp", 1, fsdp_index
        )

    def reduced_rest(part):
        piece = part.shape[0] // ctx_count
        part = part.reshape(OWNERS, low_count, piece, part.shape[1])
        part = sum_scatter(jnp.swapaxes(part, 0, 1), "ctx", 1, ctx_low)
        return sum_scatter(part, "ctx", low_count, ctx_high)

    sum_up = reduced_rest(reduced_first(grad_up))
    sum_down = reduced_rest(reduced_first(grad_down))
    piece = sum_up.shape[0]
    grad_outbias = jnp.sum(cotangent.astype(WIDE), axis=0)

    def all_rows(*sums):
        joined = jnp.concatenate(sums, axis=1).astype(LOW)
        return lax.all_gather(joined, "ctx", axis=0, tiled=True).astype(WIDE)

    all_up, all_down = jnp.split(all_rows(sum_up, sum_down), 2, axis=1)
    fresh_up = 0.95 * up_moment + all_up
    fresh_down = 0.95 * down_moment + all_down.T

    def my_rows(array, dim):
        return lax.dynamic_slice_in_dim(array, ctx_index * piece, piece, dim)

    def as_rows(up, attn, qkv, down):
        return (
            my_rows(up, 0),
            my_rows(attn, 1).T,
            my_rows(qkv, 0).reshape(piece, 3 * half),
            my_rows(down, 1).T,
        )

    spans = (2 * hidden_here, 2 * half, 6 * half, 2 * hidden_here)
    old_moments = as_rows(up_moment, attn_moment, qkv_moment, down_moment)

    def to_owners(pieces):
        owners = tuple(pieces)
        low, high = pieces[owners[0]].astype(LOW), pieces[owners[1]].astype(LOW)

        def wanted(index):
            return index // low_count in owners

        rows = [jnp.where(ctx_high == owners[0], low, high)]
        for s in range(1, OWNERS):
            sent = jnp.where(ctx_high ^ s == owners[0], low, high)
            rows.append(partner_among(sent, ("ctx",), (s * low_count,), lambda i: wanted(i[0])))
        parts = [jnp.concatenate(rows, axis=0)]
        for s in range(1, low_count):
            parts.append(partner_among(parts[0], ("ctx",), (s,), lambda i: wanted(i[0])))
        for s in range(1, fsdp_count):
            parts += [
                partner_among(part, ("fsdp", "ctx"), (s, 0), lambda i: wanted(i[1]))
                for part in parts[:low_count]
            ]
        others = [
            partner_among(part, ("ctx", "tp"), (0, 1), lambda i: wanted(i[0])) for part in parts
        ]
        return jnp.concatenate(parts, axis=0), jnp.concatenate(others, axis=0)

    wide_pair = to_owners(
        {0: 0.95 * old_moments[0] + sum_up, 3: 0.95 * old_moments[3] + sum_down}
    )

    attended, grad_q, stats = query_side(
        my_blocks,
        key_first,
        key_last,
        inverse,
        queries,
        keys,
        values,
        d_attended,
        cosine,
        sine,
        my_starts[:, None],
    )
    sum_early = reduced_rest(
        reduced_first(
            jnp.concatenate([outer(norm_out, grad_q), outer(full_cotangent, attended)], axis=1)
        )
    )
    near_stats = [stats] + [partner(stats, "ctx", s * low_count) for s in range(1, OWNERS)]
    all_stats = list(near_stats)
    for s in range(1, low_count):
        all_stats += [partner(part, "ctx", s) for part in near_stats]
    grad_k, grad_v = key_side(
        my_blocks,
        query_first,
        query_last,
        inverse,
        queries,
        keys,
        values,
        d_attended,
        cosine,
        sine,
        my_ends[:, None],
        jnp.concatenate(all_stats, axis=0),
    )
    grad_late = outer(norm_out, jnp.concatenate([grad_k, grad_v], axis=1))
    late_rows = reduced_first(grad_late)
    sum_late = reduced_rest(late_rows)
    grad_q, grad_k, grad_v, grad_late = lax.optimization_barrier(
        (grad_q, grad_k, grad_v, grad_late)
    )
    grad_proj = jnp.concatenate([grad_q, grad_k, grad_v], axis=1)
    grad_qbias = jnp.sum(grad_proj.astype(WIDE), axis=0)

    partial_out = dot_nt(attended, joint_full[:, 3 * half :]) + feed_out

    def sum_halves(array):
        return own_half(array) + partner(far_half(array).astype(LOW), "tp", 1).astype(WIDE)

    out_bias = own_half((norm_vectors[2] + norm_vectors[3])[None, :])
    mixed = (tokens.astype(WIDE) + sum_halves(partial_out) + out_bias).astype(LOW)

    grad_norm = sum_halves(dot_nt(grad_proj, joint_full[:, : 3 * half]) + feed_dx)
    my_normed = own_half(normed)
    scaled = grad_norm * own_half(norm_vectors[0:1])
    row_sums = jnp.stack([jnp.sum(scaled, axis=1), jnp.sum(scaled * my_normed, axis=1)])
    row_means = (row_sums + partner(row_sums, "tp", 1)) / width
    grad_tokens = cotangent.astype(WIDE) + inv_std * (
        scaled - row_means[0][:, None] - my_normed * row_means[1][:, None]
    )

    vector_parts = jnp.stack(
        [jnp.sum(grad_norm * my_normed, axis=0), jnp.sum(grad_norm, axis=0), grad_outbias]
    )
    small = jnp.concatenate([vector_parts.reshape(-1), grad_qbias, grad_ubias[0]])
    small = sum_everywhere(small, ("ctx",))
    small = sum_everywhere(lax.optimization_barrier((small, late_rows))[0], ("fsdp",))
    mine = small[: 3 * half].reshape(3, half)
    vectors = both_halves(mine, partner(mine, "tp", 1), 1)
    sum_vectors = jnp.concatenate([vectors, vectors[2:3]], axis=0)
    sum_qbias = small[3 * half : 6 * half].reshape(3, half)
    sum_ubias = small[6 * half :]

    sum_qkv = jnp.concatenate([sum_early[:, :half], sum_late], axis=1)
    sum_attn = sum_early[:, half:]
    gathered = all_rows(sum_qkv, sum_attn)
    fresh_qkv = 0.95 * qkv_moment + gathered[:, : 3 * half].reshape(qkv_moment.shape)
    fresh_attn = 0.95 * attn_moment + gathered[:, 3 * half :].T
    own_attn = jnp.pad(0.95 * old_moments[1] + sum_attn, ((0, 0), (0, 2 * half)))
    short_pair = to_owners({1: own_attn, 2: 0.95 * old_moments[2] + sum_qkv})
    rows_out = orthogonal_rows(
        spans, ctx_high.reshape(1), wide_pair, short_pair, OWNERS * piece
    ).reshape(OWNERS, piece, hidden_here)
    returned = jnp.stack(
        [rows_out[0]]
        + [partner(rows_out[s], "ctx", s * low_count) for s in range(1, OWNERS)]
    )
    orthogonal = [
        lax.dynamic_index_in_dim(returned, ctx_high ^ m, 0, keepdims=False).astype(WIDE)
        for m in range(OWNERS)
    ]
    full_hidden = hidden_here * 2
    olds = as_rows(w_up, w_attn, w_qkv, w_down)
    rates = (
        0.5 * math.sqrt(full_hidden / width),
        0.5 * math.sqrt(width / (width // HD)),
        0.5 * math.sqrt(3 * width / width),
        0.5 * math.sqrt(full_hidden / full_hidden),
    )
    new_up, new_attn, new_qkv, new_down = (
        old - rate * made[:, : old.shape[1]] for old, rate, made in zip(olds, rates, orthogonal)
    )

    vector_rate = 0.3 / math.sqrt(row_count * fsdp_count * ctx_count)
    mom_norm = 0.9 * norm_moment + sum_vectors
    mom_qbias = 0.9 * qbias_moment + sum_qbias
    mom_ubias = 0.9 * ubias_moment + sum_ubias
    return (
        mixed,
        grad_tokens,
        fresh_qkv,
        new_qkv.reshape(piece, 3, half),
        fresh_attn,
        new_attn.T,
        fresh_up,
        new_up,
        fresh_down,
        new_down.T,
        mom_norm,
        norm_vectors - vector_rate * mom_norm,
        mom_qbias,
        qkv_bias - vector_rate * mom_qbias,
        mom_ubias,
        up_bias - vector_rate * mom_ubias,
    )


def solution(mesh):
    return jax.shard_map(
        body,
        mesh=mesh,
        in_specs=(
            P(("fsdp", "ctx"), "tp"),
            P(("fsdp", "ctx"), "tp"),
            P("fsdp", None, "tp"),
            P("tp", "fsdp"),
            P("fsdp", "tp"),
            P("tp", "fsdp"),
            P(),
            P(None, "tp"),
            P("tp"),
            P("fsdp", None, "tp"),
            P("tp", "fsdp"),
            P("fsdp", "tp"),
            P("tp", "fsdp"),
            P(),
            P(None, "tp"),
            P("tp"),
            P("fsdp", None),
            P("fsdp", None),
        ),
        out_specs=(
            P(("fsdp", "ctx"), "tp"),
            P(("fsdp", "ctx"), "tp"),
            P("fsdp", None, "tp"),
            P(("fsdp", "ctx"), None, "tp"),
            P("tp", "fsdp"),
            P("tp", ("fsdp", "ctx")),
            P("fsdp", "tp"),
            P(("fsdp", "ctx"), "tp"),
            P("tp", "fsdp"),
            P("tp", ("fsdp", "ctx")),
            P(),
            P(),
            P(None, "tp"),
            P(None, "tp"),
            P("tp"),
            P("tp"),
        ),
        check_vma=False,
    )
```

time: 545 us -> 618 us (1.13)
  starting transfers between devices: 80.4 us -> 139 us
  local copies, waits for them, and re-layouts: 59.5 us -> 111 us
  waiting for transfers between devices: 165 us -> 121 us
  matrix products: 49.1 us -> 18.7 us
  Pallas kernels: 103 us -> 125 us
  other arithmetic: 65 us -> 75.4 us
    ppermute x67 -> x49, waiting for transfers between devices: 165 us -> 101 us  [partner(): return lax.ppermute(value, axis, [(i, i ^ step) for i in range(size)])]
    ppermute x0 -> x20, starting transfers between devices: none -> 35.5 us  [partner_among(): return lax.ppermute(value, tuple(axes), pairs)]
    dot_general x7 -> x3, matrix products: 32.5 us -> 5.78 us  [outer(): jnp.einsum('na,nb->ab', left, right, preferred_element_type=WIDE)]
    pallas_call x3 -> x5, Pallas kernels: 86.1 us -> 110 us  [the longest x1 48 us: orthogonal_rows(): pl.pallas_call(partial(ns_kernel, spans), in_specs=[smem()] + [vmem()] *...]
    ppermute x67 -> x49, starting transfers between devices: 80.3 us -> 103 us  [partner(): return lax.ppermute(value, axis, [(i, i ^ step) for i in range(size)])]
    unnamed x158 -> x160, local copies, waits for them, and re-layouts: 35.5 us -> 55.8 us
    ppermute x0 -> x20, waiting for transfers between devices: none -> 19.8 us  [partner_among(): return lax.ppermute(value, tuple(axes), pairs)]
    concatenate x3 -> x6, local copies, waits for them, and re-layouts: 0.98 us -> 14.9 us  [the longest x2 5.64 us: body(): jnp.concatenate([partner(part, 'ctx', s) for part in near], axis=0)]
  transfers between devices with their start and end apart: 68 -> 72, of which waited for: 27 -> 21; matrix products, arithmetic and copies ran while one was open for 28% -> 31% of each run, Pallas kernels for 19% -> 21%
where the time goes in v2:
time: 618 us; the launch traced here: 607 us
  starting transfers between devices  139 us (22%)
  Pallas kernels  125 us (20%)
  waiting for transfers between devices  121 us (20%)
  local copies, waits for them, and re-layouts  111 us (18%)
  other arithmetic  75.4 us (12%)
  matrix products  18.7 us (3%)
  between operations  16.8 us (3%)
    ppermute x49, starting transfers between devices, partner(): return lax.ppermute(value, axis, [(i, i ^ step) for i in range(size)])  103 us
    ppermute x49, waiting for transfers between devices, partner(): return lax.ppermute(value, axis, [(i, i ^ step) for i in range(size)])  101 us
    unnamed x160, local copies, waits for them, and re-layouts  55.8 us
    pallas_call x1, Pallas kernels, orthogonal_rows(): pl.pallas_call(partial(ns_kernel, spans), in_specs=[smem()] + [vmem()] *...  48 us
    ppermute x20, starting transfers between devices, partner_among(): return lax.ppermute(value, tuple(axes), pairs)  35.5 us
    pallas_call x2, Pallas kernels, project_rows(): pl.pallas_call(project_kernel, grid=(rows // CHUNK,), in_specs=[here] * 2...  26.6 us
    pallas_call x1, Pallas kernels, query_side(): pl.pallas_call(query_kernel, in_specs=[smem()] * 4 + [vmem()] * 7, out_sp...  21.5 us
    ppermute x20, waiting for transfers between devices, partner_among(): return lax.ppermute(value, tuple(axes), pairs)  19.8 us
  transfers between devices with their start and end apart: 72, of which 21 were waited for; matrix products, arithmetic and copies ran while one was open for 31% of the time, Pallas kernels for 21%

profile of v2, /device:TPU:0, one launch (start us, length us, event | category | flops | bytes accessed | tf_op | source)
XLA Modules:
  0.0 606.7 jit_solution(5006309901882367448)
XLA Ops:
  11.5 3.0 collective-permute-start.1
  14.5 2.6 collective-permute-start.3
  26.7 3.0 copy.120
  38.5 3.4 convolution_add_fusion.cos_ref
  42.0 3.0 copy.141
  53.3 5.1 fusion.35.sin_ref
  58.4 11.5 %collective-permute-done.3 = bf16[512,768]{0,1:T(8,128)(2,1)} collective-permute-done((bf16[512,768]{0,1:T(8,128)(2,1)}, bf16[512,768]{0,1:T(8,128)(2,1)}, u32[]{:S(2)}, u32[]{:S(2)}) %collective-permute-start.3) | collective-permute-done | bytes 786464 | tf_op jit(solution)/shard_map/ppermute | solution.py:38
  69.9 3.3 pad_maximum_fusion
  73.9 3.2 copy.123.near
  80.6 2.2 broadcast_select_fusion.5
  84.9 2.2 constant_dynamic-update-slice_fusion.3
  87.0 10.6 %collective-permute-done.2 = bf16[512,768]{0,1:T(8,128)(2,1)S(1)} collective-permute-done((bf16[512,768]{0,1:T(8,128)(2,1)}, bf16[512,768]{0,1:T(8,128)(2,1)S(1)}, u32[]{:S(2)}, u32[]{:S(2)}) %collective-permute-start.2) | collective-permute-done | bytes 786464 | tf_op jit(solution)/shard_map/ppermute | solution.py:38
  98.6 15.9 %collective-permute-done.4 = bf16[512,768]{0,1:T(8,128)(2,1)S(1)} collective-permute-done((bf16[512,768]{0,1:T(8,128)(2,1)}, bf16[512,768]{0,1:T(8,128)(2,1)S(1)}, u32[]{:S(2)}, u32[]{:S(2)}) %collective-permute-start.4) | collective-permute-done | bytes 786464 | tf_op jit(solution)/shard_map/ppermute | solution.py:38
  115.4 15.5 %collective-permute-done.6 = bf16[512,768]{0,1:T(8,128)(2,1)S(1)} collective-permute-done((bf16[512,768]{0,1:T(8,128)(2,1)}, bf16[512,768]{0,1:T(8,128)(2,1)S(1)}, u32[]{:S(2)}, u32[]{:S(2)}) %collective-permute-start.6) | collective-permute-done | bytes 786464 | tf_op jit(solution)/shard_map/ppermute | solution.py:38
  133.7 2.3 copy.133.x_ref
  136.0 2.4 fusion.76
  138.4 2.3 copy.134.g_ref
  140.7 3.3 broadcast_select_fusion.2
  146.6 4.6 copy.125.near
  151.2 4.7 copy.124.far
  155.9 13.2 %project_rows.2 = (bf16[4096,384]{1,0:T(8,128)(2,1)}, bf16[4096,384]{1,0:T(8,128)(2,1)}, bf16[4096,384]{1,0:T(8,128)(2,1)}, bf16[4096,384]{1,0:T(8,128)(2,1)}) custom-call(bf16[2048,768]{1,0:T(8,128)(2,1)} %copy.123.near, bf16[2048,768]{1,0:T(8,128)(2,1)} %copy.124.far, bf16[384,1536]{1,0:T(8,128)(2,1)} %broadcast_select_fusion.3.w_near, ...), custom_call_target="tpu_custom_call" | custom-call | flops 14495514624 | bytes 15728640 | tf_op jit(solution)/shard_map/project_rows/pallas_call | solution.py:151
  169.1 4.7 copy.126.far
  173.8 13.4 %project_rows.3 = (bf16[4096,384]{1,0:T(8,128)(2,1)}, bf16[4096,384]{1,0:T(8,128)(2,1)}, bf16[4096,384]{1,0:T(8,128)(2,1)}, bf16[4096,384]{1,0:T(8,128)(2,1)}) custom-call(bf16[2048,768]{1,0:T(8,128)(2,1)} %copy.125.near, bf16[2048,768]{1,0:T(8,128)(2,1)} %copy.126.far, ...), custom_call_target="tpu_custom_call", output_to_operand_aliasing={{0}: (9, {}), {1}: (10, {}), {2}: (11, {}), {3}: (12, {})} | custom-call | flops 14495514624 | bytes 15728640 | tf_op jit(solution)/shard_map/project_rows/pallas_call | solution.py:151
  187.3 21.5 %query_side.1 = (bf16[512,384]{1,0:T(8,128)(2,1)}, bf16[512,384]{1,0:T(8,128)(2,1)}, f32[4,16,128]{2,1,0:T(8,128)}) custom-call(s32[4]{0:T(128)} %copy-done.60, s32[4]{0:T(128)} %and_select_fusion.9.first, s32[4]{0:T(128)} %get-tuple-element.197.last, s32[32]{0:T(128)} %get-tuple-element.119.inverse, bf16[4096,384]{1,0:T(8,128)(2,1)} %get-tuple-element.42.q_ref, ...), custom_call_target="tpu_custom_call" | custom-call | flops 19327352832 | bytes 12582912 | tf_op jit(solution)/shard_map/query_side/pallas_call | solution.py:395
  208.8 21.5 %collective-permute-start.12 = (f32[4,16,128]{2,1,0:T(8,128)}, f32[4,16,128]{2,1,0:T(8,128)}, u32[]{:S(2)}, u32[]{:S(2)}) collective-permute-start(f32[4,16,128]{2,1,0:T(8,128)} %get-tuple-element.49), channel_id=1, source_target_pairs={{0,4},{2,6},{4,0},{6,2},{8,12},{10,14},{12,8},{14,10},{1,5},{3,7},... | collective-permute-start | bytes 98312 | tf_op jit(solution)/shard_map/ppermute | solution.py:38
  230.3 2.4 collective-permute-start.14
  232.8 13.8 %feed_forward.1 = (f32[512,768]{1,0:T(8,128)}, f32[512,768]{1,0:T(8,128)}, bf16[768,1536]{1,0:T(8,128)(2,1)}, bf16[768,1536]{1,0:T(8,128)(2,1)}, f32[1,1536]{1,0:T(1,128)}) custom-call(bf16[512,768]{1,0:T(8,128)(2,1)} %copy.133.x_ref, bf16[768,512]{1,0:T(8,128)(2,1)} %bitcast.219, bf16[512,768]{1,0:T(8,128)(2,1)} %copy.134.g_ref, ...), custom_call_target="tpu_custom_call" | custom-call | flops 12079595520 | bytes 14155776 | tf_op jit(solution)/shard_map/feed_forward/pallas_call | solution.py:217
  246.7 2.6 dynamic-slice_bitcast_fusion.1
  254.6 3.2 copy.136
  257.8 3.3 convolution_add_fusion.1
  261.7 3.1 copy.140
  276.5 14.7 %key_side.1 = (bf16[512,384]{1,0:T(8,128)(2,1)}, bf16[512,384]{1,0:T(8,128)(2,1)}) custom-call(s32[4]{0:T(128)} %copy-done.60, s32[4]{0:T(128)} %get-tuple-element.139.first, s32[4]{0:T(128)} %and_select_fusion.last, s32[32]{0:T(128)} %get-tuple-element.119.inverse, bf16[4096,384]{1,0:T(8,128)(2,1)} %get-tuple-element.42.q_ref, ...), custom_call_target="tpu_custom_call" | custom-call | flops 19327352832 | bytes 12582912 | tf_op jit(solution)/shard_map/key_side/pallas_call | solution.py:509
  291.2 3.1 convolution_convert_fusion
  299.3 2.6 copy.165
  308.8 5.9 collective-permute-start.64
  322.0 4.7 collective-permute-start.66
  328.8 2.3 copy.158
  333.5 10.4 %collective-permute-done.26 = bf16[384,768]{1,0:T(8,128)(2,1)} collective-permute-done((bf16[384,768]{1,0:T(8,128)(2,1)}, bf16[384,768]{1,0:T(8,128)(2,1)}, u32[]{:S(2)}, u32[]{:S(2)}) %collective-permute-start.26) | collective-permute-done | bytes 589856 | tf_op jit(solution)/shard_map/ppermute | solution.py:38
  345.8 3.0 collective-permute-done.67
  352.1 2.5 collective-permute-start.24
  362.1 2.2 collective-permute-start.30
  364.4 4.0 collective-permute-done.29
  369.9 4.0 collective-permute-start.51
  373.9 2.5 collective-permute-start.52
  391.6 11.0 %collective-permute-done.32 = bf16[4,48,1536]{2,1,0:T(8,128)(2,1)S(1)} collective-permute-done((bf16[4,48,1536]{2,1,0:T(8,128)(2,1)S(1)}, bf16[4,48,1536]{2,1,0:T(8,128)(2,1)S(1)}, u32[]{:S(2)}, u32[]{:S(2)}) %collective-permute-start.32) | collective-permute-done | bytes 589856 | tf_op jit(solution)/shard_map/ppermute | solution.py:38
  402.8 16.6 %collective-permute-start.33 = (bf16[48,1536]{1,0:T(8,128)(2,1)S(1)}, bf16[48,1536]{1,0:T(8,128)(2,1)S(1)}, u32[]{:S(2)}, u32[]{:S(2)}) collective-permute-start(bf16[48,1536]{1,0:T(8,128)(2,1)S(1)} %get-tuple-element.144), channel_id=1, source_target_pairs={{0,4},{2,6},{4,0},{6,2},{8,12},{10,14},{12,8},{14,10},{1,5},{3,7},... | collective-permute-start | bytes 442376 | tf_op jit(solution)/shard_map/ppermute | solution.py:38
  422.0 10.0 %collective-permute-start.38 = (bf16[48,1536]{1,0:T(8,128)(2,1)S(1)}, bf16[48,1536]{1,0:T(8,128)(2,1)S(1)}, u32[]{:S(2)}, u32[]{:S(2)}) collective-permute-start(bf16[48,1536]{1,0:T(8,128)(2,1)S(1)} %get-tuple-element.147), channel_id=1, source_target_pairs={{0,4},{2,6},{4,0},{6,2},{8,12},{10,14},{12,8},{14,10},{1,5},{3,7},... | collective-permute-start | bytes 442376 | tf_op jit(solution)/shard_map/ppermute | solution.py:38
  439.7 7.9 %collective-permute-done.39 = bf16[48,1536]{1,0:T(8,128)(2,1)S(1)} collective-permute-done((bf16[48,1536]{1,0:T(8,128)(2,1)S(1)}, bf16[48,1536]{1,0:T(8,128)(2,1)S(1)}, u32[]{:S(2)}, u32[]{:S(2)}) %collective-permute-start.39) | collective-permute-done | bytes 147488 | tf_op jit(solution)/shard_map/ppermute | solution.py:38
  453.8 3.5 collective-permute-start.43
  459.1 7.0 %collective-permute-done.41 = bf16[48,1536]{1,0:T(8,128)(2,1)S(1)} collective-permute-done((bf16[48,1536]{1,0:T(8,128)(2,1)}, bf16[48,1536]{1,0:T(8,128)(2,1)S(1)}, u32[]{:S(2)}, u32[]{:S(2)}) %collective-permute-start.41) | collective-permute-done | bytes 147488 | tf_op jit(solution)/shard_map/ppermute | solution.py:54
  471.0 2.5 collective-permute-start.45
  476.8 11.3 %collective-permute-done.44 = bf16[192,1536]{1,0:T(8,128)(2,1)} collective-permute-done((bf16[192,1536]{1,0:T(8,128)(2,1)}, bf16[192,1536]{1,0:T(8,128)(2,1)}, u32[]{:S(2)}, u32[]{:S(2)}) %collective-permute-start.44) | collective-permute-done | bytes 589856 | tf_op jit(solution)/shard_map/ppermute | solution.py:54
  490.0 2.5 pad_maximum_fusion.5.far_b
  494.5 2.4 collective-permute-start.49
  500.7 2.5 slice.194
  503.2 2.8 copy.146
  507.9 3.4 multiply_add_fusion
  511.3 2.8 copy.159
  517.7 3.2 pad_maximum_fusion.2.far_a
  520.8 48.0 %orthogonal_rows.1 = bf16[192,1536]{1,0:T(8,128)(2,1)} custom-call(s32[1]{0:T(128)} %bitcast.39.high, bf16[768,1536]{1,0:T(8,128)(2,1)} %constant_dynamic-update-slice_fusion.15.near_a, bf16[768,1536]{1,0:T(8,128)(2,1)} %pad_maximum_fusion.2.far_a, bf16[768,1152]{1,0:T(8,128)(2,1)} %constant_dynamic-update-slice_fusion.22.near_b, ...), custom_call_target="tpu_custom_call" | custom-call | flops 45298483200 | bytes 9437184 | tf_op jit(solution)/shard_map/orthogonal_rows/pallas_call | solution.py:600
  570.8 4.3 collective-permute-start.63
  576.0 2.2 copy.161
  578.5 6.4 %collective-permute-done.62 = bf16[48,1536]{1,0:T(8,128)(2,1)} collective-permute-done((bf16[48,1536]{1,0:T(8,128)(2,1)}, bf16[48,1536]{1,0:T(8,128)(2,1)}, u32[]{:S(2)}, u32[]{:S(2)}) %collective-permute-start.62) | collective-permute-done | bytes 147488 | tf_op jit(solution)/shard_map/ppermute | solution.py:38
  590.3 2.2 convert_element_type.371
  (394 shorter events, 168.9 us)
Async XLA Ops:
  8.0 224.8 %all-gather.4.cloned.1.call-start = ((), (), s32[]{:S(2)}) async-start(), calls=%async_computation | async-start | bytes 7077888 | tf_op jit(solution)/shard_map/all_gather | solution.py:702
  11.5 46.9 %collective-permute-start.1 = (bf16[512,768]{0,1:T(8,128)(2,1)}, bf16[512,768]{0,1:T(8,128)(2,1)}, u32[]{:S(2)}, u32[]{:S(2)}) collective-permute-start(bf16[512,768]{0,1:T(8,128)(2,1)} %pad_maximum_fusion.10), channel_id=1, source_target_pairs={{0,4},{2,6},{4,0},{6,2},{8,12},{10,14},{12,8},{14,10},{1,5},{3,7},... | collective-permute-start | bytes 2359304 | tf_op jit(solution)/shard_map/ppermute | solution.py:38
  14.5 55.4 %collective-permute-start.3 = (bf16[512,768]{0,1:T(8,128)(2,1)}, bf16[512,768]{0,1:T(8,128)(2,1)}, u32[]{:S(2)}, u32[]{:S(2)}) collective-permute-start(bf16[512,768]{0,1:T(8,128)(2,1)} %pad_maximum_fusion.10), channel_id=1, source_target_pairs={{0,8},{2,10},{4,12},{6,14},{8,0},{10,2},{12,4},{14,6},{1,9},{3,11}... | collective-permute-start | bytes 2359304 | tf_op jit(solution)/shard_map/ppermute | solution.py:38
  17.1 52.8 %collective-permute-start.5 = (bf16[512,768]{0,1:T(8,128)(2,1)}, bf16[512,768]{0,1:T(8,128)(2,1)}, u32[]{:S(2)}, u32[]{:S(2)}) collective-permute-start(bf16[512,768]{0,1:T(8,128)(2,1)} %pad_maximum_fusion.10), channel_id=1, source_target_pairs={{0,12},{2,14},{4,8},{6,10},{8,4},{10,6},{12,0},{14,2},{1,13},{3,15... | collective-permute-start | bytes 2359304 | tf_op jit(solution)/shard_map/ppermute | solution.py:38
  17.1 66.2 %collective-permute-start = (bf16[512,768]{0,1:T(8,128)(2,1)}, bf16[512,768]{0,1:T(8,128)(2,1)}, u32[]{:S(2)}, u32[]{:S(2)}) collective-permute-start(bf16[512,768]{0,1:T(8,128)(2,1)} %pad_maximum_fusion.10), channel_id=1, source_target_pairs={{0,2},{2,0},{4,6},{6,4},{8,10},{10,8},{12,14},{14,12},{1,3},{3,1},... | collective-permute-start | bytes 2359304 | tf_op jit(solution)/shard_map/ppermute | solution.py:38
  18.8 60.3 %collective-permute-start.10 = (bf16[512,768]{0,1:T(8,128)(2,1)}, bf16[512,768]{0,1:T(8,128)(2,1)}, u32[]{:S(2)}, u32[]{:S(2)}) collective-permute-start(bf16[512,768]{0,1:T(8,128)(2,1)} %pad_maximum_fusion.10), channel_id=1, source_target_pairs={{0,1},{1,0},{2,3},{3,2},{4,5},{5,4},{6,7},{7,6},{8,9},{9,8},{10,11... | collective-permute-start | bytes 2359304 | tf_op jit(solution)/shard_map/ppermute | solution.py:38
  25.3 475.4 %all-gather.6.cloned.1.call-start = ((), (), s32[]{:S(2)}) async-start(), calls=%async_computation.1 | async-start | bytes 1327104 | tf_op jit(solution)/shard_map/all_gather | solution.py:792
  73.2 78.1 %collective-permute-start.9 = (bf16[2048,768]{0,1:T(8,128)(2,1)S(1)}, bf16[2048,768]{0,1:T(8,128)(2,1)}, u32[]{:S(2)}, u32[]{:S(2)}) collective-permute-start(bf16[2048,768]{0,1:T(8,128)(2,1)S(1)} %pad_maximum_fusion), channel_id=1, source_target_pairs={{0,1},{1,0},{2,3},{3,2},{4,5},{5,4},{6,7},{7,6},{8,9},{9,8},{10,11... | collective-permute-start | bytes 9437192 | tf_op jit(solution)/shard_map/ppermute | solution.py:38
  77.0 20.6 %collective-permute-start.2 = (bf16[512,768]{0,1:T(8,128)(2,1)}, bf16[512,768]{0,1:T(8,128)(2,1)S(1)}, u32[]{:S(2)}, u32[]{:S(2)}) collective-permute-start(bf16[512,768]{0,1:T(8,128)(2,1)} %collective-permute-done.1), channel_id=1, source_target_pairs={{0,2},{2,0},{4,6},{6,4},{8,10},{10,8},{12,14},{14,12},{1,3},{3,1},... | collective-permute-start | bytes 2359304 | tf_op jit(solution)/shard_map/ppermute | solution.py:38
  78.6 35.9 %collective-permute-start.4 = (bf16[512,768]{0,1:T(8,128)(2,1)}, bf16[512,768]{0,1:T(8,128)(2,1)S(1)}, u32[]{:S(2)}, u32[]{:S(2)}) collective-permute-start(bf16[512,768]{0,1:T(8,128)(2,1)} %collective-permute-done.3), channel_id=1, source_target_pairs={{0,2},{2,0},{4,6},{6,4},{8,10},{10,8},{12,14},{14,12},{1,3},{3,1},... | collective-permute-start | bytes 2359304 | tf_op jit(solution)/shard_map/ppermute | solution.py:38
  79.1 51.8 %collective-permute-start.6 = (bf16[512,768]{0,1:T(8,128)(2,1)}, bf16[512,768]{0,1:T(8,128)(2,1)S(1)}, u32[]{:S(2)}, u32[]{:S(2)}) collective-permute-start(bf16[512,768]{0,1:T(8,128)(2,1)} %collective-permute-done.5), channel_id=1, source_target_pairs={{0,2},{2,0},{4,6},{6,4},{8,10},{10,8},{12,14},{14,12},{1,3},{3,1},... | collective-permute-start | bytes 2359304 | tf_op jit(solution)/shard_map/ppermute | solution.py:38
  83.3 57.4 %collective-permute-start.8 = (bf16[384,1536]{1,0:T(8,128)(2,1)}, bf16[384,1536]{1,0:T(8,128)(2,1)}, u32[]{:S(2)}, u32[]{:S(2)}) collective-permute-start(bf16[384,1536]{1,0:T(8,128)(2,1)} %pad_maximum_fusion.8), channel_id=1, source_target_pairs={{0,16},{16,0},{1,17},{17,1},{2,18},{18,2},{3,19},{19,3},{4,20},{20... | collective-permute-start | bytes 3538952 | tf_op jit(solution)/shard_map/ppermute | solution.py:38
  131.9 37.2 %collective-permute-start.7 = (bf16[2048,768]{0,1:T(8,128)(2,1)}, bf16[2048,768]{0,1:T(8,128)(2,1)}, u32[]{:S(2)}, u32[]{:S(2)}) collective-permute-start(bf16[2048,768]{0,1:T(8,128)(2,1)} %constant_dynamic-update-slice_fusion), channel_id=1, source_target_pairs={{0,1},{1,0},{2,3},{3,2},{4,5},{5,4},{6,7},{7,6},{8,9},{9,8},{10,11... | collective-permute-start | bytes 9437192 | tf_op jit(solution)/shard_map/ppermute | solution.py:38
  208.8 55.9 %collective-permute-start.12 = (f32[4,16,128]{2,1,0:T(8,128)}, f32[4,16,128]{2,1,0:T(8,128)}, u32[]{:S(2)}, u32[]{:S(2)}) collective-permute-start(f32[4,16,128]{2,1,0:T(8,128)} %get-tuple-element.49), channel_id=1, source_target_pairs={{0,4},{2,6},{4,0},{6,2},{8,12},{10,14},{12,8},{14,10},{1,5},{3,7},... | collective-permute-start | bytes 98312 | tf_op jit(solution)/shard_map/ppermute | solution.py:38
  230.3 36.3 %collective-permute-start.13 = (f32[4,16,128]{2,1,0:T(8,128)}, f32[4,16,128]{2,1,0:T(8,128)}, u32[]{:S(2)}, u32[]{:S(2)}) collective-permute-start(f32[4,16,128]{2,1,0:T(8,128)} %get-tuple-element.49), channel_id=1, source_target_pairs={{0,8},{2,10},{4,12},{6,14},{8,0},{10,2},{12,4},{14,6},{1,9},{3,11}... | collective-permute-start | bytes 98312 | tf_op jit(solution)/shard_map/ppermute | solution.py:38
  230.3 39.5 %collective-permute-start.14 = (f32[4,16,128]{2,1,0:T(8,128)}, f32[4,16,128]{2,1,0:T(8,128)}, u32[]{:S(2)}, u32[]{:S(2)}) collective-permute-start(f32[4,16,128]{2,1,0:T(8,128)} %get-tuple-element.49), channel_id=1, source_target_pairs={{0,12},{2,14},{4,8},{6,10},{8,4},{10,6},{12,0},{14,2},{1,13},{3,15... | collective-permute-start | bytes 98312 | tf_op jit(solution)/shard_map/ppermute | solution.py:38
  232.7 38.7 %collective-permute-start.15 = (f32[4,16,128]{2,1,0:T(8,128)}, f32[4,16,128]{2,1,0:T(8,128)}, u32[]{:S(2)}, u32[]{:S(2)}) collective-permute-start(f32[4,16,128]{2,1,0:T(8,128)} %get-tuple-element.49), channel_id=1, source_target_pairs={{0,2},{2,0},{4,6},{6,4},{8,10},{10,8},{12,14},{14,12},{1,3},{3,1},... | collective-permute-start | bytes 98312 | tf_op jit(solution)/shard_map/ppermute | solution.py:38
  249.2 134.8 %collective-permute-start.31 = (bf16[384,1536]{1,0:T(8,128)(2,1)}, bf16[384,1536]{1,0:T(8,128)(2,1)}, u32[]{:S(2)}, u32[]{:S(2)}) collective-permute-start(bf16[384,1536]{1,0:T(8,128)(2,1)} %dynamic-slice_bitcast_fusion.1), channel_id=1, source_target_pairs={{0,16},{16,0},{1,17},{17,1},{2,18},{18,2},{3,19},{19,3},{4,20},{20... | collective-permute-start | bytes 3538952 | tf_op jit(solution)/shard_map/ppermute | solution.py:38
  264.7 122.8 %collective-permute-start.36 = (bf16[384,1536]{1,0:T(8,128)(2,1)}, bf16[384,1536]{1,0:T(8,128)(2,1)}, u32[]{:S(2)}, u32[]{:S(2)}) collective-permute-start(bf16[384,1536]{1,0:T(8,128)(2,1)} %dynamic-slice_bitcast_fusion), channel_id=1, source_target_pairs={{0,16},{16,0},{1,17},{17,1},{2,18},{18,2},{3,19},{19,3},{4,20},{20... | collective-permute-start | bytes 3538952 | tf_op jit(solution)/shard_map/ppermute | solution.py:38
  266.6 8.0 %collective-permute-start.16 = (f32[4,16,128]{2,1,0:T(8,128)}, f32[4,16,128]{2,1,0:T(8,128)S(1)}, u32[]{:S(2)}, u32[]{:S(2)}) collective-permute-start(f32[4,16,128]{2,1,0:T(8,128)} %collective-permute-done.12), channel_id=1, source_target_pairs={{0,2},{2,0},{4,6},{6,4},{8,10},{10,8},{12,14},{14,12},{1,3},{3,1},... | collective-permute-start | bytes 98312 | tf_op jit(solution)/shard_map/ppermute | solution.py:38
  297.8 6.4 %collective-permute-start.19 = (bf16[512,384]{0,1:T(8,128)(2,1)}, bf16[512,384]{0,1:T(8,128)(2,1)}, u32[]{:S(2)}, u32[]{:S(2)}) collective-permute-start(bf16[512,384]{0,1:T(8,128)(2,1)} %select_convert_fusion), channel_id=1, source_target_pairs={{0,1},{1,0},{2,3},{3,2},{4,5},{5,4},{6,7},{7,6},{8,9},{9,8},{10,11... | collective-permute-start | bytes 1179656 | tf_op jit(solution)/shard_map/ppermute | solution.py:38
  302.8 19.3 %collective-permute-start.11 = (bf16[512,384]{0,1:T(8,128)(2,1)}, bf16[512,384]{0,1:T(8,128)(2,1)}, u32[]{:S(2)}, u32[]{:S(2)}) collective-permute-start(bf16[512,384]{0,1:T(8,128)(2,1)} %select_convert_fusion.1), channel_id=1, source_target_pairs={{0,1},{1,0},{2,3},{3,2},{4,5},{5,4},{6,7},{7,6},{8,9},{9,8},{10,11... | collective-permute-start | bytes 1179656 | tf_op jit(solution)/shard_map/ppermute | solution.py:38
  308.8 7.6 %collective-permute-start.64 = (f32[3840]{0:T(1024)S(1)}, f32[3840]{0:T(1024)S(1)}, u32[]{:S(2)}, u32[]{:S(2)}) collective-permute-start(f32[3840]{0:T(1024)S(1)} %pad_maximum_fusion.18), channel_id=1, source_target_pairs={{0,2},{2,0},{4,6},{6,4},{8,10},{10,8},{12,14},{14,12},{1,3},{3,1},... | collective-permute-start | bytes 46088 | tf_op jit(solution)/shard_map/ppermute | solution.py:38
  315.6 16.5 %collective-permute-start.21 = (bf16[384,768]{1,0:T(8,128)(2,1)}, bf16[384,768]{1,0:T(8,128)(2,1)}, u32[]{:S(2)}, u32[]{:S(2)}) collective-permute-start(bf16[384,768]{1,0:T(8,128)(2,1)} %dynamic-slice_bitcast_fusion.3), channel_id=1, source_target_pairs={{0,16},{16,0},{1,17},{17,1},{2,18},{18,2},{3,19},{19,3},{4,20},{20... | collective-permute-start | bytes 1769480 | tf_op jit(solution)/shard_map/ppermute | solution.py:38
  320.3 23.6 %collective-permute-start.26 = (bf16[384,768]{1,0:T(8,128)(2,1)}, bf16[384,768]{1,0:T(8,128)(2,1)}, u32[]{:S(2)}, u32[]{:S(2)}) collective-permute-start(bf16[384,768]{1,0:T(8,128)(2,1)} %dynamic-slice_bitcast_fusion.2), channel_id=1, source_target_pairs={{0,16},{16,0},{1,17},{17,1},{2,18},{18,2},{3,19},{19,3},{4,20},{20... | collective-permute-start | bytes 1769480 | tf_op jit(solution)/shard_map/ppermute | solution.py:38
  322.0 9.1 %collective-permute-start.66 = (f32[3840]{0:T(1024)}, f32[3840]{0:T(1024)}, u32[]{:S(2)}, u32[]{:S(2)}) collective-permute-start(f32[3840]{0:T(1024)} %add.464), channel_id=1, source_target_pairs={{0,8},{2,10},{4,12},{6,14},{8,0},{10,2},{12,4},{14,6},{1,9},{3,11}... | collective-permute-start | bytes 46088 | tf_op jit(solution)/shard_map/ppermute | solution.py:38
  333.4 17.4 %collective-permute-start.22 = (bf16[4,48,768]{2,1,0:T(8,128)(2,1)S(1)}, bf16[4,48,768]{2,1,0:T(8,128)(2,1)S(1)}, u32[]{:S(2)}, u32[]{:S(2)}) collective-permute-start(bf16[4,48,768]{2,1,0:T(8,128)(2,1)S(1)} %fusion.16), channel_id=1, source_target_pairs={{0,2},{2,0},{4,6},{6,4},{8,10},{10,8},{12,14},{14,12},{1,3},{3,1},... | collective-permute-start | bytes 884744 | tf_op jit(solution)/shard_map/ppermute | solution.py:38
  345.4 9.2 %collective-permute-start.27 = (bf16[4,48,768]{2,1,0:T(8,128)(2,1)S(1)}, bf16[4,48,768]{2,1,0:T(8,128)(2,1)S(1)}, u32[]{:S(2)}, u32[]{:S(2)}) collective-permute-start(bf16[4,48,768]{2,1,0:T(8,128)(2,1)S(1)} %fusion.17), channel_id=1, source_target_pairs={{0,2},{2,0},{4,6},{6,4},{8,10},{10,8},{12,14},{14,12},{1,3},{3,1},... | collective-permute-start | bytes 884744 | tf_op jit(solution)/shard_map/ppermute | solution.py:38
  352.0 6.3 %collective-permute-start.23 = (bf16[48,768]{1,0:T(8,128)(2,1)S(1)}, bf16[48,768]{1,0:T(8,128)(2,1)S(1)}, u32[]{:S(2)}, u32[]{:S(2)}) collective-permute-start(bf16[48,768]{1,0:T(8,128)(2,1)S(1)} %get-tuple-element.171), channel_id=1, source_target_pairs={{0,4},{2,6},{4,0},{6,2},{8,12},{10,14},{12,8},{14,10},{1,5},{3,7},... | collective-permute-start | bytes 221192 | tf_op jit(solution)/shard_map/ppermute | solution.py:38
  352.1 7.9 %collective-permute-start.24 = (bf16[48,768]{1,0:T(8,128)(2,1)S(1)}, bf16[48,768]{1,0:T(8,128)(2,1)S(1)}, u32[]{:S(2)}, u32[]{:S(2)}) collective-permute-start(bf16[48,768]{1,0:T(8,128)(2,1)S(1)} %get-tuple-element.173), channel_id=1, source_target_pairs={{0,8},{2,10},{4,12},{6,14},{8,0},{10,2},{12,4},{14,6},{1,9},{3,11}... | collective-permute-start | bytes 221192 | tf_op jit(solution)/shard_map/ppermute | solution.py:38
  355.3 6.8 %collective-permute-start.25 = (bf16[48,768]{1,0:T(8,128)(2,1)S(1)}, bf16[48,768]{1,0:T(8,128)(2,1)S(1)}, u32[]{:S(2)}, u32[]{:S(2)}) collective-permute-start(bf16[48,768]{1,0:T(8,128)(2,1)S(1)} %get-tuple-element.172), channel_id=1, source_target_pairs={{0,12},{2,14},{4,8},{6,10},{8,4},{10,6},{12,0},{14,2},{1,13},{3,15... | collective-permute-start | bytes 221192 | tf_op jit(solution)/shard_map/ppermute | solution.py:38
  358.3 6.1 %collective-permute-start.28 = (bf16[48,768]{1,0:T(8,128)(2,1)S(1)}, bf16[48,768]{1,0:T(8,128)(2,1)S(1)}, u32[]{:S(2)}, u32[]{:S(2)}) collective-permute-start(bf16[48,768]{1,0:T(8,128)(2,1)S(1)} %get-tuple-element.168), channel_id=1, source_target_pairs={{0,4},{2,6},{4,0},{6,2},{8,12},{10,14},{12,8},{14,10},{1,5},{3,7},... | collective-permute-start | bytes 221192 | tf_op jit(solution)/shard_map/ppermute | solution.py:38
  360.0 8.4 %collective-permute-start.29 = (bf16[48,768]{1,0:T(8,128)(2,1)S(1)}, bf16[48,768]{1,0:T(8,128)(2,1)S(1)}, u32[]{:S(2)}, u32[]{:S(2)}) collective-permute-start(bf16[48,768]{1,0:T(8,128)(2,1)S(1)} %get-tuple-element.170), channel_id=1, source_target_pairs={{0,8},{2,10},{4,12},{6,14},{8,0},{10,2},{12,4},{14,6},{1,9},{3,11}... | collective-permute-start | bytes 221192 | tf_op jit(solution)/shard_map/ppermute | solution.py:38
  362.1 6.3 %collective-permute-start.30 = (bf16[48,768]{1,0:T(8,128)(2,1)S(1)}, bf16[48,768]{1,0:T(8,128)(2,1)S(1)}, u32[]{:S(2)}, u32[]{:S(2)}) collective-permute-start(bf16[48,768]{1,0:T(8,128)(2,1)S(1)} %get-tuple-element.169), channel_id=1, source_target_pairs={{0,12},{2,14},{4,8},{6,10},{8,4},{10,6},{12,0},{14,2},{1,13},{3,15... | collective-permute-start | bytes 221192 | tf_op jit(solution)/shard_map/ppermute | solution.py:38
  369.9 7.9 %collective-permute-start.51 = (bf16[48,1152]{1,0:T(8,128)(2,1)}, bf16[48,1152]{1,0:T(8,128)(2,1)S(1)}, u32[]{:S(2)}, u32[]{:S(2)}) collective-permute-start(bf16[48,1152]{1,0:T(8,128)(2,1)} %get-tuple-element.181), channel_id=1, source_target_pairs={{0,4},{2,6},{12,8},{14,10},{1,5},{3,7},{13,9},{15,11},{16,20},{18,... | collective-permute-start | bytes 331784 | tf_op jit(solution)/shard_map/ppermute | solution.py:54
  377.7 212.6 %all-gather.8.cloned.1.call-start = ((), (), s32[]{:S(2)}) async-start(), calls=%async_computation.2 | async-start | bytes 2654208 | tf_op jit(solution)/shard_map/all_gather | solution.py:792
  380.0 9.8 %collective-permute-start.54 = (bf16[192,1152]{1,0:T(8,128)(2,1)}, bf16[192,1152]{1,0:T(8,128)(2,1)}, u32[]{:S(2)}, u32[]{:S(2)}) collective-permute-start(bf16[192,1152]{1,0:T(8,128)(2,1)} %pad_maximum_fusion.15), channel_id=1, source_target_pairs={{6,4},{4,6},{10,8},{8,10},{7,5},{5,7},{11,9},{9,11},{22,20},{20,22... | collective-permute-start | bytes 1327112 | tf_op jit(solution)/shard_map/ppermute | solution.py:54
  381.4 50.6 %collective-permute-start.55 = (bf16[192,1152]{1,0:T(8,128)(2,1)}, bf16[192,1152]{1,0:T(8,128)(2,1)S(1)}, u32[]{:S(2)}, u32[]{:S(2)}) collective-permute-start(bf16[192,1152]{1,0:T(8,128)(2,1)} %pad_maximum_fusion.15), channel_id=1, source_target_pairs={{20,4},{22,6},{24,8},{26,10},{4,20},{6,22},{8,24},{10,26},{21,5},{... | collective-permute-start | bytes 1327112 | tf_op jit(solution)/shard_map/ppermute | solution.py:54
  386.0 16.7 %collective-permute-start.32 = (bf16[4,48,1536]{2,1,0:T(8,128)(2,1)S(1)}, bf16[4,48,1536]{2,1,0:T(8,128)(2,1)S(1)}, u32[]{:S(2)}, u32[]{:S(2)}) collective-permute-start(bf16[4,48,1536]{2,1,0:T(8,128)(2,1)S(1)} %fusion.10), channel_id=1, source_target_pairs={{0,2},{2,0},{4,6},{6,4},{8,10},{10,8},{12,14},{14,12},{1,3},{3,1},... | collective-permute-start | bytes 1769480 | tf_op jit(solution)/shard_map/ppermute | solution.py:38
  389.2 32.6 %collective-permute-start.37 = (bf16[4,48,1536]{2,1,0:T(8,128)(2,1)S(1)}, bf16[4,48,1536]{2,1,0:T(8,128)(2,1)S(1)}, u32[]{:S(2)}, u32[]{:S(2)}) collective-permute-start(bf16[4,48,1536]{2,1,0:T(8,128)(2,1)S(1)} %fusion.11), channel_id=1, source_target_pairs={{0,2},{2,0},{4,6},{6,4},{8,10},{10,8},{12,14},{14,12},{1,3},{3,1},... | collective-permute-start | bytes 1769480 | tf_op jit(solution)/shard_map/ppermute | solution.py:38
  402.8 30.1 %collective-permute-start.33 = (bf16[48,1536]{1,0:T(8,128)(2,1)S(1)}, bf16[48,1536]{1,0:T(8,128)(2,1)S(1)}, u32[]{:S(2)}, u32[]{:S(2)}) collective-permute-start(bf16[48,1536]{1,0:T(8,128)(2,1)S(1)} %get-tuple-element.144), channel_id=1, source_target_pairs={{0,4},{2,6},{4,0},{6,2},{8,12},{10,14},{12,8},{14,10},{1,5},{3,7},... | collective-permute-start | bytes 442376 | tf_op jit(solution)/shard_map/ppermute | solution.py:38
  419.4 15.9 %collective-permute-start.34 = (bf16[48,1536]{1,0:T(8,128)(2,1)S(1)}, bf16[48,1536]{1,0:T(8,128)(2,1)S(1)}, u32[]{:S(2)}, u32[]{:S(2)}) collective-permute-start(bf16[48,1536]{1,0:T(8,128)(2,1)S(1)} %get-tuple-element.146), channel_id=1, source_target_pairs={{0,8},{2,10},{4,12},{6,14},{8,0},{10,2},{12,4},{14,6},{1,9},{3,11}... | collective-permute-start | bytes 442376 | tf_op jit(solution)/shard_map/ppermute | solution.py:38
  420.1 16.6 %collective-permute-start.35 = (bf16[48,1536]{1,0:T(8,128)(2,1)S(1)}, bf16[48,1536]{1,0:T(8,128)(2,1)S(1)}, u32[]{:S(2)}, u32[]{:S(2)}) collective-permute-start(bf16[48,1536]{1,0:T(8,128)(2,1)S(1)} %get-tuple-element.145), channel_id=1, source_target_pairs={{0,12},{2,14},{4,8},{6,10},{8,4},{10,6},{12,0},{14,2},{1,13},{3,15... | collective-permute-start | bytes 442376 | tf_op jit(solution)/shard_map/ppermute | solution.py:38
  422.0 16.2 %collective-permute-start.38 = (bf16[48,1536]{1,0:T(8,128)(2,1)S(1)}, bf16[48,1536]{1,0:T(8,128)(2,1)S(1)}, u32[]{:S(2)}, u32[]{:S(2)}) collective-permute-start(bf16[48,1536]{1,0:T(8,128)(2,1)S(1)} %get-tuple-element.147), channel_id=1, source_target_pairs={{0,4},{2,6},{4,0},{6,2},{8,12},{10,14},{12,8},{14,10},{1,5},{3,7},... | collective-permute-start | bytes 442376 | tf_op jit(solution)/shard_map/ppermute | solution.py:38
  432.0 15.6 %collective-permute-start.39 = (bf16[48,1536]{1,0:T(8,128)(2,1)S(1)}, bf16[48,1536]{1,0:T(8,128)(2,1)S(1)}, u32[]{:S(2)}, u32[]{:S(2)}) collective-permute-start(bf16[48,1536]{1,0:T(8,128)(2,1)S(1)} %get-tuple-element.149), channel_id=1, source_target_pairs={{0,8},{2,10},{4,12},{6,14},{8,0},{10,2},{12,4},{14,6},{1,9},{3,11}... | collective-permute-start | bytes 442376 | tf_op jit(solution)/shard_map/ppermute | solution.py:38
  432.9 14.7 %collective-permute-start.40 = (bf16[48,1536]{1,0:T(8,128)(2,1)S(1)}, bf16[48,1536]{1,0:T(8,128)(2,1)S(1)}, u32[]{:S(2)}, u32[]{:S(2)}) collective-permute-start(bf16[48,1536]{1,0:T(8,128)(2,1)S(1)} %get-tuple-element.148), channel_id=1, source_target_pairs={{0,12},{2,14},{4,8},{6,10},{8,4},{10,6},{12,0},{14,2},{1,13},{3,15... | collective-permute-start | bytes 442376 | tf_op jit(solution)/shard_map/ppermute | solution.py:38
  435.3 35.7 %collective-permute-start.57 = (bf16[192,1152]{1,0:T(8,128)(2,1)}, bf16[192,1152]{1,0:T(8,128)(2,1)}, u32[]{:S(2)}, u32[]{:S(2)}) collective-permute-start(bf16[192,1152]{1,0:T(8,128)(2,1)} %pad_maximum_fusion.15), channel_id=1, source_target_pairs={{5,4},{4,5},{7,6},{6,7},{9,8},{8,9},{11,10},{10,11},{21,20},{20,21... | collective-permute-start | bytes 1327112 | tf_op jit(solution)/shard_map/ppermute | solution.py:54
  436.7 17.0 %collective-permute-start.56 = (bf16[192,1152]{1,0:T(8,128)(2,1)}, bf16[192,1152]{1,0:T(8,128)(2,1)}, u32[]{:S(2)}, u32[]{:S(2)}) collective-permute-start(bf16[192,1152]{1,0:T(8,128)(2,1)} %collective-permute-done.54), channel_id=1, source_target_pairs={{20,4},{22,6},{24,8},{26,10},{4,20},{6,22},{8,24},{10,26},{21,5},{... | collective-permute-start | bytes 1327112 | tf_op jit(solution)/shard_map/ppermute | solution.py:54
  438.2 36.6 %collective-permute-start.58 = (bf16[192,1152]{1,0:T(8,128)(2,1)}, bf16[192,1152]{1,0:T(8,128)(2,1)}, u32[]{:S(2)}, u32[]{:S(2)}) collective-permute-start(bf16[192,1152]{1,0:T(8,128)(2,1)} %collective-permute-done.54), channel_id=1, source_target_pairs={{5,4},{4,5},{7,6},{6,7},{9,8},{8,9},{11,10},{10,11},{21,20},{20,21... | collective-permute-start | bytes 1327112 | tf_op jit(solution)/shard_map/ppermute | solution.py:54
  450.2 16.0 %collective-permute-start.41 = (bf16[48,1536]{1,0:T(8,128)(2,1)}, bf16[48,1536]{1,0:T(8,128)(2,1)S(1)}, u32[]{:S(2)}, u32[]{:S(2)}) collective-permute-start(bf16[48,1536]{1,0:T(8,128)(2,1)} %get-tuple-element.177), channel_id=1, source_target_pairs={{4,0},{6,2},{8,12},{10,14},{5,1},{7,3},{9,13},{11,15},{20,16},{22,... | collective-permute-start | bytes 442376 | tf_op jit(solution)/shard_map/ppermute | solution.py:54
  451.5 15.4 %collective-permute-start.42 = (bf16[48,1536]{1,0:T(8,128)(2,1)}, bf16[48,1536]{1,0:T(8,128)(2,1)S(1)}, u32[]{:S(2)}, u32[]{:S(2)}) collective-permute-start(bf16[48,1536]{1,0:T(8,128)(2,1)} %get-tuple-element.176), channel_id=1, source_target_pairs={{8,0},{10,2},{4,12},{6,14},{9,1},{11,3},{5,13},{7,15},{24,16},{26,... | collective-permute-start | bytes 442376 | tf_op jit(solution)/shard_map/ppermute | solution.py:54
  453.8 13.8 %collective-permute-start.43 = (bf16[48,1536]{1,0:T(8,128)(2,1)}, bf16[48,1536]{1,0:T(8,128)(2,1)S(1)}, u32[]{:S(2)}, u32[]{:S(2)}) collective-permute-start(bf16[48,1536]{1,0:T(8,128)(2,1)} %get-tuple-element.130), channel_id=1, source_target_pairs={{12,0},{14,2},{0,12},{2,14},{13,1},{15,3},{1,13},{3,15},{28,16},{3... | collective-permute-start | bytes 442376 | tf_op jit(solution)/shard_map/ppermute | solution.py:54
  466.2 23.8 %collective-permute-start.59 = (bf16[192,1152]{1,0:T(8,128)(2,1)}, bf16[192,1152]{1,0:T(8,128)(2,1)S(1)}, u32[]{:S(2)}, u32[]{:S(2)}) collective-permute-start(bf16[192,1152]{1,0:T(8,128)(2,1)} %copy-done.38), channel_id=1, source_target_pairs={{5,4},{4,5},{7,6},{6,7},{9,8},{8,9},{11,10},{10,11},{21,20},{20,21... | collective-permute-start | bytes 1327112 | tf_op jit(solution)/shard_map/ppermute | solution.py:54
  466.9 23.1 %collective-permute-start.60 = (bf16[192,1152]{1,0:T(8,128)(2,1)}, bf16[192,1152]{1,0:T(8,128)(2,1)S(1)}, u32[]{:S(2)}, u32[]{:S(2)}) collective-permute-start(bf16[192,1152]{1,0:T(8,128)(2,1)} %collective-permute-done.56), channel_id=1, source_target_pairs={{5,4},{4,5},{7,6},{6,7},{9,8},{8,9},{11,10},{10,11},{21,20},{20,21... | collective-permute-start | bytes 1327112 | tf_op jit(solution)/shard_map/ppermute | solution.py:54
  468.5 19.6 %collective-permute-start.44 = (bf16[192,1536]{1,0:T(8,128)(2,1)}, bf16[192,1536]{1,0:T(8,128)(2,1)}, u32[]{:S(2)}, u32[]{:S(2)}) collective-permute-start(bf16[192,1536]{1,0:T(8,128)(2,1)} %pad_maximum_fusion.13), channel_id=1, source_target_pairs={{2,0},{0,2},{14,12},{12,14},{3,1},{1,3},{15,13},{13,15},{18,16},{1... | collective-permute-start | bytes 1769480 | tf_op jit(solution)/shard_map/ppermute | solution.py:54
  471.0 23.4 %collective-permute-start.45 = (bf16[192,1536]{1,0:T(8,128)(2,1)}, bf16[192,1536]{1,0:T(8,128)(2,1)}, u32[]{:S(2)}, u32[]{:S(2)}) collective-permute-start(bf16[192,1536]{1,0:T(8,128)(2,1)} %pad_maximum_fusion.13), channel_id=1, source_target_pairs={{16,0},{18,2},{28,12},{30,14},{0,16},{2,18},{12,28},{14,30},{17,1}... | collective-permute-start | bytes 1769480 | tf_op jit(solution)/shard_map/ppermute | solution.py:54
  474.9 42.8 %collective-permute-start.47 = (bf16[192,1536]{1,0:T(8,128)(2,1)}, bf16[192,1536]{1,0:T(8,128)(2,1)}, u32[]{:S(2)}, u32[]{:S(2)}) collective-permute-start(bf16[192,1536]{1,0:T(8,128)(2,1)} %pad_maximum_fusion.13), channel_id=1, source_target_pairs={{1,0},{0,1},{3,2},{2,3},{13,12},{12,13},{15,14},{14,15},{17,16},{1... | collective-permute-start | bytes 1769480 | tf_op jit(solution)/shard_map/ppermute | solution.py:54
  488.1 17.9 %collective-permute-start.46 = (bf16[192,1536]{1,0:T(8,128)(2,1)}, bf16[192,1536]{1,0:T(8,128)(2,1)}, u32[]{:S(2)}, u32[]{:S(2)}) collective-permute-start(bf16[192,1536]{1,0:T(8,128)(2,1)} %collective-permute-done.44), channel_id=1, source_target_pairs={{16,0},{18,2},{28,12},{30,14},{0,16},{2,18},{12,28},{14,30},{17,1}... | collective-permute-start | bytes 1769480 | tf_op jit(solution)/shard_map/ppermute | solution.py:54
  492.5 25.1 %collective-permute-start.48 = (bf16[192,1536]{1,0:T(8,128)(2,1)}, bf16[192,1536]{1,0:T(8,128)(2,1)}, u32[]{:S(2)}, u32[]{:S(2)}) collective-permute-start(bf16[192,1536]{1,0:T(8,128)(2,1)} %collective-permute-done.44), channel_id=1, source_target_pairs={{1,0},{0,1},{3,2},{2,3},{13,12},{12,13},{15,14},{14,15},{17,16},{1... | collective-permute-start | bytes 1769480 | tf_op jit(solution)/shard_map/ppermute | solution.py:54
  494.5 23.2 %collective-permute-start.49 = (bf16[192,1536]{1,0:T(8,128)(2,1)}, bf16[192,1536]{1,0:T(8,128)(2,1)}, u32[]{:S(2)}, u32[]{:S(2)}) collective-permute-start(bf16[192,1536]{1,0:T(8,128)(2,1)} %collective-permute-done.45), channel_id=1, source_target_pairs={{1,0},{0,1},{3,2},{2,3},{13,12},{12,13},{15,14},{14,15},{17,16},{1... | collective-permute-start | bytes 1769480 | tf_op jit(solution)/shard_map/ppermute | solution.py:54
  506.0 11.7 %collective-permute-start.50 = (bf16[192,1536]{1,0:T(8,128)(2,1)}, bf16[192,1536]{1,0:T(8,128)(2,1)}, u32[]{:S(2)}, u32[]{:S(2)}) collective-permute-start(bf16[192,1536]{1,0:T(8,128)(2,1)} %collective-permute-done.46), channel_id=1, source_target_pairs={{1,0},{0,1},{3,2},{2,3},{13,12},{12,13},{15,14},{14,15},{17,16},{1... | collective-permute-start | bytes 1769480 | tf_op jit(solution)/shard_map/ppermute | solution.py:54
  570.7 7.8 %collective-permute-start.61 = (bf16[48,1536]{1,0:T(8,128)(2,1)}, bf16[48,1536]{1,0:T(8,128)(2,1)}, u32[]{:S(2)}, u32[]{:S(2)}) collective-permute-start(bf16[48,1536]{1,0:T(8,128)(2,1)} %get-tuple-element.167), channel_id=1, source_target_pairs={{0,4},{2,6},{4,0},{6,2},{8,12},{10,14},{12,8},{14,10},{1,5},{3,7},... | collective-permute-start | bytes 442376 | tf_op jit(solution)/shard_map/ppermute | solution.py:38
  570.7 14.2 %collective-permute-start.62 = (bf16[48,1536]{1,0:T(8,128)(2,1)}, bf16[48,1536]{1,0:T(8,128)(2,1)}, u32[]{:S(2)}, u32[]{:S(2)}) collective-permute-start(bf16[48,1536]{1,0:T(8,128)(2,1)} %get-tuple-element.166), channel_id=1, source_target_pairs={{0,8},{2,10},{4,12},{6,14},{8,0},{10,2},{12,4},{14,6},{1,9},{3,11}... | collective-permute-start | bytes 442376 | tf_op jit(solution)/shard_map/ppermute | solution.py:38
  570.8 14.2 %collective-permute-start.63 = (bf16[48,1536]{1,0:T(8,128)(2,1)S(1)}, bf16[48,1536]{1,0:T(8,128)(2,1)}, u32[]{:S(2)}, u32[]{:S(2)}) collective-permute-start(bf16[48,1536]{1,0:T(8,128)(2,1)S(1)} %get-tuple-element.165), channel_id=1, source_target_pairs={{0,12},{2,14},{4,8},{6,10},{8,4},{10,6},{12,0},{14,2},{1,13},{3,15... | collective-permute-start | bytes 442376 | tf_op jit(solution)/shard_map/ppermute | solution.py:38
  (70 other events, 503.1 us)
Sparse Core Ops, SparseCore 0:
  25.4 65.4 all-gather.3
Sparse Core Ops, SparseCore 1:
  377.8 51.8 all-gather.5
  453.8 52.3 all-gather.7

commit v3 on v2

--- a/solution.py
+++ b/solution.py
@@ -102,12 +102,12 @@
 
 
 def project_kernel(
-    near, far, w_near, w_far, bias, vec_near, vec_far, cos_ref, sin_ref, *outs
+    near, far, w_near, w_far, a_near, a_far, bias, vec_near, vec_far, cos_ref, sin_ref, *outs
 ):
     outs = outs[-4:]
-    half = outs[0].shape[1]
+    rows, half = outs[0].shape
     width = 2 * half
-    own, other = near[:, :half].astype(WIDE), far[:, :half].astype(WIDE)
+    own, other = near[:rows].astype(WIDE), far[:rows].astype(WIDE)
     mean = (
         jnp.sum(own, axis=1, keepdims=True) + jnp.sum(other, axis=1, keepdims=True)
     ) / width
@@ -118,59 +118,51 @@
     inv_std = lax.rsqrt(var + 1e-5)
     own = (own * inv_std * vec_near[0:1] + vec_near[1:2]).astype(LOW)
     other = (other * inv_std * vec_far[0:1] + vec_far[1:2]).astype(LOW)
-    lane = lax.broadcasted_iota(jnp.int32, (own.shape[0], BLK), 1)
+    lane = lax.broadcasted_iota(jnp.int32, (rows, BLK), 1)
     cosine, sine = cos_ref[...], sin_ref[...]
     for part, out in enumerate(outs[:3]):
-        span = slice(part * half, (part + 1) * half)
-        made = dot_nn(own, w_near[:, span]) + dot_nn(other, w_far[:, span]) + bias[:, span]
+        made = dot_nn(own, w_near[part]) + dot_nn(other, w_far[part]) + bias[part : part + 1]
         for pair in range(half // BLK):
             lanes = slice(pair * BLK, (pair + 1) * BLK)
             block = made[:, lanes]
             if part < 2:
                 block = turned(block, cosine, sine, lane)
             out[:, lanes] = block.astype(LOW)
-    span = slice(3 * half, 4 * half)
-    outs[3][...] = (
-        dot_nn(near[:, half:], w_near[:, span]) + dot_nn(far[:, half:], w_far[:, span])
-    ).astype(LOW)
-
-
-def project_rows(part, pack, near, far, weights, cosine, sine, made):
-    rows = near.shape[0]
-    half = near.shape[1] // 2
-    base = part * (rows // CHUNK)
+    outs[3][...] = (dot_nt(near[rows:], a_near[...]) + dot_nt(far[rows:], a_far[...])).astype(LOW)
+
+
+def project_rows(place, count, near, far, weights, cosine, sine, made, after):
+    rows, half = near.shape[0] // 2, near.shape[1]
 
     def fixed(array):
         return pl.BlockSpec(array.shape, lambda i: (0,) * array.ndim)
 
     def placed(width):
-        return pl.BlockSpec((CHUNK, width), lambda i: (i + base, 0))
-
-    here = pl.BlockSpec((CHUNK, 2 * half), lambda i: (i, 0))
+        return pl.BlockSpec((rows, width), lambda i: (place, 0))
+
+    extra = tuple(made) + tuple(after)
     before = 4 + len(weights)
     return pl.pallas_call(
         project_kernel,
-        grid=(rows // CHUNK,),
-        in_specs=[here] * 2
+        grid=(1,),
+        in_specs=[fixed(near), fixed(far)]
         + [fixed(w) for w in weights]
         + [placed(BLK)] * 2
-        + [pl.BlockSpec(memory_space=pl.ANY)] * len(made),
+        + [pl.BlockSpec(memory_space=pl.ANY)] * len(extra),
         out_specs=[placed(half)] * 4,
-        out_shape=[jax.ShapeDtypeStruct((pack, half), LOW)] * 4,
+        out_shape=[jax.ShapeDtypeStruct((count * rows, half), LOW)] * 4,
         input_output_aliases={before + i: i for i in range(len(made))},
         compiler_params=pltpu.CompilerParams(vmem_limit_bytes=VMEM_ASK),
         cost_estimate=pl.CostEstimate(
-            flops=48 * rows * half * half, bytes_accessed=20 * rows * half, transcendentals=0
+            flops=60 * rows * half * half, bytes_accessed=20 * rows * half, transcendentals=0
         ),
         name="project_rows",
-    )(near, far, *weights, cosine, sine, *made)
+    )(near, far, *weights, cosine, sine, *extra)
 
 
 def feed_kernel(
     x_ref,
-    xt_ref,
     g_ref,
-    gt_ref,
     up_ref,
     down_ref,
     bias_ref,
@@ -179,32 +171,30 @@
     dup_ref,
     ddown_ref,
     dbias_ref,
+    xt_ref,
+    gt_ref,
 ):
+    @pl.when(pl.program_id(0) == 0)
+    def _():
+        xt_ref[...] = x_ref[...].T
+        gt_ref[...] = g_ref[...].T
+        out_ref[...] = jnp.zeros(out_ref.shape, WIDE)
+        dx_ref[...] = jnp.zeros(dx_ref.shape, WIDE)
+
     hidden = dot_nn(x_ref[...], up_ref[...]) + bias_ref[...]
-    grad = dot_nn(g_ref[...], down_ref[...])
+    grad = dot_nt(g_ref[...], down_ref[...])
     below = 0.5 + 0.5 * lax.erf(hidden * math.sqrt(0.5))
     density = jnp.exp(-0.5 * hidden * hidden) * (1.0 / math.sqrt(2.0 * math.pi))
     active = (hidden * below).astype(LOW)
     grad = (grad * (below + hidden * density)).astype(LOW)
     dbias_ref[...] = jnp.sum(grad.astype(WIDE), axis=0, keepdims=True)
-    out = dot_nt(active, down_ref[...])
-    dx = dot_nt(grad, up_ref[...])
-
-    @pl.when(pl.program_id(0) == 0)
-    def _():
-        out_ref[...] = out
-        dx_ref[...] = dx
-
-    @pl.when(pl.program_id(0) != 0)
-    def _():
-        out_ref[...] += out
-        dx_ref[...] += dx
-
+    out_ref[...] += dot_nn(active, down_ref[...])
+    dx_ref[...] += dot_nt(grad, up_ref[...])
     dup_ref[...] = dot_nn(xt_ref[...], grad).astype(LOW)
     ddown_ref[...] = dot_nn(gt_ref[...], active).astype(LOW)
 
 
-def feed_forward(x, g, up_down, bias):
+def feed_forward(x, g, up, down, bias):
     rows, width = x.shape
     hidden = bias.shape[1]
     step = 512
@@ -214,24 +204,25 @@
         return pl.BlockSpec(shape, lambda i: (0, 0))
 
     column = pl.BlockSpec((width, step), lambda i: (0, i))
+    line = pl.BlockSpec((1, step), lambda i: (0, i))
     return pl.pallas_call(
         feed_kernel,
         grid=(steps,),
         in_specs=[
             whole((rows, width)),
-            whole((width, rows)),
             whole((rows, width)),
-            whole((width, rows)),
             column,
-            pl.BlockSpec((width, step), lambda i: (0, i + steps)),
-            pl.BlockSpec((1, step), lambda i: (0, i)),
+            pl.BlockSpec((step, width), lambda i: (i, 0)),
+            line,
         ],
         out_specs=[
             whole((rows, width)),
             whole((rows, width)),
             column,
             column,
-            pl.BlockSpec((1, step), lambda i: (0, i)),
+            line,
+            whole((width, rows)),
+            whole((width, rows)),
         ],
         out_shape=[
             jax.ShapeDtypeStruct((rows, width), WIDE),
@@ -239,13 +230,37 @@
             jax.ShapeDtypeStruct((width, hidden), LOW),
             jax.ShapeDtypeStruct((width, hidden), LOW),
             jax.ShapeDtypeStruct((1, hidden), WIDE),
+            jax.ShapeDtypeStruct((width, rows), LOW),
+            jax.ShapeDtypeStruct((width, rows), LOW),
         ],
         compiler_params=pltpu.CompilerParams(vmem_limit_bytes=VMEM_ASK),
         cost_estimate=pl.CostEstimate(
-            flops=20 * rows * width * hidden, bytes_accessed=12 * width * hidden, transcendentals=0
+            flops=26 * rows * width * hidden, bytes_accessed=12 * width * hidden, transcendentals=0
         ),
         name="feed_forward",
-    )(x, x.T, g, g.T, up_down, up_down, bias)
+    )(x, g, up, down, bias)
+
+
+def outer_kernel(left_a, right_a, left_b, right_b, out_ref):
+    half = right_a.shape[1]
+    out_ref[:, :half] = dot_nn(left_a[...], right_a[...]).astype(LOW)
+    out_ref[:, half:] = dot_nn(left_b[...], right_b[...]).astype(LOW)
+
+
+def outer_pair(left_a, right_a, left_b, right_b):
+    rows, depth = left_a.shape
+    half = right_a.shape[1]
+    return pl.pallas_call(
+        outer_kernel,
+        in_specs=[vmem()] * 4,
+        out_specs=vmem(),
+        out_shape=jax.ShapeDtypeStruct((rows, 2 * half), LOW),
+        compiler_params=pltpu.CompilerParams(vmem_limit_bytes=VMEM_ASK),
+        cost_estimate=pl.CostEstimate(
+            flops=8 * rows * depth * half, bytes_accessed=6 * rows * depth, transcendentals=0
+        ),
+        name="outer_pair",
+    )(left_a, right_a, left_b, right_b)
 
 
 def lane_tiles(array, combine):
@@ -426,6 +441,7 @@
     first,
     last,
     inverse,
+    natural,
     q_ref,
     k_ref,
     v_ref,
@@ -434,13 +450,9 @@
     sin_ref,
     end_ref,
     stat_ref,
-    dk_out,
-    dv_out,
-    k_scr,
-    v_scr,
-    dk_scr,
-    dv_scr,
+    *rest,
 ):
+    dk_out, dv_out, k_scr, v_scr, dk_scr, dv_scr = rest[-6:]
     pairs = q_ref.shape[1] // BLK
     own = dk_out.shape[0] // BLK
     half_stat = stat_ref.shape[1] // 2
@@ -469,7 +481,7 @@
             query_place = query0 + lax.broadcasted_iota(jnp.int32, (BLK, CHUNK), 1)
             allowed = (query_place >= places) & (query_place < ends)
             count = CHUNK // BLK
-            slots = [inverse[c * count + i] for i in range(count)]
+            slots = [natural[c * count + i] for i in range(count)]
 
             def stat(row):
                 return jnp.concatenate([stat_ref[slot, row : row + 1, :] for slot in slots], 1)
@@ -500,7 +512,20 @@
 
 
 def key_side(
-    blocks, first, last, inverse, queries, keys, values, grads, cosine, sine, ends, stats
+    blocks,
+    first,
+    last,
+    inverse,
+    natural,
+    queries,
+    keys,
+    values,
+    grads,
+    cosine,
+    sine,
+    ends,
+    stats,
+    after,
 ):
     own = blocks.shape[0]
     width = queries.shape[1]
@@ -508,7 +533,7 @@
     work = 2 * BLK * CHUNK
     return pl.pallas_call(
         key_kernel,
-        in_specs=[smem()] * 4 + [vmem()] * 8,
+        in_specs=[smem()] * 5 + [vmem()] * 8 + [pl.BlockSpec(memory_space=pl.ANY)] * len(after),
         out_specs=[vmem()] * 2,
         out_shape=[jax.ShapeDtypeStruct((own * BLK, width), LOW)] * 2,
         scratch_shapes=[
@@ -524,7 +549,22 @@
             transcendentals=own * pairs * 4 * work,
         ),
         name="key_side",
-    )(blocks, first, last, inverse, queries, keys, values, grads, cosine, sine, ends, stats)
+    )(
+        blocks,
+        first,
+        last,
+        inverse,
+        natural,
+        queries,
+        keys,
+        values,
+        grads,
+        cosine,
+        sine,
+        ends,
+        stats,
+        *after,
+    )
 
 
 TILE = 256
@@ -543,15 +583,15 @@
     half = span // 2
     step = 768
     cuts = [slice(i, i + step) for i in range(0, span, step)]
+    pltpu.sync_copy(near.at[:, pl.ds(0, half)], low_scr.at[:, pl.ds(0, half)])
+    pltpu.sync_copy(far.at[:, pl.ds(0, half)], low_scr.at[:, pl.ds(half, half)])
     total = jnp.zeros((1, 1), WIDE)
-    for source, base in ((near, 0), (far, half)):
-        for i in range(0, half, 384):
-            part = source[:, i : i + 384].astype(WIDE)
-            wide_scr[:, base + i : base + i + 384] = part
-            total = total + jnp.sum(part * part)
+    for cut in cuts:
+        part = low_scr[:, cut].astype(WIDE)
+        total = total + jnp.sum(part * part)
     factor = 1.0 / (jnp.sqrt(total) + 1e-7)
     for cut in cuts:
-        part = wide_scr[:, cut] * factor
+        part = low_scr[:, cut].astype(WIDE) * factor
         wide_scr[:, cut] = part
         low_scr[:, cut] = part.astype(LOW)
 
@@ -572,6 +612,8 @@
 
     polynomial()
     rows = out_ref.shape[0]
+    if half < out_ref.shape[1]:
+        out_ref[:, half:] = jnp.zeros((rows, out_ref.shape[1] - half), LOW)
     for i in range(0, half, 384):
         cut = slice(i, i + 384)
         out_ref[:, cut] = (
@@ -580,7 +622,6 @@
 
 
 def ns_kernel(spans, high, near_a, far_a, near_b, far_b, out_ref, *scratch):
-    out_ref[...] = jnp.zeros(out_ref.shape, LOW)
     widest = max(spans)
     for span in sorted(set(spans)):
         wanted = jnp.bool_(False)
@@ -599,7 +640,7 @@
     kept = rows if rows % 16 == 0 else size
     out = pl.pallas_call(
         partial(ns_kernel, spans),
-        in_specs=[smem()] + [vmem()] * 4,
+        in_specs=[smem()] + [pl.BlockSpec(memory_space=pl.ANY)] * 4,
         out_specs=vmem(),
         out_shape=jax.ShapeDtypeStruct((kept, half), LOW),
         scratch_shapes=[
@@ -681,40 +722,63 @@
     def far_half(array):
         return jnp.where(first_tp, array[:, half:], array[:, :half])
 
-    own_pair = jnp.concatenate([tokens, cotangent], axis=1)
-    far_pair = partner(own_pair, "tp", 1)
-    inputs_low = both_halves(tokens, far_pair[:, :half], 1)
-    full_cotangent = both_halves(cotangent, far_pair[:, half:], 1)
-
-    near = [own_pair] + [partner(own_pair, "ctx", s * low_count) for s in range(1, OWNERS)]
-    near_parts = [jnp.concatenate(near, axis=0)]
-    for s in range(1, low_count):
-        near_parts.append(jnp.concatenate([partner(part, "ctx", s) for part in near], axis=0))
-    far_parts = [partner(part, "tp", 1) for part in near_parts]
-
-    joint_full = gather_axis(
-        jnp.concatenate(
-            [w_qkv.astype(LOW).reshape(w_qkv.shape[0], 3 * half), w_attn.astype(LOW).T], axis=1
-        ),
-        "fsdp",
-        0,
-    )
-    up_down = lax.all_gather(
-        jnp.concatenate([w_up.astype(LOW), w_down.astype(LOW).T], axis=1),
-        "fsdp",
-        axis=0,
-        tiled=True,
+    own_pair = jnp.concatenate([tokens, cotangent], axis=0)
+
+    def send_high(value, pairs):
+        return lax.ppermute(
+            value,
+            "ctx",
+            [(a * low_count + i, b * low_count + i) for a, b in pairs for i in range(low_count)],
+        )
+
+    inner = (ctx_high == 1) | (ctx_high == 2)
+    between, outward = [(1, 2), (2, 1)], [(1, 0), (2, 3)]
+    beside = send_high(own_pair, [(0, 1), (1, 0), (2, 3), (3, 2)])
+    middle = send_high(own_pair, between)
+    lasting = send_high(beside, between)
+    line = [
+        own_pair,
+        beside,
+        jnp.where(inner, middle, send_high(middle, outward)),
+        jnp.where(inner, lasting, send_high(lasting, outward)),
+    ]
+    order = sorted(
+        ((low, slot) for low in range(low_count) for slot in range(OWNERS)),
+        key=lambda item: (item[1] + (item[0] > 0), item[0]),
+    )
+    blocks_near = [
+        line[slot] if low == 0 else partner(line[slot], "ctx", low) for low, slot in order
+    ]
+    blocks_far = [partner(block, "tp", 1) for block in blocks_near]
+    far_pair = blocks_far[0]
+    inputs_low = both_halves(tokens, far_pair[:row_count], 1)
+    full_cotangent = both_halves(cotangent, far_pair[row_count:], 1)
+
+    up_full = gather_axis(w_up.astype(LOW), "fsdp", 0)
+    down_full = gather_axis(w_down.astype(LOW), "fsdp", 1)
+    attn_full = gather_axis(w_attn.astype(LOW), "fsdp", 1)
+    qkv_full = lax.all_gather(
+        jnp.transpose(w_qkv, (1, 0, 2)).astype(LOW), "fsdp", axis=1, tiled=True
     )
 
     def group_place(ctx):
-        differs = ctx ^ ctx_index
-        return (differs % low_count) * OWNERS + differs // low_count
+        high = ctx // low_count
+        slot = jnp.where(
+            high == ctx_high,
+            0,
+            jnp.where(high == ctx_high ^ 1, 1, jnp.where((high == 1) | (high == 2), 2, 3)),
+        )
+        low = (ctx % low_count) ^ ctx_low
+        place = jnp.zeros_like(ctx)
+        for k, (its_low, its_slot) in enumerate(order):
+            place = jnp.where((low == its_low) & (slot == its_slot), k, place)
+        return place
 
     slot_blocks = jnp.arange(block_row.shape[0], dtype=jnp.int32)
     slot_places = group_place(slot_blocks // own_blocks) * own_blocks + slot_blocks % own_blocks
-    inverse = jnp.sum(
-        jnp.where(block_row[None, :] == slot_blocks[:, None], slot_places[None, :], 0), axis=1
-    ).astype(jnp.int32)
+    holds = block_row[None, :] == slot_blocks[:, None]
+    inverse = jnp.sum(jnp.where(holds, slot_places[None, :], 0), axis=1).astype(jnp.int32)
+    natural = jnp.sum(jnp.where(holds, slot_blocks[None, :], 0), axis=1).astype(jnp.int32)
     my_blocks = lax.dynamic_slice_in_dim(block_row, ctx_index * own_blocks, own_blocks)
 
     seq_ends = jnp.cumsum(length_row).astype(jnp.int32)
@@ -745,30 +809,29 @@
         left, right = jnp.split(array, 2, axis=dim)
         return jnp.where(first_tp, left, right), jnp.where(first_tp, right, left)
 
-    projections = (
-        *own_first(joint_full, 0),
-        qkv_bias.reshape(1, 3 * half),
-        *own_first(norm_vectors, 1),
-    )
-    made = ()
-    for part, (near_part, far_part) in enumerate(zip(near_parts, far_parts)):
-        made = project_rows(
-            part, pack, near_part, far_part, projections, cosine, sine, made
-        )
-    queries, keys, values, d_attended = made
-
     inputs = inputs_low.astype(WIDE)
     centered = inputs - jnp.mean(inputs, axis=1, keepdims=True)
     inv_std = lax.rsqrt(jnp.mean(centered * centered, axis=1, keepdims=True) + 1e-05)
     normed = centered * inv_std
     norm_out = (normed * norm_vectors[0] + norm_vectors[1]).astype(LOW)
     hidden_here = up_bias.shape[0]
-    feed_out, feed_dx, grad_up, grad_down, grad_ubias = feed_forward(
-        norm_out, full_cotangent, up_down, up_bias.reshape(1, hidden_here)
-    )
-
-    def outer(left, right):
-        return jnp.einsum("na,nb->ab", left, right, preferred_element_type=WIDE).astype(LOW)
+    feed_out, feed_dx, grad_up, grad_down, grad_ubias, norm_t, cotangent_t = feed_forward(
+        norm_out, full_cotangent, up_full, down_full, up_bias.reshape(1, hidden_here)
+    )
+
+    projections = (
+        *own_first(qkv_full, 1),
+        *own_first(attn_full, 1),
+        qkv_bias,
+        *own_first(norm_vectors, 1),
+    )
+    made = ()
+    for place, (near, far) in enumerate(zip(blocks_near, blocks_far)):
+        after = (grad_ubias,) if place == len(order) - 3 else ()
+        made = project_rows(
+            place, len(order), near, far, projections, cosine, sine, made, after
+        )
+    queries, keys, values, d_attended = made
 
     def reduced_first(gradient):
         rows = gradient.shape[0] // fsdp_count
@@ -782,8 +845,20 @@
         part = sum_scatter(jnp.swapaxes(part, 0, 1), "ctx", 1, ctx_low)
         return sum_scatter(part, "ctx", low_count, ctx_high)
 
-    sum_up = reduced_rest(reduced_first(grad_up))
-    sum_down = reduced_rest(reduced_first(grad_down))
+    first_up, first_down = reduced_first(grad_up), reduced_first(grad_down)
+
+    def scatter_low(part):
+        piece = part.shape[0] // ctx_count
+        part = part.reshape(OWNERS, low_count, piece, part.shape[1])
+        return sum_scatter(jnp.swapaxes(part, 0, 1), "ctx", 1, ctx_low)
+
+    sum_feed = sum_scatter(
+        jnp.concatenate([scatter_low(first_up), scatter_low(first_down)], axis=2),
+        "ctx",
+        low_count,
+        ctx_high,
+    )
+    sum_up, sum_down = sum_feed[:, :hidden_here], sum_feed[:, hidden_here:]
     piece = sum_up.shape[0]
     grad_outbias = jnp.sum(cotangent.astype(WIDE), axis=0)
 
@@ -802,7 +877,7 @@
         return (
             my_rows(up, 0),
             my_rows(attn, 1).T,
-            my_rows(qkv, 0).reshape(piece, 3 * half),
+            jnp.concatenate([my_rows(qkv, 0)[:, i] for i in range(3)], axis=1),
             my_rows(down, 1).T,
         )
 
@@ -828,10 +903,14 @@
                 partner_among(part, ("fsdp", "ctx"), (s, 0), lambda i: wanted(i[1]))
                 for part in parts[:low_count]
             ]
+        joined = [
+            jnp.concatenate(parts[i : i + low_count], axis=0)
+            for i in range(0, len(parts), low_count)
+        ]
         others = [
-            partner_among(part, ("ctx", "tp"), (0, 1), lambda i: wanted(i[0])) for part in parts
+            partner_among(part, ("ctx", "tp"), (0, 1), lambda i: wanted(i[0])) for part in joined
         ]
-        return jnp.concatenate(parts, axis=0), jnp.concatenate(others, axis=0)
+        return jnp.concatenate(joined, axis=0), jnp.concatenate(others, axis=0)
 
     wide_pair = to_owners(
         {0: 0.95 * old_moments[0] + sum_up, 3: 0.95 * old_moments[3] + sum_down}
@@ -851,19 +930,15 @@
         my_starts[:, None],
     )
     sum_early = reduced_rest(
-        reduced_first(
-            jnp.concatenate([outer(norm_out, grad_q), outer(full_cotangent, attended)], axis=1)
-        )
-    )
-    near_stats = [stats] + [partner(stats, "ctx", s * low_count) for s in range(1, OWNERS)]
-    all_stats = list(near_stats)
-    for s in range(1, low_count):
-        all_stats += [partner(part, "ctx", s) for part in near_stats]
+        reduced_first(outer_pair(norm_t, grad_q, cotangent_t, attended))
+    )
+    all_stats = lax.all_gather(stats, "ctx", axis=0, tiled=True)
     grad_k, grad_v = key_side(
         my_blocks,
         query_first,
         query_last,
         inverse,
+        natural,
         queries,
         keys,
         values,
@@ -871,18 +946,19 @@
         cosine,
         sine,
         my_ends[:, None],
-        jnp.concatenate(all_stats, axis=0),
-    )
-    grad_late = outer(norm_out, jnp.concatenate([grad_k, grad_v], axis=1))
+        all_stats,
+        (first_up, first_down),
+    )
+    grad_late = outer_pair(norm_t, grad_k, norm_t, grad_v)
     late_rows = reduced_first(grad_late)
     sum_late = reduced_rest(late_rows)
     grad_q, grad_k, grad_v, grad_late = lax.optimization_barrier(
         (grad_q, grad_k, grad_v, grad_late)
     )
-    grad_proj = jnp.concatenate([grad_q, grad_k, grad_v], axis=1)
-    grad_qbias = jnp.sum(grad_proj.astype(WIDE), axis=0)
-
-    partial_out = dot_nt(attended, joint_full[:, 3 * half :]) + feed_out
+    grad_proj = (grad_q, grad_k, grad_v)
+    grad_qbias = jnp.concatenate([jnp.sum(grad.astype(WIDE), axis=0) for grad in grad_proj])
+
+    partial_out = dot_nn(attended, attn_full) + feed_out
 
     def sum_halves(array):
         return own_half(array) + partner(far_half(array).astype(LOW), "tp", 1).astype(WIDE)
@@ -890,7 +966,9 @@
     out_bias = own_half((norm_vectors[2] + norm_vectors[3])[None, :])
     mixed = (tokens.astype(WIDE) + sum_halves(partial_out) + out_bias).astype(LOW)
 
-    grad_norm = sum_halves(dot_nt(grad_proj, joint_full[:, : 3 * half]) + feed_dx)
+    grad_norm = sum_halves(
+        sum(dot_nt(grad, qkv_full[i]) for i, grad in enumerate(grad_proj)) + feed_dx
+    )
     my_normed = own_half(normed)
     scaled = grad_norm * own_half(norm_vectors[0:1])
     row_sums = jnp.stack([jnp.sum(scaled, axis=1), jnp.sum(scaled * my_normed, axis=1)])
@@ -914,7 +992,7 @@
     sum_qkv = jnp.concatenate([sum_early[:, :half], sum_late], axis=1)
     sum_attn = sum_early[:, half:]
     gathered = all_rows(sum_qkv, sum_attn)
-    fresh_qkv = 0.95 * qkv_moment + gathered[:, : 3 * half].reshape(qkv_moment.shape)
+    fresh_qkv = 0.95 * qkv_moment + jnp.stack(jnp.split(gathered[:, : 3 * half], 3, axis=1), axis=1)
     fresh_attn = 0.95 * attn_moment + gathered[:, 3 * half :].T
     own_attn = jnp.pad(0.95 * old_moments[1] + sum_attn, ((0, 0), (0, 2 * half)))
     short_pair = to_owners({1: own_attn, 2: 0.95 * old_moments[2] + sum_qkv})
@@ -949,7 +1027,7 @@
         mixed,
         grad_tokens,
         fresh_qkv,
-        new_qkv.reshape(piece, 3, half),
+        jnp.stack(jnp.split(new_qkv, 3, axis=1), axis=1),
         fresh_attn,
         new_attn.T,
         fresh_up,

time: 618 us -> 569 us (0.921)
  local copies, waits for them, and re-layouts: 111 us -> 54.5 us
  starting transfers between devices: 139 us -> 89.2 us
  blocking collectives: 0 us -> 35.5 us
  Pallas kernels: 125 us -> 147 us
  waiting for transfers between devices: 121 us -> 137 us
  other arithmetic: 75.4 us -> 66.7 us
  matrix products: 18.7 us -> 12 us
    ppermute x49 -> x43, starting transfers between devices: 103 us -> 52 us  [partner(): return lax.ppermute(value, axis, [(i, i ^ step) for i in range(size)])]
    all_gather x0 -> x1, blocking collectives: none -> 35.5 us  [body(): all_stats = lax.all_gather(stats, 'ctx', axis=0, tiled=True)]
    unnamed x160 -> x169, local copies, waits for them, and re-layouts: 55.8 us -> 27.5 us
    pallas_call x4 -> x12, Pallas kernels: 89.3 us -> 115 us  [the longest x1 46.1 us: orthogonal_rows(): pl.pallas_call(partial(ns_kernel, spans), in_specs=[smem()] + [pl.BlockSp...]
    concatenate x8 -> x6, local copies, waits for them, and re-layouts: 15.5 us -> 6.02 us  [the longest x2 2.26 us: to_owners(): jnp.concatenate(parts[i:i + low_count], axis=0)]
    ppermute x2 -> x0, local copies, waits for them, and re-layouts: 9.4 us -> none  [partner(): return lax.ppermute(value, axis, [(i, i ^ step) for i in range(size)])]
    ppermute x0 -> x5, starting transfers between devices: none -> 8.85 us  [send_high(): lax.ppermute(value, 'ctx', [(a * low_count + i, b * low_count + i) for a,...]
    ppermute x0 -> x5, waiting for transfers between devices: none -> 8.31 us  [send_high(): lax.ppermute(value, 'ctx', [(a * low_count + i, b * low_count + i) for a,...]
  transfers between devices with their start and end apart: 72 -> 67, of which waited for: 21 -> 22; matrix products, arithmetic and copies ran while one was open for 31% -> 20% of each run, Pallas kernels for 21% -> 26%
where the time goes in v3:
time: 569 us; the launch traced here: 558 us
  Pallas kernels  147 us (26%)
  waiting for transfers between devices  137 us (24%)
  starting transfers between devices  89.2 us (16%)
  other arithmetic  66.7 us (12%)
  local copies, waits for them, and re-layouts  54.5 us (10%)
  blocking collectives  35.5 us (6%)
  between operations  15.5 us (3%)
  matrix products  12 us (2%)
    ppermute x43, waiting for transfers between devices, partner(): return lax.ppermute(value, axis, [(i, i ^ step) for i in range(size)])  109 us
    ppermute x43, starting transfers between devices, partner(): return lax.ppermute(value, axis, [(i, i ^ step) for i in range(size)])  52 us
    pallas_call x1, Pallas kernels, orthogonal_rows(): pl.pallas_call(partial(ns_kernel, spans), in_specs=[smem()] + [pl.BlockSp...  46.1 us
    pallas_call x8, Pallas kernels, project_rows(): pl.pallas_call(project_kernel, grid=(1,), in_specs=[fixed(near), fixed(fa...  43.7 us
    all_gather x1, blocking collectives, body(): all_stats = lax.all_gather(stats, 'ctx', axis=0, tiled=True)  35.5 us
    ppermute x16, starting transfers between devices, partner_among(): return lax.ppermute(value, tuple(axes), pairs)  28.3 us
    unnamed x169, local copies, waits for them, and re-layouts  27.5 us
    pallas_call x1, Pallas kernels, query_side(): pl.pallas_call(query_kernel, in_specs=[smem()] * 4 + [vmem()] * 7, out_sp...  20.2 us
  transfers between devices with their start and end apart: 67, of which 22 were waited for; matrix products, arithmetic and copies ran while one was open for 20% of the time, Pallas kernels for 26%

profile of v3, /device:TPU:0, one launch (start us, length us, event | category | flops | bytes accessed | tf_op | source)
XLA Modules:
  0.0 557.8 jit_solution(3736214413675951050)
XLA Ops:
  7.2 1.9 constant_dynamic-update-slice_fusion.1
  9.2 1.8 constant_dynamic-update-slice_fusion.near
  11.4 2.6 collective-permute-start
  26.8 3.4 convolution_add_fusion.cos_ref
  31.4 2.8 convert_element_type.270
  36.6 2.1 copy.105
  38.7 3.1 copy.104
  41.8 2.1 copy.117
  44.6 5.1 fusion.38.sin_ref
  57.3 1.8 fusion.1
  59.1 19.6 %collective-permute-done.18 = bf16[384,1536]{1,0:T(8,128)(2,1)S(1)} collective-permute-done((bf16[384,1536]{1,0:T(8,128)(2,1)S(1)}, bf16[384,1536]{1,0:T(8,128)(2,1)S(1)}, u32[]{:S(2)}, u32[]{:S(2)}) %collective-permute-start.18) | collective-permute-done | bytes 1179680 | tf_op jit(solution)/shard_map/ppermute | solution.py:38
  82.6 20.0 %collective-permute-done.19 = bf16[1536,384]{1,0:T(8,128)(2,1)S(1)} collective-permute-done((bf16[1536,384]{1,0:T(8,128)(2,1)S(1)}, bf16[1536,384]{1,0:T(8,128)(2,1)S(1)}, u32[]{:S(2)}, u32[]{:S(2)}) %collective-permute-start.19) | collective-permute-done | bytes 1179680 | tf_op jit(solution)/shard_map/ppermute | solution.py:38
  106.0 12.4 %feed_forward.1 = (f32[512,768]{1,0:T(8,128)}, f32[512,768]{1,0:T(8,128)}, bf16[768,1536]{1,0:T(8,128)(2,1)}, bf16[768,1536]{1,0:T(8,128)(2,1)}, f32[1,1536]{1,0...) custom-call(bf16[512,768]{1,0:T(8,128)(2,1)} %get-tuple-element.236.x_ref, ...), custom_call_target="tpu_custom_call" | custom-call | flops 15703474176 | bytes 14155776 | tf_op jit(solution)/shard_map/feed_forward/pallas_call | solution.py:208
  118.4 2.5 dynamic-slice_bitcast_fusion
  124.2 3.1 broadcast_select_fusion.4
  127.2 5.4 project_rows.8
  135.9 5.4 project_rows.9
  141.3 5.4 project_rows.10
  147.3 6.8 %collective-permute-done.2 = bf16[1024,384]{1,0:T(8,128)(2,1)S(1)} collective-permute-done((bf16[1024,384]{1,0:T(8,128)(2,1)}, bf16[1024,384]{1,0:T(8,128)(2,1)S(1)}, u32[]{:S(2)}, u32[]{:S(2)}) %collective-permute-start.2) | collective-permute-done | bytes 786464 | tf_op jit(solution)/shard_map/ppermute | solution.py:728
  157.9 5.5 project_rows.11
  163.4 11.3 %collective-permute-done.21 = bf16[384,1536]{1,0:T(8,128)(2,1)S(1)} collective-permute-done((bf16[384,1536]{1,0:T(8,128)(2,1)}, bf16[384,1536]{1,0:T(8,128)(2,1)S(1)}, u32[]{:S(2)}, u32[]{:S(2)}) %collective-permute-start.21) | collective-permute-done | bytes 1179680 | tf_op jit(solution)/shard_map/ppermute | solution.py:38
  179.4 5.5 project_rows.12
  184.8 11.9 %collective-permute-done.36 = bf16[4,48,1536]{2,1,0:T(8,128)(2,1)} collective-permute-done((bf16[4,48,1536]{2,1,0:T(8,128)(2,1)}, bf16[4,48,1536]{2,1,0:T(8,128)(2,1)}, u32[]{:S(2)}, u32[]{:S(2)}) %collective-permute-start.36) | collective-permute-done | bytes 589856 | tf_op jit(solution)/shard_map/ppermute | solution.py:38
  198.1 5.6 %project_rows.13 = (bf16[4096,384]{1,0:T(8,128)(2,1)}, bf16[4096,384]{1,0:T(8,128)(2,1)}, bf16[4096,384]{1,0:T(8,128)(2,1)}, bf16[4096,384]{1,0:T(8,128)(2,1)}) custom-call(bf16[1024,384]{1,0:T(8,128)(2,1)} %copy-done.18, bf16[1024,384]{1,0:T(8,128)(2,1)} %collective-permute-done.10.far, ...), custom_call_target="tpu_custom_call", output_to_operand_aliasing={{0}: (11, {}), {1}: (12, {}), {2}: (13, {}), {3}: (14, {})} | custom-call | flops 4529848320 | bytes 3932160 | tf_op jit(solution)/shard_map/project_rows/pallas_call | solution.py:145
  204.6 5.4 project_rows.14
  210.9 5.4 project_rows.15
  216.3 20.2 %query_side.1 = (bf16[512,384]{1,0:T(8,128)(2,1)}, bf16[512,384]{1,0:T(8,128)(2,1)}, f32[4,16,128]{2,1,0:T(8,128)}) custom-call(s32[4]{0:T(128)} %copy-done.72, s32[4]{0:T(128)} %and_select_fusion.16.first, s32[4]{0:T(128)} %get-tuple-element.293.last, s32[32]{0:T(128)} %get-tuple-element.187.inverse, bf16[4096,384]{1,0:T(8,128)(2,1)} %get-tuple-element.93.q_ref, ...), custom_call_target="tpu_custom_call" | custom-call | flops 19327352832 | bytes 12582912 | tf_op jit(solution)/shard_map/query_side/pallas_call | solution.py:410
  236.5 35.5 %all_gather.13.stat_ref = f32[32,16,128]{2,1,0:T(8,128)} all-gather(f32[4,16,128]{2,1,0:T(8,128)} %get-tuple-element.100), channel_id=1, replica_groups=mesh['fsdp'=2,'ctx'=8,'tp'=2] {'ctx'}, dimensions={0}, use_global_device_ids=true | all-gather | bytes 294912 | tf_op jit(solution)/shard_map/all_gather | solution.py:935
  272.0 3.6 outer_pair.3
  276.7 2.5 collective-permute-start.25
  279.2 17.8 %key_side.1 = (bf16[512,384]{1,0:T(8,128)(2,1)}, bf16[512,384]{1,0:T(8,128)(2,1)}) custom-call(s32[4]{0:T(128)} %copy-done.72, s32[4]{0:T(128)} %get-tuple-element.208.first, s32[4]{0:T(128)} %and_select_fusion.last, s32[32]{0:T(128)} %get-tuple-element.187.inverse, s32[32]{0:T(128)} %get-tuple-element.188.natural, ...), custom_call_target="tpu_custom_call" | custom-call | flops 19327352832 | bytes 12582912 | tf_op jit(solution)/shard_map/key_side/pallas_call | solution.py:534
  297.0 3.7 outer_pair.2
  303.5 3.8 collective-permute-start.26
  307.3 4.5 collective-permute-done.30
  312.0 1.9 collective-permute-start.31
  316.1 2.7 collective-permute-start.29
  320.6 2.7 collective-permute-start.34
  324.3 2.6 collective-permute-done.34
  329.3 3.3 collective-permute-start.38
  338.2 5.4 collective-permute-done.37
  343.6 8.9 %collective-permute-done.38 = bf16[48,3072]{1,0:T(8,128)(2,1)} collective-permute-done((bf16[48,3072]{1,0:T(8,128)(2,1)}, bf16[48,3072]{1,0:T(8,128)(2,1)}, u32[]{:S(2)}, u32[]{:S(2)}) %collective-permute-start.38) | collective-permute-done | bytes 294944 | tf_op jit(solution)/shard_map/ppermute | solution.py:38
  352.5 2.1 fusion.74
  359.6 5.7 %collective-permute-start.42 = (bf16[48,1536]{1,0:T(8,128)(2,1)S(1)}, bf16[48,1536]{1,0:T(8,128)(2,1)S(1)}, u32[]{:S(2)}, u32[]{:S(2)}) collective-permute-start(bf16[48,1536]{1,0:T(8,128)(2,1)S(1)} %get-tuple-element.259), channel_id=1, source_target_pairs={{12,0},{14,2},{0,12},{2,14},{13,1},{15,3},{1,13},{3,15},{28,16},{3... | collective-permute-start | bytes 442376 | tf_op jit(solution)/shard_map/ppermute | solution.py:54
  366.0 16.2 %collective-permute-done.40 = bf16[48,1536]{1,0:T(8,128)(2,1)S(1)} collective-permute-done((bf16[48,1536]{1,0:T(8,128)(2,1)}, bf16[48,1536]{1,0:T(8,128)(2,1)S(1)}, u32[]{:S(2)}, u32[]{:S(2)}) %collective-permute-start.40) | collective-permute-done | bytes 147488 | tf_op jit(solution)/shard_map/ppermute | solution.py:54
  383.2 1.9 collective-permute-start.43
  385.1 4.6 collective-permute-start.44
  408.3 2.2 constant_dynamic-update-slice_fusion.9
  410.5 1.9 collective-permute-start.46
  412.4 1.9 collective-permute-start.45
  416.7 3.8 collective-permute-done.61
  420.5 1.8 collective-permute-start.62
  423.2 7.4 %collective-permute-done.62 = f32[3840]{0:T(1024)S(1)} collective-permute-done((f32[3840]{0:T(1024)S(1)}, f32[3840]{0:T(1024)S(1)}, u32[]{:S(2)}, u32[]{:S(2)}) %collective-permute-start.62) | collective-permute-done | bytes 15392 | tf_op jit(solution)/shard_map/ppermute | solution.py:38
  439.0 2.4 collective-permute-start.47
  452.4 1.9 constant_dynamic-update-slice_fusion.2.near_a
  454.4 2.8 pad_maximum_fusion.2.far_a
  459.1 46.1 %orthogonal_rows.1 = bf16[192,1536]{1,0:T(8,128)(2,1)} custom-call(s32[1]{0:T(128)} %bitcast.50.high, bf16[768,1536]{1,0:T(8,128)(2,1)} %constant_dynamic-update-slice_fusion.2.near_a, bf16[768,1536]{1,0:T(8,128)(2,1)} %pad_maximum_fusion.2.far_a, bf16[768,1152]{1,0:T(8,128)(2,1)} %copy-done.70, bf16[768,1152]{1,0:T(8,128)(2,1)} %pad_maximum_fusion.3.far_b), custom_call_target="tpu_custom_call" | custom-call | flops 45298483200 | bytes 9437184 | tf_op jit(solution)/shard_map/orthogonal_rows/pallas_call | solution.py:641
  506.5 12.6 %collective-permute-start.57 = (bf16[48,1536]{1,0:T(8,128)(2,1)S(1)}, bf16[48,1536]{1,0:T(8,128)(2,1)S(1)}, u32[]{:S(2)}, u32[]{:S(2)}) collective-permute-start(bf16[48,1536]{1,0:T(8,128)(2,1)S(1)} %get-tuple-element.245), channel_id=1, source_target_pairs={{0,8},{2,10},{4,12},{6,14},{8,0},{10,2},{12,4},{14,6},{1,9},{3,11}... | collective-permute-start | bytes 442376 | tf_op jit(solution)/shard_map/ppermute | solution.py:38
  521.1 2.7 collective-permute-done.57
  523.8 7.3 %collective-permute-done.58 = bf16[48,1536]{1,0:T(8,128)(2,1)S(1)} collective-permute-done((bf16[48,1536]{1,0:T(8,128)(2,1)S(1)}, bf16[48,1536]{1,0:T(8,128)(2,1)S(1)}, u32[]{:S(2)}, u32[]{:S(2)}) %collective-permute-start.58) | collective-permute-done | bytes 147488 | tf_op jit(solution)/shard_map/ppermute | solution.py:38
  532.7 1.8 fusion.28
  542.1 2.2 convert_element_type.336
  544.3 1.8 fusion
  546.6 1.8 slice_add_fusion
  548.9 1.9 copy.111
  (399 shorter events, 130.1 us)
Async XLA Ops:
  7.2 117.0 %all-gather.4.cloned.1.call-start = ((), (), s32[]{:S(2)}) async-start(), calls=%async_computation | async-start | bytes 2654208 | tf_op jit(solution)/shard_map/all_gather | solution.py:760
  11.0 42.0 %collective-permute-start.17 = (bf16[1024,384]{1,0:T(8,128)(2,1)}, bf16[1024,384]{1,0:T(8,128)(2,1)}, u32[]{:S(2)}, u32[]{:S(2)}) collective-permute-start(bf16[1024,384]{1,0:T(8,128)(2,1)} %constant_dynamic-update-slice_fusion.near), channel_id=1, source_target_pairs={{0,1},{1,0},{2,3},{3,2},{4,5},{5,4},{6,7},{7,6},{8,9},{9,8},{10,11... | collective-permute-start | bytes 2359304 | tf_op jit(solution)/shard_map/ppermute | solution.py:38
  11.4 43.0 %collective-permute-start = (bf16[1024,384]{1,0:T(8,128)(2,1)}, bf16[1024,384]{1,0:T(8,128)(2,1)}, u32[]{:S(2)}, u32[]{:S(2)}) collective-permute-start(bf16[1024,384]{1,0:T(8,128)(2,1)} %constant_dynamic-update-slice_fusion.near), channel_id=1, source_target_pairs={{0,4},{2,6},{4,0},{6,2},{8,12},{10,14},{12,8},{14,10},{1,5},{3,7},... | collective-permute-start | bytes 2359304 | tf_op jit(solution)/shard_map/ppermute | solution.py:728
  14.0 67.1 %collective-permute-start.14 = (bf16[1024,384]{1,0:T(8,128)(2,1)}, bf16[1024,384]{1,0:T(8,128)(2,1)}, u32[]{:S(2)}, u32[]{:S(2)}) collective-permute-start(bf16[1024,384]{1,0:T(8,128)(2,1)} %constant_dynamic-update-slice_fusion.near), channel_id=1, source_target_pairs={{0,2},{2,0},{4,6},{6,4},{8,10},{10,8},{12,14},{14,12},{1,3},{3,1},... | collective-permute-start | bytes 2359304 | tf_op jit(solution)/shard_map/ppermute | solution.py:38
  15.5 67.1 %collective-permute-start.6 = (bf16[1024,384]{1,0:T(8,128)(2,1)}, bf16[1024,384]{1,0:T(8,128)(2,1)}, u32[]{:S(2)}, u32[]{:S(2)}) collective-permute-start(bf16[1024,384]{1,0:T(8,128)(2,1)} %constant_dynamic-update-slice_fusion.near), channel_id=1, source_target_pairs={{4,8},{6,10},{8,4},{10,6},{5,9},{7,11},{9,5},{11,7},{20,24},{22,26... | collective-permute-start | bytes 2359304 | tf_op jit(solution)/shard_map/ppermute | solution.py:728
  17.2 32.6 %collective-permute-start.5 = (bf16[384,384]{1,0:T(8,128)(2,1)S(1)}, bf16[384,384]{1,0:T(8,128)(2,1)}, u32[]{:S(2)}, u32[]{:S(2)}) collective-permute-start(bf16[384,384]{1,0:T(8,128)(2,1)S(1)} %convert_element_type.265), channel_id=1, source_target_pairs={{0,16},{16,0},{1,17},{17,1},{2,18},{18,2},{3,19},{19,3},{4,20},{20... | collective-permute-start | bytes 884744 | tf_op jit(solution)/shard_map/ppermute | solution.py:38
  19.8 514.8 %all-gather.6.cloned.1.call-start = ((), (), s32[]{:S(2)}) async-start(), calls=%async_computation.1 | async-start | bytes 1327104 | tf_op jit(solution)/shard_map/all_gather | solution.py:867
  49.8 28.9 %collective-permute-start.18 = (bf16[384,1536]{1,0:T(8,128)(2,1)S(1)}, bf16[384,1536]{1,0:T(8,128)(2,1)S(1)}, u32[]{:S(2)}, u32[]{:S(2)}) collective-permute-start(bf16[384,1536]{1,0:T(8,128)(2,1)S(1)} %copy-done.35), channel_id=1, source_target_pairs={{0,16},{16,0},{1,17},{17,1},{2,18},{18,2},{3,19},{19,3},{4,20},{20... | collective-permute-start | bytes 3538952 | tf_op jit(solution)/shard_map/ppermute | solution.py:38
  52.9 49.7 %collective-permute-start.19 = (bf16[1536,384]{1,0:T(8,128)(2,1)S(1)}, bf16[1536,384]{1,0:T(8,128)(2,1)S(1)}, u32[]{:S(2)}, u32[]{:S(2)}) collective-permute-start(bf16[1536,384]{1,0:T(8,128)(2,1)S(1)} %copy-done.34), channel_id=1, source_target_pairs={{0,16},{16,0},{1,17},{17,1},{2,18},{18,2},{3,19},{19,3},{4,20},{20... | collective-permute-start | bytes 3538952 | tf_op jit(solution)/shard_map/ppermute | solution.py:38
  54.4 78.2 %collective-permute-start.16 = (bf16[1024,384]{1,0:T(8,128)(2,1)}, bf16[1024,384]{1,0:T(8,128)(2,1)}, u32[]{:S(2)}, u32[]{:S(2)}) collective-permute-start(bf16[1024,384]{1,0:T(8,128)(2,1)} %collective-permute-done.near), channel_id=1, source_target_pairs={{0,1},{1,0},{2,3},{3,2},{4,5},{5,4},{6,7},{7,6},{8,9},{9,8},{10,11... | collective-permute-start | bytes 2359304 | tf_op jit(solution)/shard_map/ppermute | solution.py:38
  78.7 68.1 %collective-permute-start.11 = (bf16[1024,384]{1,0:T(8,128)(2,1)}, bf16[1024,384]{1,0:T(8,128)(2,1)S(1)}, u32[]{:S(2)}, u32[]{:S(2)}) collective-permute-start(bf16[1024,384]{1,0:T(8,128)(2,1)} %collective-permute-done.near), channel_id=1, source_target_pairs={{0,2},{2,0},{4,6},{6,4},{8,10},{10,8},{12,14},{14,12},{1,3},{3,1},... | collective-permute-start | bytes 2359304 | tf_op jit(solution)/shard_map/ppermute | solution.py:38
  81.0 53.1 %collective-permute-start.1 = (bf16[1024,384]{1,0:T(8,128)(2,1)}, bf16[1024,384]{1,0:T(8,128)(2,1)}, u32[]{:S(2)}, u32[]{:S(2)}) collective-permute-start(bf16[1024,384]{1,0:T(8,128)(2,1)} %collective-permute-done.near), channel_id=1, source_target_pairs={{4,8},{6,10},{8,4},{10,6},{5,9},{7,11},{9,5},{11,7},{20,24},{22,26... | collective-permute-start | bytes 2359304 | tf_op jit(solution)/shard_map/ppermute | solution.py:728
  82.6 58.7 %collective-permute-start.15 = (bf16[1024,384]{1,0:T(8,128)(2,1)}, bf16[1024,384]{1,0:T(8,128)(2,1)}, u32[]{:S(2)}, u32[]{:S(2)}) collective-permute-start(bf16[1024,384]{1,0:T(8,128)(2,1)} %collective-permute-done.14.near), channel_id=1, source_target_pairs={{0,1},{1,0},{2,3},{3,2},{4,5},{5,4},{6,7},{7,6},{8,9},{9,8},{10,11... | collective-permute-start | bytes 2359304 | tf_op jit(solution)/shard_map/ppermute | solution.py:38
  102.6 20.9 %collective-permute-start.7 = (bf16[1024,384]{1,0:T(8,128)(2,1)}, bf16[1024,384]{1,0:T(8,128)(2,1)S(1)}, u32[]{:S(2)}, u32[]{:S(2)}) collective-permute-start(bf16[1024,384]{1,0:T(8,128)(2,1)} %collective-permute-done.6), channel_id=1, source_target_pairs={{4,0},{6,2},{8,12},{10,14},{5,1},{7,3},{9,13},{11,15},{20,16},{22,... | collective-permute-start | bytes 2359304 | tf_op jit(solution)/shard_map/ppermute | solution.py:728
  123.5 30.7 %collective-permute-start.22 = (bf16[384,1536]{1,0:T(8,128)(2,1)}, bf16[384,1536]{1,0:T(8,128)(2,1)}, u32[]{:S(2)}, u32[]{:S(2)}) collective-permute-start(bf16[384,1536]{1,0:T(8,128)(2,1)} %dynamic-slice_bitcast_fusion), channel_id=1, source_target_pairs={{0,16},{16,0},{1,17},{17,1},{2,18},{18,2},{3,19},{19,3},{4,20},{20... | collective-permute-start | bytes 3538952 | tf_op jit(solution)/shard_map/ppermute | solution.py:38
  132.7 42.0 %collective-permute-start.21 = (bf16[384,1536]{1,0:T(8,128)(2,1)}, bf16[384,1536]{1,0:T(8,128)(2,1)S(1)}, u32[]{:S(2)}, u32[]{:S(2)}) collective-permute-start(bf16[384,1536]{1,0:T(8,128)(2,1)} %dynamic-slice_bitcast_fusion.1), channel_id=1, source_target_pairs={{0,16},{16,0},{1,17},{17,1},{2,18},{18,2},{3,19},{19,3},{4,20},{20... | collective-permute-start | bytes 3538952 | tf_op jit(solution)/shard_map/ppermute | solution.py:38
  134.2 20.0 %collective-permute-start.2 = (bf16[1024,384]{1,0:T(8,128)(2,1)}, bf16[1024,384]{1,0:T(8,128)(2,1)S(1)}, u32[]{:S(2)}, u32[]{:S(2)}) collective-permute-start(bf16[1024,384]{1,0:T(8,128)(2,1)} %collective-permute-done.1), channel_id=1, source_target_pairs={{4,0},{6,2},{8,12},{10,14},{5,1},{7,3},{9,13},{11,15},{20,16},{22,... | collective-permute-start | bytes 2359304 | tf_op jit(solution)/shard_map/ppermute | solution.py:728
  141.3 16.1 %collective-permute-start.13 = (bf16[1024,384]{1,0:T(8,128)(2,1)S(1)}, bf16[1024,384]{1,0:T(8,128)(2,1)}, u32[]{:S(2)}, u32[]{:S(2)}) collective-permute-start(bf16[1024,384]{1,0:T(8,128)(2,1)S(1)} %broadcast_select_fusion.6.near), channel_id=1, source_target_pairs={{0,1},{1,0},{2,3},{3,2},{4,5},{5,4},{6,7},{7,6},{8,9},{9,8},{10,11... | collective-permute-start | bytes 2359304 | tf_op jit(solution)/shard_map/ppermute | solution.py:38
  146.8 32.6 %collective-permute-start.8 = (bf16[1024,384]{1,0:T(8,128)(2,1)S(1)}, bf16[1024,384]{1,0:T(8,128)(2,1)}, u32[]{:S(2)}, u32[]{:S(2)}) collective-permute-start(bf16[1024,384]{1,0:T(8,128)(2,1)S(1)} %broadcast_select_fusion.6.near), channel_id=1, source_target_pairs={{0,2},{2,0},{4,6},{6,4},{8,10},{10,8},{12,14},{14,12},{1,3},{3,1},... | collective-permute-start | bytes 2359304 | tf_op jit(solution)/shard_map/ppermute | solution.py:38
  154.1 23.7 %collective-permute-start.12 = (bf16[1024,384]{1,0:T(8,128)(2,1)S(1)}, bf16[1024,384]{1,0:T(8,128)(2,1)}, u32[]{:S(2)}, u32[]{:S(2)}) collective-permute-start(bf16[1024,384]{1,0:T(8,128)(2,1)S(1)} %collective-permute-done.11.near), channel_id=1, source_target_pairs={{0,1},{1,0},{2,3},{3,2},{4,5},{5,4},{6,7},{7,6},{8,9},{9,8},{10,11... | collective-permute-start | bytes 2359304 | tf_op jit(solution)/shard_map/ppermute | solution.py:38
  154.2 43.8 %collective-permute-start.10 = (bf16[1024,384]{1,0:T(8,128)(2,1)S(1)}, bf16[1024,384]{1,0:T(8,128)(2,1)}, u32[]{:S(2)}, u32[]{:S(2)}) collective-permute-start(bf16[1024,384]{1,0:T(8,128)(2,1)S(1)} %broadcast_select_fusion.7.near), channel_id=1, source_target_pairs={{0,1},{1,0},{2,3},{3,2},{4,5},{5,4},{6,7},{7,6},{8,9},{9,8},{10,11... | collective-permute-start | bytes 2359304 | tf_op jit(solution)/shard_map/ppermute | solution.py:38
  157.4 40.6 %collective-permute-start.3 = (bf16[1024,384]{1,0:T(8,128)(2,1)S(1)}, bf16[1024,384]{1,0:T(8,128)(2,1)}, u32[]{:S(2)}, u32[]{:S(2)}) collective-permute-start(bf16[1024,384]{1,0:T(8,128)(2,1)S(1)} %broadcast_select_fusion.7.near), channel_id=1, source_target_pairs={{0,2},{2,0},{4,6},{6,4},{8,10},{10,8},{12,14},{14,12},{1,3},{3,1},... | collective-permute-start | bytes 2359304 | tf_op jit(solution)/shard_map/ppermute | solution.py:38
  174.7 22.1 %collective-permute-start.36 = (bf16[4,48,1536]{2,1,0:T(8,128)(2,1)}, bf16[4,48,1536]{2,1,0:T(8,128)(2,1)}, u32[]{:S(2)}, u32[]{:S(2)}) collective-permute-start(bf16[4,48,1536]{2,1,0:T(8,128)(2,1)} %fusion.5), channel_id=1, source_target_pairs={{0,2},{2,0},{4,6},{6,4},{8,10},{10,8},{12,14},{14,12},{1,3},{3,1},... | collective-permute-start | bytes 1769480 | tf_op jit(solution)/shard_map/ppermute | solution.py:38
  177.8 124.1 %collective-permute-start.35 = (bf16[4,48,1536]{2,1,0:T(8,128)(2,1)}, bf16[4,48,1536]{2,1,0:T(8,128)(2,1)}, u32[]{:S(2)}, u32[]{:S(2)}) collective-permute-start(bf16[4,48,1536]{2,1,0:T(8,128)(2,1)} %fusion.4), channel_id=1, source_target_pairs={{0,2},{2,0},{4,6},{6,4},{8,10},{10,8},{12,14},{14,12},{1,3},{3,1},... | collective-permute-start | bytes 1769480 | tf_op jit(solution)/shard_map/ppermute | solution.py:38
  179.4 24.3 %collective-permute-start.9 = (bf16[1024,384]{1,0:T(8,128)(2,1)}, bf16[1024,384]{1,0:T(8,128)(2,1)S(1)}, u32[]{:S(2)}, u32[]{:S(2)}) collective-permute-start(bf16[1024,384]{1,0:T(8,128)(2,1)} %collective-permute-done.8.near), channel_id=1, source_target_pairs={{0,1},{1,0},{2,3},{3,2},{4,5},{5,4},{6,7},{7,6},{8,9},{9,8},{10,11... | collective-permute-start | bytes 2359304 | tf_op jit(solution)/shard_map/ppermute | solution.py:38
  198.0 12.0 %collective-permute-start.4 = (bf16[1024,384]{1,0:T(8,128)(2,1)}, bf16[1024,384]{1,0:T(8,128)(2,1)S(1)}, u32[]{:S(2)}, u32[]{:S(2)}) collective-permute-start(bf16[1024,384]{1,0:T(8,128)(2,1)} %collective-permute-done.3.near), channel_id=1, source_target_pairs={{0,1},{1,0},{2,3},{3,2},{4,5},{5,4},{6,7},{7,6},{8,9},{9,8},{10,11... | collective-permute-start | bytes 2359304 | tf_op jit(solution)/shard_map/ppermute | solution.py:38
  276.7 26.6 %collective-permute-start.25 = (bf16[384,768]{1,0:T(8,128)(2,1)S(1)}, bf16[384,768]{1,0:T(8,128)(2,1)S(1)}, u32[]{:S(2)}, u32[]{:S(2)}) collective-permute-start(bf16[384,768]{1,0:T(8,128)(2,1)S(1)} %dynamic-slice_bitcast_fusion.3), channel_id=1, source_target_pairs={{0,16},{16,0},{1,17},{17,1},{2,18},{18,2},{3,19},{19,3},{4,20},{20... | collective-permute-start | bytes 1769480 | tf_op jit(solution)/shard_map/ppermute | solution.py:38
  301.9 9.9 %collective-permute-start.30 = (bf16[384,768]{1,0:T(8,128)(2,1)S(1)}, bf16[384,768]{1,0:T(8,128)(2,1)S(1)}, u32[]{:S(2)}, u32[]{:S(2)}) collective-permute-start(bf16[384,768]{1,0:T(8,128)(2,1)S(1)} %dynamic-slice_bitcast_fusion.2), channel_id=1, source_target_pairs={{0,16},{16,0},{1,17},{17,1},{2,18},{18,2},{3,19},{19,3},{4,20},{20... | collective-permute-start | bytes 1769480 | tf_op jit(solution)/shard_map/ppermute | solution.py:38
  303.5 10.8 %collective-permute-start.26 = (bf16[4,48,768]{2,1,0:T(8,128)(2,1)S(1)}, bf16[4,48,768]{2,1,0:T(8,128)(2,1)S(1)}, u32[]{:S(2)}, u32[]{:S(2)}) collective-permute-start(bf16[4,48,768]{2,1,0:T(8,128)(2,1)S(1)} %fusion.24), channel_id=1, source_target_pairs={{0,2},{2,0},{4,6},{6,4},{8,10},{10,8},{12,14},{14,12},{1,3},{3,1},... | collective-permute-start | bytes 884744 | tf_op jit(solution)/shard_map/ppermute | solution.py:38
  312.0 6.8 %collective-permute-start.31 = (bf16[4,48,768]{2,1,0:T(8,128)(2,1)S(1)}, bf16[4,48,768]{2,1,0:T(8,128)(2,1)S(1)}, u32[]{:S(2)}, u32[]{:S(2)}) collective-permute-start(bf16[4,48,768]{2,1,0:T(8,128)(2,1)S(1)} %fusion.25), channel_id=1, source_target_pairs={{0,2},{2,0},{4,6},{6,4},{8,10},{10,8},{12,14},{14,12},{1,3},{3,1},... | collective-permute-start | bytes 884744 | tf_op jit(solution)/shard_map/ppermute | solution.py:38
  314.3 6.3 %collective-permute-start.27 = (bf16[48,768]{1,0:T(8,128)(2,1)S(1)}, bf16[48,768]{1,0:T(8,128)(2,1)S(1)}, u32[]{:S(2)}, u32[]{:S(2)}) collective-permute-start(bf16[48,768]{1,0:T(8,128)(2,1)S(1)} %get-tuple-element.252), channel_id=1, source_target_pairs={{0,4},{2,6},{4,0},{6,2},{8,12},{10,14},{12,8},{14,10},{1,5},{3,7},... | collective-permute-start | bytes 221192 | tf_op jit(solution)/shard_map/ppermute | solution.py:38
  314.4 8.9 %collective-permute-start.28 = (bf16[48,768]{1,0:T(8,128)(2,1)S(1)}, bf16[48,768]{1,0:T(8,128)(2,1)S(1)}, u32[]{:S(2)}, u32[]{:S(2)}) collective-permute-start(bf16[48,768]{1,0:T(8,128)(2,1)S(1)} %get-tuple-element.254), channel_id=1, source_target_pairs={{0,8},{2,10},{4,12},{6,14},{8,0},{10,2},{12,4},{14,6},{1,9},{3,11}... | collective-permute-start | bytes 221192 | tf_op jit(solution)/shard_map/ppermute | solution.py:38
  316.1 7.3 %collective-permute-start.29 = (bf16[48,768]{1,0:T(8,128)(2,1)S(1)}, bf16[48,768]{1,0:T(8,128)(2,1)S(1)}, u32[]{:S(2)}, u32[]{:S(2)}) collective-permute-start(bf16[48,768]{1,0:T(8,128)(2,1)S(1)} %get-tuple-element.253), channel_id=1, source_target_pairs={{0,12},{2,14},{4,8},{6,10},{8,4},{10,6},{12,0},{14,2},{1,13},{3,15... | collective-permute-start | bytes 221192 | tf_op jit(solution)/shard_map/ppermute | solution.py:38
  318.9 4.6 collective-permute-start.32
  319.0 5.3 collective-permute-start.33
  320.6 6.2 %collective-permute-start.34 = (bf16[48,768]{1,0:T(8,128)(2,1)S(1)}, bf16[48,768]{1,0:T(8,128)(2,1)S(1)}, u32[]{:S(2)}, u32[]{:S(2)}) collective-permute-start(bf16[48,768]{1,0:T(8,128)(2,1)S(1)} %get-tuple-element.250), channel_id=1, source_target_pairs={{0,12},{2,14},{4,8},{6,10},{8,4},{10,6},{12,0},{14,2},{1,13},{3,15... | collective-permute-start | bytes 221192 | tf_op jit(solution)/shard_map/ppermute | solution.py:38
  328.3 213.8 %all-gather.8.cloned.1.call-start = ((), (), s32[]{:S(2)}) async-start(), calls=%async_computation.2 | async-start | bytes 2654208 | tf_op jit(solution)/shard_map/all_gather | solution.py:867
  329.3 14.3 %collective-permute-start.37 = (bf16[48,3072]{1,0:T(8,128)(2,1)}, bf16[48,3072]{1,0:T(8,128)(2,1)}, u32[]{:S(2)}, u32[]{:S(2)}) collective-permute-start(bf16[48,3072]{1,0:T(8,128)(2,1)} %get-tuple-element.213), channel_id=1, source_target_pairs={{0,4},{2,6},{4,0},{6,2},{8,12},{10,14},{12,8},{14,10},{1,5},{3,7},... | collective-permute-start | bytes 884744 | tf_op jit(solution)/shard_map/ppermute | solution.py:38
  329.3 23.2 %collective-permute-start.38 = (bf16[48,3072]{1,0:T(8,128)(2,1)}, bf16[48,3072]{1,0:T(8,128)(2,1)}, u32[]{:S(2)}, u32[]{:S(2)}) collective-permute-start(bf16[48,3072]{1,0:T(8,128)(2,1)} %get-tuple-element.214), channel_id=1, source_target_pairs={{0,8},{2,10},{4,12},{6,14},{8,0},{10,2},{12,4},{14,6},{1,9},{3,11}... | collective-permute-start | bytes 884744 | tf_op jit(solution)/shard_map/ppermute | solution.py:38
  332.6 19.9 %collective-permute-start.39 = (bf16[48,3072]{1,0:T(8,128)(2,1)}, bf16[48,3072]{1,0:T(8,128)(2,1)}, u32[]{:S(2)}, u32[]{:S(2)}) collective-permute-start(bf16[48,3072]{1,0:T(8,128)(2,1)} %get-tuple-element.215), channel_id=1, source_target_pairs={{0,12},{2,14},{4,8},{6,10},{8,4},{10,6},{12,0},{14,2},{1,13},{3,15... | collective-permute-start | bytes 884744 | tf_op jit(solution)/shard_map/ppermute | solution.py:38
  357.0 25.1 %collective-permute-start.40 = (bf16[48,1536]{1,0:T(8,128)(2,1)}, bf16[48,1536]{1,0:T(8,128)(2,1)S(1)}, u32[]{:S(2)}, u32[]{:S(2)}) collective-permute-start(bf16[48,1536]{1,0:T(8,128)(2,1)} %get-tuple-element.261), channel_id=1, source_target_pairs={{4,0},{6,2},{8,12},{10,14},{5,1},{7,3},{9,13},{11,15},{20,16},{22,... | collective-permute-start | bytes 442376 | tf_op jit(solution)/shard_map/ppermute | solution.py:54
  358.3 23.9 %collective-permute-start.41 = (bf16[48,1536]{1,0:T(8,128)(2,1)}, bf16[48,1536]{1,0:T(8,128)(2,1)S(1)}, u32[]{:S(2)}, u32[]{:S(2)}) collective-permute-start(bf16[48,1536]{1,0:T(8,128)(2,1)} %get-tuple-element.260), channel_id=1, source_target_pairs={{8,0},{10,2},{4,12},{6,14},{9,1},{11,3},{5,13},{7,15},{24,16},{26,... | collective-permute-start | bytes 442376 | tf_op jit(solution)/shard_map/ppermute | solution.py:54
  359.6 22.6 %collective-permute-start.42 = (bf16[48,1536]{1,0:T(8,128)(2,1)S(1)}, bf16[48,1536]{1,0:T(8,128)(2,1)S(1)}, u32[]{:S(2)}, u32[]{:S(2)}) collective-permute-start(bf16[48,1536]{1,0:T(8,128)(2,1)S(1)} %get-tuple-element.259), channel_id=1, source_target_pairs={{12,0},{14,2},{0,12},{2,14},{13,1},{15,3},{1,13},{3,15},{28,16},{3... | collective-permute-start | bytes 442376 | tf_op jit(solution)/shard_map/ppermute | solution.py:54
  383.2 25.1 %collective-permute-start.43 = (bf16[192,1536]{1,0:T(8,128)(2,1)}, bf16[192,1536]{1,0:T(8,128)(2,1)}, u32[]{:S(2)}, u32[]{:S(2)}) collective-permute-start(bf16[192,1536]{1,0:T(8,128)(2,1)} %pad_maximum_fusion.8), channel_id=1, source_target_pairs={{2,0},{0,2},{14,12},{12,14},{3,1},{1,3},{15,13},{13,15},{18,16},{1... | collective-permute-start | bytes 1769480 | tf_op jit(solution)/shard_map/ppermute | solution.py:54
  385.1 30.7 %collective-permute-start.44 = (bf16[192,1536]{1,0:T(8,128)(2,1)}, bf16[192,1536]{1,0:T(8,128)(2,1)S(1)}, u32[]{:S(2)}, u32[]{:S(2)}) collective-permute-start(bf16[192,1536]{1,0:T(8,128)(2,1)} %pad_maximum_fusion.8), channel_id=1, source_target_pairs={{16,0},{18,2},{28,12},{30,14},{0,16},{2,18},{12,28},{14,30},{17,1}... | collective-permute-start | bytes 1769480 | tf_op jit(solution)/shard_map/ppermute | solution.py:54
  398.4 3.0 collective-permute-start.23
  404.5 3.8 collective-permute-start.59
  406.9 15.4 %collective-permute-start.20 = (bf16[512,384]{1,0:T(8,128)(2,1)S(1)}, bf16[512,384]{1,0:T(8,128)(2,1)S(1)}, u32[]{:S(2)}, u32[]{:S(2)}) collective-permute-start(bf16[512,384]{1,0:T(8,128)(2,1)S(1)} %select_convert_fusion.1), channel_id=1, source_target_pairs={{0,1},{1,0},{2,3},{3,2},{4,5},{5,4},{6,7},{7,6},{8,9},{9,8},{10,11... | collective-permute-start | bytes 1179656 | tf_op jit(solution)/shard_map/ppermute | solution.py:38
  408.3 6.0 %collective-permute-start.60 = (f32[3840]{0:T(1024)S(1)}, f32[3840]{0:T(1024)S(1)}, u32[]{:S(2)}, u32[]{:S(2)}) collective-permute-start(f32[3840]{0:T(1024)S(1)} %add.451), channel_id=1, source_target_pairs={{0,4},{2,6},{4,0},{6,2},{8,12},{10,14},{12,8},{14,10},{1,5},{3,7},... | collective-permute-start | bytes 46088 | tf_op jit(solution)/shard_map/ppermute | solution.py:38
  410.5 43.9 %collective-permute-start.46 = (bf16[384,1536]{1,0:T(8,128)(2,1)}, bf16[384,1536]{1,0:T(8,128)(2,1)}, u32[]{:S(2)}, u32[]{:S(2)}) collective-permute-start(bf16[384,1536]{1,0:T(8,128)(2,1)} %get-tuple-element.247), channel_id=1, source_target_pairs={{1,0},{0,1},{3,2},{2,3},{13,12},{12,13},{15,14},{14,15},{17,16},{1... | collective-permute-start | bytes 3538952 | tf_op jit(solution)/shard_map/ppermute | solution.py:54
  412.4 25.4 %collective-permute-start.45 = (bf16[192,1536]{1,0:T(8,128)(2,1)}, bf16[192,1536]{1,0:T(8,128)(2,1)}, u32[]{:S(2)}, u32[]{:S(2)}) collective-permute-start(bf16[192,1536]{1,0:T(8,128)(2,1)} %collective-permute-done.43), channel_id=1, source_target_pairs={{16,0},{18,2},{28,12},{30,14},{0,16},{2,18},{12,28},{14,30},{17,1}... | collective-permute-start | bytes 1769480 | tf_op jit(solution)/shard_map/ppermute | solution.py:54
  414.4 6.1 %collective-permute-start.61 = (f32[3840]{0:T(1024)S(1)}, f32[3840]{0:T(1024)S(1)}, u32[]{:S(2)}, u32[]{:S(2)}) collective-permute-start(f32[3840]{0:T(1024)S(1)} %add.452), channel_id=1, source_target_pairs={{0,8},{2,10},{4,12},{6,14},{8,0},{10,2},{12,4},{14,6},{1,9},{3,11}... | collective-permute-start | bytes 46088 | tf_op jit(solution)/shard_map/ppermute | solution.py:38
  420.5 10.1 %collective-permute-start.62 = (f32[3840]{0:T(1024)S(1)}, f32[3840]{0:T(1024)S(1)}, u32[]{:S(2)}, u32[]{:S(2)}) collective-permute-start(f32[3840]{0:T(1024)S(1)} %add.453), channel_id=1, source_target_pairs={{0,16},{16,0},{1,17},{17,1},{2,18},{18,2},{3,19},{19,3},{4,20},{20... | collective-permute-start | bytes 46088 | tf_op jit(solution)/shard_map/ppermute | solution.py:38
  433.1 4.0 collective-permute-start.63
  439.0 15.4 %collective-permute-start.47 = (bf16[384,1536]{1,0:T(8,128)(2,1)S(1)}, bf16[384,1536]{1,0:T(8,128)(2,1)S(1)}, u32[]{:S(2)}, u32[]{:S(2)}) collective-permute-start(bf16[384,1536]{1,0:T(8,128)(2,1)S(1)} %pad_maximum_fusion.4), channel_id=1, source_target_pairs={{1,0},{0,1},{3,2},{2,3},{13,12},{12,13},{15,14},{14,15},{17,16},{1... | collective-permute-start | bytes 3538952 | tf_op jit(solution)/shard_map/ppermute | solution.py:54
  441.6 4.7 collective-permute-start.48
  442.9 5.1 collective-permute-start.49
  444.2 3.8 collective-permute-start.50
  448.8 2.8 collective-permute-start.52
  450.9 6.4 %collective-permute-start.54 = (bf16[384,1152]{1,0:T(8,128)(2,1)S(1)}, bf16[384,1152]{1,0:T(8,128)(2,1)S(1)}, u32[]{:S(2)}, u32[]{:S(2)}) collective-permute-start(bf16[384,1152]{1,0:T(8,128)(2,1)S(1)} %get-tuple-element.255), channel_id=1, source_target_pairs={{5,4},{4,5},{7,6},{6,7},{9,8},{8,9},{11,10},{10,11},{21,20},{20,21... | collective-permute-start | bytes 2654216 | tf_op jit(solution)/shard_map/ppermute | solution.py:54
  451.7 5.6 %collective-permute-start.55 = (bf16[384,1152]{1,0:T(8,128)(2,1)S(1)}, bf16[384,1152]{1,0:T(8,128)(2,1)S(1)}, u32[]{:S(2)}, u32[]{:S(2)}) collective-permute-start(bf16[384,1152]{1,0:T(8,128)(2,1)S(1)} %pad_maximum_fusion.5), channel_id=1, source_target_pairs={{5,4},{4,5},{7,6},{6,7},{9,8},{8,9},{11,10},{10,11},{21,20},{20,21... | collective-permute-start | bytes 2654216 | tf_op jit(solution)/shard_map/ppermute | solution.py:54
  506.4 14.7 %collective-permute-start.56 = (bf16[48,1536]{1,0:T(8,128)(2,1)S(1)}, bf16[48,1536]{1,0:T(8,128)(2,1)S(1)}, u32[]{:S(2)}, u32[]{:S(2)}) collective-permute-start(bf16[48,1536]{1,0:T(8,128)(2,1)S(1)} %get-tuple-element.246), channel_id=1, source_target_pairs={{0,4},{2,6},{4,0},{6,2},{8,12},{10,14},{12,8},{14,10},{1,5},{3,7},... | collective-permute-start | bytes 442376 | tf_op jit(solution)/shard_map/ppermute | solution.py:38
  506.5 17.3 %collective-permute-start.57 = (bf16[48,1536]{1,0:T(8,128)(2,1)S(1)}, bf16[48,1536]{1,0:T(8,128)(2,1)S(1)}, u32[]{:S(2)}, u32[]{:S(2)}) collective-permute-start(bf16[48,1536]{1,0:T(8,128)(2,1)S(1)} %get-tuple-element.245), channel_id=1, source_target_pairs={{0,8},{2,10},{4,12},{6,14},{8,0},{10,2},{12,4},{14,6},{1,9},{3,11}... | collective-permute-start | bytes 442376 | tf_op jit(solution)/shard_map/ppermute | solution.py:38
  519.1 12.0 %collective-permute-start.58 = (bf16[48,1536]{1,0:T(8,128)(2,1)S(1)}, bf16[48,1536]{1,0:T(8,128)(2,1)S(1)}, u32[]{:S(2)}, u32[]{:S(2)}) collective-permute-start(bf16[48,1536]{1,0:T(8,128)(2,1)S(1)} %get-tuple-element.244), channel_id=1, source_target_pairs={{0,12},{2,14},{4,8},{6,10},{8,4},{10,6},{12,0},{14,2},{1,13},{3,15... | collective-permute-start | bytes 442376 | tf_op jit(solution)/shard_map/ppermute | solution.py:38
  (77 other events, 772.1 us)
Sparse Core Ops, SparseCore 0:
  19.9 28.6 all-gather.3
  328.4 54.9 all-gather.5
  385.5 52.5 all-gather.7

commit v4 on v3

--- a/solution.py
+++ b/solution.py
@@ -63,16 +63,6 @@
     return total
 
 
-def gather_axis(shard, axis, dim):
-    if lax.axis_size(axis) != 2:
-        return lax.all_gather(shard, axis, axis=dim, tiled=True)
-    other = partner(shard, axis, 1)
-    first = lax.axis_index(axis) == 0
-    return jnp.concatenate(
-        [jnp.where(first, shard, other), jnp.where(first, other, shard)], axis=dim
-    )
-
-
 def sum_everywhere(value, axes):
     for axis in axes:
         step = 1
@@ -102,12 +92,11 @@
 
 
 def project_kernel(
-    near, far, w_near, w_far, a_near, a_far, bias, vec_near, vec_far, cos_ref, sin_ref, *outs
+    near, far, w_near, w_far, bias, vec_near, vec_far, cos_ref, sin_ref, *outs
 ):
-    outs = outs[-4:]
     rows, half = outs[0].shape
     width = 2 * half
-    own, other = near[:rows].astype(WIDE), far[:rows].astype(WIDE)
+    own, other = near[...].astype(WIDE), far[...].astype(WIDE)
     mean = (
         jnp.sum(own, axis=1, keepdims=True) + jnp.sum(other, axis=1, keepdims=True)
     ) / width
@@ -120,51 +109,49 @@
     other = (other * inv_std * vec_far[0:1] + vec_far[1:2]).astype(LOW)
     lane = lax.broadcasted_iota(jnp.int32, (rows, BLK), 1)
     cosine, sine = cos_ref[...], sin_ref[...]
-    for part, out in enumerate(outs[:3]):
-        made = dot_nn(own, w_near[part]) + dot_nn(other, w_far[part]) + bias[part : part + 1]
+    for part, out in enumerate(outs):
+        span = slice(part * half, (part + 1) * half)
+        made = dot_nn(own, w_near[span]) + dot_nn(other, w_far[span]) + bias[part : part + 1]
         for pair in range(half // BLK):
             lanes = slice(pair * BLK, (pair + 1) * BLK)
             block = made[:, lanes]
             if part < 2:
                 block = turned(block, cosine, sine, lane)
             out[:, lanes] = block.astype(LOW)
-    outs[3][...] = (dot_nt(near[rows:], a_near[...]) + dot_nt(far[rows:], a_far[...])).astype(LOW)
-
-
-def project_rows(place, count, near, far, weights, cosine, sine, made, after):
-    rows, half = near.shape[0] // 2, near.shape[1]
+
+
+def project_rows(near, far, weights, cosine, sine):
+    rows, half = near.shape
 
     def fixed(array):
         return pl.BlockSpec(array.shape, lambda i: (0,) * array.ndim)
 
-    def placed(width):
-        return pl.BlockSpec((rows, width), lambda i: (place, 0))
-
-    extra = tuple(made) + tuple(after)
-    before = 4 + len(weights)
+    def chunk(width):
+        return pl.BlockSpec((CHUNK, width), lambda i: (i, 0))
+
     return pl.pallas_call(
         project_kernel,
-        grid=(1,),
-        in_specs=[fixed(near), fixed(far)]
-        + [fixed(w) for w in weights]
-        + [placed(BLK)] * 2
-        + [pl.BlockSpec(memory_space=pl.ANY)] * len(extra),
-        out_specs=[placed(half)] * 4,
-        out_shape=[jax.ShapeDtypeStruct((count * rows, half), LOW)] * 4,
-        input_output_aliases={before + i: i for i in range(len(made))},
+        grid=(rows // CHUNK,),
+        in_specs=[chunk(half)] * 2 + [fixed(w) for w in weights] + [chunk(BLK)] * 2,
+        out_specs=[chunk(half)] * 3,
+        out_shape=[jax.ShapeDtypeStruct((rows, half), LOW)] * 3,
         compiler_params=pltpu.CompilerParams(vmem_limit_bytes=VMEM_ASK),
         cost_estimate=pl.CostEstimate(
-            flops=60 * rows * half * half, bytes_accessed=20 * rows * half, transcendentals=0
+            flops=44 * rows * half * half, bytes_accessed=14 * rows * half, transcendentals=0
         ),
         name="project_rows",
-    )(near, far, *weights, cosine, sine, *extra)
+    )(near, far, *weights, cosine, sine)
 
 
 def feed_kernel(
-    x_ref,
-    g_ref,
-    up_ref,
-    down_ref,
+    xa_ref,
+    xb_ref,
+    ga_ref,
+    gb_ref,
+    up_a,
+    up_b,
+    down_a,
+    down_b,
     bias_ref,
     out_ref,
     dx_ref,
@@ -174,47 +161,50 @@
     xt_ref,
     gt_ref,
 ):
+    half = xa_ref.shape[1]
+    first, second = slice(0, half), slice(half, 2 * half)
+
     @pl.when(pl.program_id(0) == 0)
     def _():
-        xt_ref[...] = x_ref[...].T
-        gt_ref[...] = g_ref[...].T
+        xt_ref[first] = xa_ref[...].T
+        xt_ref[second] = xb_ref[...].T
+        gt_ref[first] = ga_ref[...].T
+        gt_ref[second] = gb_ref[...].T
         out_ref[...] = jnp.zeros(out_ref.shape, WIDE)
         dx_ref[...] = jnp.zeros(dx_ref.shape, WIDE)
 
-    hidden = dot_nn(x_ref[...], up_ref[...]) + bias_ref[...]
-    grad = dot_nt(g_ref[...], down_ref[...])
+    hidden = dot_nn(xa_ref[...], up_a[...]) + dot_nn(xb_ref[...], up_b[...]) + bias_ref[...]
+    grad = dot_nt(ga_ref[...], down_a[...]) + dot_nt(gb_ref[...], down_b[...])
     below = 0.5 + 0.5 * lax.erf(hidden * math.sqrt(0.5))
     density = jnp.exp(-0.5 * hidden * hidden) * (1.0 / math.sqrt(2.0 * math.pi))
     active = (hidden * below).astype(LOW)
     grad = (grad * (below + hidden * density)).astype(LOW)
     dbias_ref[...] = jnp.sum(grad.astype(WIDE), axis=0, keepdims=True)
-    out_ref[...] += dot_nn(active, down_ref[...])
-    dx_ref[...] += dot_nt(grad, up_ref[...])
+    out_ref[:, first] += dot_nn(active, down_a[...])
+    out_ref[:, second] += dot_nn(active, down_b[...])
+    dx_ref[:, first] += dot_nt(grad, up_a[...])
+    dx_ref[:, second] += dot_nt(grad, up_b[...])
     dup_ref[...] = dot_nn(xt_ref[...], grad).astype(LOW)
     ddown_ref[...] = dot_nn(gt_ref[...], active).astype(LOW)
 
 
-def feed_forward(x, g, up, down, bias):
-    rows, width = x.shape
+def feed_forward(x_halves, g_halves, stacks, bias):
+    rows, half = x_halves[0].shape
+    width = 2 * half
     hidden = bias.shape[1]
-    step = 512
-    steps = hidden // step
+    steps = hidden // half
 
     def whole(shape):
         return pl.BlockSpec(shape, lambda i: (0, 0))
 
-    column = pl.BlockSpec((width, step), lambda i: (0, i))
-    line = pl.BlockSpec((1, step), lambda i: (0, i))
+    up = pl.BlockSpec((half, half), lambda i: (i, 0))
+    down = pl.BlockSpec((half, half), lambda i: (i + steps, 0))
+    column = pl.BlockSpec((width, half), lambda i: (0, i))
+    line = pl.BlockSpec((1, half), lambda i: (0, i))
     return pl.pallas_call(
         feed_kernel,
         grid=(steps,),
-        in_specs=[
-            whole((rows, width)),
-            whole((rows, width)),
-            column,
-            pl.BlockSpec((step, width), lambda i: (i, 0)),
-            line,
-        ],
+        in_specs=[whole((rows, half))] * 4 + [up, up, down, down, line],
         out_specs=[
             whole((rows, width)),
             whole((rows, width)),
@@ -238,7 +228,7 @@
             flops=26 * rows * width * hidden, bytes_accessed=12 * width * hidden, transcendentals=0
         ),
         name="feed_forward",
-    )(x, g, up, down, bias)
+    )(*x_halves, *g_halves, *stacks, *stacks, bias)
 
 
 def outer_kernel(left_a, right_a, left_b, right_b, out_ref):
@@ -285,7 +275,8 @@
     blocks,
     first,
     last,
-    inverse,
+    natural,
+    base,
     q_ref,
     k_ref,
     v_ref,
@@ -316,10 +307,11 @@
     def _(j):
         row0 = pl.multiple_of(blocks[j] * BLK, BLK)
         out0 = pl.multiple_of(j * BLK, BLK)
+        here = pl.multiple_of(base[0] + out0, BLK)
         lo = first[j]
         hi = last[j]
         for g in range(pairs):
-            q_scr[g] = two_heads(q_ref[pl.ds(out0, BLK), lanes(g)].astype(WIDE), lane).astype(
+            q_scr[g] = two_heads(q_ref[pl.ds(here, BLK), lanes(g)].astype(WIDE), lane).astype(
                 LOW
             ) * LOW(SCALE)
             d_scr[g] = two_heads(d_ref[pl.ds(out0, BLK), lanes(g)].astype(WIDE), lane).astype(LOW)
@@ -338,7 +330,7 @@
             key_place = key0 + lax.broadcasted_iota(jnp.int32, (2 * BLK, CHUNK), 1)
             allowed = (key_place >= starts) & (key_place <= places)
             for g in range(pairs):
-                scores = dot_nt(q_scr[g], gathered_blocks(k_ref, inverse, c, lanes(g)))
+                scores = dot_nt(q_scr[g], gathered_blocks(k_ref, natural, c, lanes(g)))
                 scores = jnp.where(allowed, scores, NEG_BIG)
                 s_scr[g, c - lo] = scores
                 m_scr[g] = jnp.maximum(m_scr[g], lane_tiles(scores, jnp.maximum))
@@ -351,7 +343,7 @@
         @pl.loop(lo, hi)
         def _(c):
             for g in range(pairs):
-                values = gathered_blocks(v_ref, inverse, c, lanes(g))
+                values = gathered_blocks(v_ref, natural, c, lanes(g))
                 top = m_scr[g]
                 weights = jnp.exp(s_scr[g, c - lo] - jnp.concatenate([top] * (CHUNK // BLK), 1))
                 l_scr[g] += lane_tiles(weights, jnp.add)
@@ -370,9 +362,9 @@
             stat_out[j, 2 * g : 2 * g + 1, :] = log_sum[:BLK].T[0:1]
             stat_out[j, 2 * g + 1 : 2 * g + 2, :] = log_sum[BLK:].T[0:1]
             wide = jnp.broadcast_to(delta, (2 * BLK, BLK))
-            base = stat_out.shape[1] // 2 + 2 * g
-            stat_out[j, base : base + 1, :] = wide[:BLK].T[0:1]
-            stat_out[j, base + 1 : base + 2, :] = wide[BLK:].T[0:1]
+            line = stat_out.shape[1] // 2 + 2 * g
+            stat_out[j, line : line + 1, :] = wide[:BLK].T[0:1]
+            stat_out[j, line + 1 : line + 2, :] = wide[BLK:].T[0:1]
             l_scr[g] = jnp.broadcast_to(share, (2 * BLK, BLK))
             e_scr[g] = wide
         o_scr[...] = jnp.zeros(o_scr.shape, WIDE)
@@ -383,11 +375,11 @@
                 wide = jnp.concatenate([e_scr[g]] * (CHUNK // BLK), 1)
                 grad_score = s_scr[g, c - lo] * (p_scr[g, c - lo] - wide)
                 o_scr[g] += dot_nn(
-                    grad_score.astype(LOW), gathered_blocks(k_ref, inverse, c, lanes(g))
+                    grad_score.astype(LOW), gathered_blocks(k_ref, natural, c, lanes(g))
                 )
 
-        cosine = cos_ref[pl.ds(out0, BLK), :]
-        sine = sin_ref[pl.ds(out0, BLK), :]
+        cosine = cos_ref[pl.ds(here, BLK), :]
+        sine = sin_ref[pl.ds(here, BLK), :]
         for g in range(pairs):
             grad = one_of_two(o_scr[g] * l_scr[g], lane) * SCALE
             dq_out[pl.ds(out0, BLK), lanes(g)] = turned(grad, cosine, -sine, lane).astype(LOW)
@@ -401,7 +393,7 @@
     return pl.BlockSpec(memory_space=pltpu.VMEM)
 
 
-def query_side(blocks, first, last, inverse, queries, keys, values, grads, cosine, sine, starts):
+def query_side(blocks, first, last, natural, base, queries, keys, values, grads, cosine, sine, starts):
     own = blocks.shape[0]
     width = queries.shape[1]
     pairs = width // BLK
@@ -409,7 +401,7 @@
     work = 2 * BLK * CHUNK
     return pl.pallas_call(
         query_kernel,
-        in_specs=[smem()] * 4 + [vmem()] * 7,
+        in_specs=[smem()] * 5 + [vmem()] * 7,
         out_specs=[vmem()] * 3,
         out_shape=[
             jax.ShapeDtypeStruct((own * BLK, width), LOW),
@@ -433,15 +425,17 @@
             transcendentals=own * pairs * 4 * work,
         ),
         name="query_side",
-    )(blocks, first, last, inverse, queries, keys, values, grads, cosine, sine, starts)
+    )(blocks, first, last, natural, base, queries, keys, values, grads, cosine, sine, starts)
 
 
 def key_kernel(
     blocks,
     first,
     last,
-    inverse,
     natural,
+    by_partner,
+    stat_place,
+    base,
     q_ref,
     k_ref,
     v_ref,
@@ -465,11 +459,12 @@
     def _(j):
         row0 = pl.multiple_of(blocks[j] * BLK, BLK)
         out0 = pl.multiple_of(j * BLK, BLK)
+        here = pl.multiple_of(base[0] + out0, BLK)
         for g in range(pairs):
-            k_scr[g] = two_heads(k_ref[pl.ds(out0, BLK), lanes(g)].astype(WIDE), lane).astype(
+            k_scr[g] = two_heads(k_ref[pl.ds(here, BLK), lanes(g)].astype(WIDE), lane).astype(
                 LOW
             ) * LOW(SCALE)
-            v_scr[g] = two_heads(v_ref[pl.ds(out0, BLK), lanes(g)].astype(WIDE), lane).astype(LOW)
+            v_scr[g] = two_heads(v_ref[pl.ds(here, BLK), lanes(g)].astype(WIDE), lane).astype(LOW)
         dk_scr[...] = jnp.zeros(dk_scr.shape, WIDE)
         dv_scr[...] = jnp.zeros(dv_scr.shape, WIDE)
         ends = end_ref[pl.ds(out0, BLK), :]
@@ -481,14 +476,14 @@
             query_place = query0 + lax.broadcasted_iota(jnp.int32, (BLK, CHUNK), 1)
             allowed = (query_place >= places) & (query_place < ends)
             count = CHUNK // BLK
-            slots = [natural[c * count + i] for i in range(count)]
+            slots = [stat_place[c * count + i] for i in range(count)]
 
             def stat(row):
                 return jnp.concatenate([stat_ref[slot, row : row + 1, :] for slot in slots], 1)
 
             for g in range(pairs):
-                queries = gathered_blocks(q_ref, inverse, c, lanes(g))
-                grads = gathered_blocks(d_ref, inverse, c, lanes(g))
+                queries = gathered_blocks(q_ref, natural, c, lanes(g))
+                grads = gathered_blocks(d_ref, by_partner, c, lanes(g))
                 scores = dot_nt(k_scr[g], queries)
                 grad_prob = dot_nt(v_scr[g], grads)
                 probs, grad_scores = [], []
@@ -503,8 +498,8 @@
                 dv_scr[g] += dot_nn(jnp.concatenate(probs, 0), grads)
                 dk_scr[g] += dot_nn(jnp.concatenate(grad_scores, 0), queries)
 
-        cosine = cos_ref[pl.ds(out0, BLK), :]
-        sine = sin_ref[pl.ds(out0, BLK), :]
+        cosine = cos_ref[pl.ds(here, BLK), :]
+        sine = sin_ref[pl.ds(here, BLK), :]
         for g in range(pairs):
             grad = one_of_two(dk_scr[g], lane) * SCALE
             dk_out[pl.ds(out0, BLK), lanes(g)] = turned(grad, cosine, -sine, lane).astype(LOW)
@@ -515,8 +510,10 @@
     blocks,
     first,
     last,
-    inverse,
     natural,
+    by_partner,
+    stat_place,
+    base,
     queries,
     keys,
     values,
@@ -533,7 +530,7 @@
     work = 2 * BLK * CHUNK
     return pl.pallas_call(
         key_kernel,
-        in_specs=[smem()] * 5 + [vmem()] * 8 + [pl.BlockSpec(memory_space=pl.ANY)] * len(after),
+        in_specs=[smem()] * 7 + [vmem()] * 8 + [pl.BlockSpec(memory_space=pl.ANY)] * len(after),
         out_specs=[vmem()] * 2,
         out_shape=[jax.ShapeDtypeStruct((own * BLK, width), LOW)] * 2,
         scratch_shapes=[
@@ -553,8 +550,10 @@
         blocks,
         first,
         last,
-        inverse,
         natural,
+        by_partner,
+        stat_place,
+        base,
         queries,
         keys,
         values,
@@ -723,62 +722,61 @@
         return jnp.where(first_tp, array[:, half:], array[:, :half])
 
     own_pair = jnp.concatenate([tokens, cotangent], axis=0)
-
-    def send_high(value, pairs):
-        return lax.ppermute(
-            value,
-            "ctx",
-            [(a * low_count + i, b * low_count + i) for a, b in pairs for i in range(low_count)],
+    far_pair = partner(own_pair, "tp", 1)
+
+    g_near = [
+        jnp.concatenate(
+            [cotangent] + [partner(cotangent, "ctx", s * low_count) for s in range(1, OWNERS)],
+            axis=0,
         )
-
-    inner = (ctx_high == 1) | (ctx_high == 2)
-    between, outward = [(1, 2), (2, 1)], [(1, 0), (2, 3)]
-    beside = send_high(own_pair, [(0, 1), (1, 0), (2, 3), (3, 2)])
-    middle = send_high(own_pair, between)
-    lasting = send_high(beside, between)
-    line = [
-        own_pair,
-        beside,
-        jnp.where(inner, middle, send_high(middle, outward)),
-        jnp.where(inner, lasting, send_high(lasting, outward)),
     ]
-    order = sorted(
-        ((low, slot) for low in range(low_count) for slot in range(OWNERS)),
-        key=lambda item: (item[1] + (item[0] > 0), item[0]),
-    )
-    blocks_near = [
-        line[slot] if low == 0 else partner(line[slot], "ctx", low) for low, slot in order
-    ]
-    blocks_far = [partner(block, "tp", 1) for block in blocks_near]
-    far_pair = blocks_far[0]
-    inputs_low = both_halves(tokens, far_pair[:row_count], 1)
-    full_cotangent = both_halves(cotangent, far_pair[row_count:], 1)
-
-    up_full = gather_axis(w_up.astype(LOW), "fsdp", 0)
-    down_full = gather_axis(w_down.astype(LOW), "fsdp", 1)
-    attn_full = gather_axis(w_attn.astype(LOW), "fsdp", 1)
-    qkv_full = lax.all_gather(
-        jnp.transpose(w_qkv, (1, 0, 2)).astype(LOW), "fsdp", axis=1, tiled=True
-    )
-
-    def group_place(ctx):
-        high = ctx // low_count
-        slot = jnp.where(
-            high == ctx_high,
-            0,
-            jnp.where(high == ctx_high ^ 1, 1, jnp.where((high == 1) | (high == 2), 2, 3)),
+    x_near = lax.all_gather(tokens, "ctx", axis=0, tiled=True)
+    for s in range(1, low_count):
+        g_near.append(partner(g_near[0], "ctx", s))
+    g_far = [partner(part, "tp", 1) for part in g_near]
+    x_far = partner(x_near, "tp", 1)
+
+    def stacked(up, down, qkv, attn):
+        cuts = range(0, up.shape[1], half)
+        return jnp.concatenate(
+            [up[:, i : i + half] for i in cuts] + [down] + [qkv[:, i] for i in range(3)] + [attn],
+            axis=0,
         )
-        low = (ctx % low_count) ^ ctx_low
-        place = jnp.zeros_like(ctx)
-        for k, (its_low, its_slot) in enumerate(order):
-            place = jnp.where((low == its_low) & (slot == its_slot), k, place)
-        return place
+
+    low_weights = [w.astype(LOW) for w in (w_up, w_down, w_qkv, w_attn)]
+    if fsdp_count == 2:
+        stack = stacked(*low_weights)
+        other = partner(stack, "fsdp", 1)
+        first_fsdp = fsdp_index == 0
+        stacks = (jnp.where(first_fsdp, stack, other), jnp.where(first_fsdp, other, stack))
+    else:
+        whole_up, whole_down, whole_qkv, whole_attn = (
+            lax.all_gather(w, "fsdp", axis=dim, tiled=True)
+            for w, dim in zip(low_weights, (0, 1, 0, 1))
+        )
+        stacks = tuple(
+            stacked(whole_up[cut], whole_down[:, cut], whole_qkv[cut], whole_attn[:, cut])
+            for cut in (slice(0, half), slice(half, 2 * half))
+        )
+    hidden_here = up_bias.shape[0]
+    late_stacks = tuple(part[2 * hidden_here :] for part in stacks)
+    attn_halves = tuple(part[3 * half :] for part in late_stacks)
+
+    def by_partners(ctx):
+        differs = ctx ^ ctx_index
+        return (differs % low_count) * OWNERS + differs // low_count
 
     slot_blocks = jnp.arange(block_row.shape[0], dtype=jnp.int32)
-    slot_places = group_place(slot_blocks // own_blocks) * own_blocks + slot_blocks % own_blocks
+    slot_ctx, slot_rest = slot_blocks // own_blocks, slot_blocks % own_blocks
     holds = block_row[None, :] == slot_blocks[:, None]
-    inverse = jnp.sum(jnp.where(holds, slot_places[None, :], 0), axis=1).astype(jnp.int32)
-    natural = jnp.sum(jnp.where(holds, slot_blocks[None, :], 0), axis=1).astype(jnp.int32)
+
+    def located(places):
+        return jnp.sum(jnp.where(holds, places[None, :], 0), axis=1).astype(jnp.int32)
+
+    natural = located(slot_blocks)
+    by_partner = located(by_partners(slot_ctx) * own_blocks + slot_rest)
+    stat_place = located((slot_ctx ^ ctx_index) * own_blocks + slot_rest)
+    row_base = (ctx_index * row_count).reshape(1)
     my_blocks = lax.dynamic_slice_in_dim(block_row, ctx_index * own_blocks, own_blocks)
 
     seq_ends = jnp.cumsum(length_row).astype(jnp.int32)
@@ -791,11 +789,8 @@
             jnp.sum(jnp.where(inside, seq_ends[None, :], 0), axis=1).astype(jnp.int32),
         )
 
-    group_blocks = jnp.sum(
-        jnp.where(slot_places[None, :] == slot_blocks[:, None], block_row[None, :], 0), axis=1
-    )
     offsets = jnp.arange(BLK, dtype=jnp.int32)
-    packed = (group_blocks[:, None] * BLK + offsets[None, :]).reshape(-1)
+    packed = (block_row[:, None] * BLK + offsets[None, :]).reshape(-1)
     cosine, sine = rotary_tables(packed - bounds(packed)[0])
     my_starts, my_ends = bounds(
         (my_blocks[:, None] * BLK + offsets[None, :]).reshape(-1)
@@ -809,29 +804,39 @@
         left, right = jnp.split(array, 2, axis=dim)
         return jnp.where(first_tp, left, right), jnp.where(first_tp, right, left)
 
-    inputs = inputs_low.astype(WIDE)
-    centered = inputs - jnp.mean(inputs, axis=1, keepdims=True)
-    inv_std = lax.rsqrt(jnp.mean(centered * centered, axis=1, keepdims=True) + 1e-05)
-    normed = centered * inv_std
-    norm_out = (normed * norm_vectors[0] + norm_vectors[1]).astype(LOW)
-    hidden_here = up_bias.shape[0]
+    def two_halves(mine, other):
+        return jnp.where(first_tp, mine, other), jnp.where(first_tp, other, mine)
+
+    x_halves = [half_x.astype(WIDE) for half_x in two_halves(tokens, far_pair[:row_count])]
+    row_mean = sum(jnp.sum(x, axis=1, keepdims=True) for x in x_halves) / width
+    centered = [x - row_mean for x in x_halves]
+    inv_std = lax.rsqrt(sum(jnp.sum(x * x, axis=1, keepdims=True) for x in centered) / width + 1e-5)
+    norm_halves = [
+        (x * inv_std * vec[0] + vec[1]).astype(LOW)
+        for x, vec in zip(centered, jnp.split(norm_vectors, 2, axis=1))
+    ]
     feed_out, feed_dx, grad_up, grad_down, grad_ubias, norm_t, cotangent_t = feed_forward(
-        norm_out, full_cotangent, up_full, down_full, up_bias.reshape(1, hidden_here)
-    )
-
-    projections = (
-        *own_first(qkv_full, 1),
-        *own_first(attn_full, 1),
-        qkv_bias,
-        *own_first(norm_vectors, 1),
-    )
-    made = ()
-    for place, (near, far) in enumerate(zip(blocks_near, blocks_far)):
-        after = (grad_ubias,) if place == len(order) - 3 else ()
-        made = project_rows(
-            place, len(order), near, far, projections, cosine, sine, made, after
-        )
-    queries, keys, values, d_attended = made
+        norm_halves,
+        two_halves(cotangent, far_pair[row_count:]),
+        stacks,
+        up_bias.reshape(1, hidden_here),
+    )
+
+    queries, keys, values = project_rows(
+        x_near,
+        x_far,
+        (*two_halves(*late_stacks), qkv_bias, *own_first(norm_vectors, 1)),
+        cosine,
+        sine,
+    )
+    attn_near, attn_far = two_halves(*attn_halves)
+    d_attended = jnp.concatenate(
+        [
+            (dot_nt(near, attn_near) + dot_nt(far, attn_far)).astype(LOW)
+            for near, far in zip(g_near, g_far)
+        ],
+        axis=0,
+    )
 
     def reduced_first(gradient):
         rows = gradient.shape[0] // fsdp_count
@@ -846,18 +851,12 @@
         return sum_scatter(part, "ctx", low_count, ctx_high)
 
     first_up, first_down = reduced_first(grad_up), reduced_first(grad_down)
-
-    def scatter_low(part):
-        piece = part.shape[0] // ctx_count
-        part = part.reshape(OWNERS, low_count, piece, part.shape[1])
-        return sum_scatter(jnp.swapaxes(part, 0, 1), "ctx", 1, ctx_low)
-
-    sum_feed = sum_scatter(
-        jnp.concatenate([scatter_low(first_up), scatter_low(first_down)], axis=2),
+    sum_feed = lax.psum_scatter(
+        jnp.concatenate([first_up, first_down], axis=1).astype(LOW),
         "ctx",
-        low_count,
-        ctx_high,
-    )
+        scatter_dimension=0,
+        tiled=True,
+    ).astype(WIDE)
     sum_up, sum_down = sum_feed[:, :hidden_here], sum_feed[:, hidden_here:]
     piece = sum_up.shape[0]
     grad_outbias = jnp.sum(cotangent.astype(WIDE), axis=0)
@@ -920,7 +919,8 @@
         my_blocks,
         key_first,
         key_last,
-        inverse,
+        natural,
+        row_base,
         queries,
         keys,
         values,
@@ -929,16 +929,20 @@
         sine,
         my_starts[:, None],
     )
-    sum_early = reduced_rest(
-        reduced_first(outer_pair(norm_t, grad_q, cotangent_t, attended))
-    )
-    all_stats = lax.all_gather(stats, "ctx", axis=0, tiled=True)
+    early_rows = reduced_first(outer_pair(norm_t, grad_q, cotangent_t, attended))
+    all_stats = stats
+    step = 1
+    while step < ctx_count:
+        all_stats = jnp.concatenate([all_stats, partner(all_stats, "ctx", step)], axis=0)
+        step *= 2
     grad_k, grad_v = key_side(
         my_blocks,
         query_first,
         query_last,
-        inverse,
         natural,
+        by_partner,
+        stat_place,
+        row_base,
         queries,
         keys,
         values,
@@ -951,14 +955,18 @@
     )
     grad_late = outer_pair(norm_t, grad_k, norm_t, grad_v)
     late_rows = reduced_first(grad_late)
-    sum_late = reduced_rest(late_rows)
+    joint_rows = jnp.concatenate([early_rows, late_rows], axis=1)
+    sum_joint = reduced_rest(lax.optimization_barrier((joint_rows, sum_feed))[0])
     grad_q, grad_k, grad_v, grad_late = lax.optimization_barrier(
         (grad_q, grad_k, grad_v, grad_late)
     )
     grad_proj = (grad_q, grad_k, grad_v)
     grad_qbias = jnp.concatenate([jnp.sum(grad.astype(WIDE), axis=0) for grad in grad_proj])
 
-    partial_out = dot_nn(attended, attn_full) + feed_out
+    def joined(pair):
+        return jnp.concatenate(pair, axis=1)
+
+    partial_out = joined([dot_nn(attended, attn) for attn in attn_halves]) + feed_out
 
     def sum_halves(array):
         return own_half(array) + partner(far_half(array).astype(LOW), "tp", 1).astype(WIDE)
@@ -967,9 +975,18 @@
     mixed = (tokens.astype(WIDE) + sum_halves(partial_out) + out_bias).astype(LOW)
 
     grad_norm = sum_halves(
-        sum(dot_nt(grad, qkv_full[i]) for i, grad in enumerate(grad_proj)) + feed_dx
-    )
-    my_normed = own_half(normed)
+        joined(
+            [
+                sum(
+                    dot_nt(grad, stack[i * half : (i + 1) * half])
+                    for i, grad in enumerate(grad_proj)
+                )
+                for stack in late_stacks
+            ]
+        )
+        + feed_dx
+    )
+    my_normed = jnp.where(first_tp, *centered) * inv_std
     scaled = grad_norm * own_half(norm_vectors[0:1])
     row_sums = jnp.stack([jnp.sum(scaled, axis=1), jnp.sum(scaled * my_normed, axis=1)])
     row_means = (row_sums + partner(row_sums, "tp", 1)) / width
@@ -989,8 +1006,8 @@
     sum_qbias = small[3 * half : 6 * half].reshape(3, half)
     sum_ubias = small[6 * half :]
 
-    sum_qkv = jnp.concatenate([sum_early[:, :half], sum_late], axis=1)
-    sum_attn = sum_early[:, half:]
+    sum_qkv = jnp.concatenate([sum_joint[:, :half], sum_joint[:, 2 * half :]], axis=1)
+    sum_attn = sum_joint[:, half : 2 * half]
     gathered = all_rows(sum_qkv, sum_attn)
     fresh_qkv = 0.95 * qkv_moment + jnp.stack(jnp.split(gathered[:, : 3 * half], 3, axis=1), axis=1)
     fresh_attn = 0.95 * attn_moment + gathered[:, 3 * half :].T

time: 569 us -> 544 us (0.956)
  blocking collectives: 35.5 us -> 0 us
  matrix products: 12 us -> 31.4 us
  Pallas kernels: 147 us -> 130 us
  local copies, waits for them, and re-layouts: 54.5 us -> 46.8 us
  starting transfers between devices: 89.2 us -> 96.7 us
  waiting for transfers between devices: 137 us -> 143 us
    all_gather x1 -> x0, blocking collectives: 35.5 us -> none  [body(): all_stats = lax.all_gather(stats, 'ctx', axis=0, tiled=True)]
    pallas_call x11 -> x4, Pallas kernels: 94 us -> 74.1 us  [the longest x1 24.3 us: query_side(): pl.pallas_call(query_kernel, in_specs=[smem()] * 5 + [vmem()] * 7, out_sp...]
    ppermute x43 -> x31, starting transfers between devices: 52 us -> 70.9 us  [partner(): return lax.ppermute(value, axis, [(i, i ^ step) for i in range(size)])]
    dot_general x3 -> x10, matrix products: 1.77 us -> 19.2 us  [dot_nt(): return lax.dot_general(left, right, NT, preferred_element_type=WIDE)]
    select_n x4 -> x3, other arithmetic: 0.72 us -> 12 us  [the longest x1 6.66 us: body(): jnp.where(first_fsdp, other, stack)]
    ppermute x43 -> x31, waiting for transfers between devices: 109 us -> 120 us  [partner(): return lax.ppermute(value, axis, [(i, i ^ step) for i in range(size)])]
    ppermute x5 -> x0, starting transfers between devices: 8.85 us -> none  [send_high(): lax.ppermute(value, 'ctx', [(a * low_count + i, b * low_count + i) for a,...]
    ppermute x5 -> x0, waiting for transfers between devices: 8.31 us -> none  [send_high(): lax.ppermute(value, 'ctx', [(a * low_count + i, b * low_count + i) for a,...]
  transfers between devices with their start and end apart: 67 -> 51, of which waited for: 22 -> 20; matrix products, arithmetic and copies ran while one was open for 20% -> 26% of each run, Pallas kernels for 26% -> 24%
where the time goes in v4:
time: 544 us; the launch traced here: 534 us
  waiting for transfers between devices  143 us (26%)
  Pallas kernels  130 us (24%)
  starting transfers between devices  96.7 us (18%)
  other arithmetic  71.1 us (13%)
  local copies, waits for them, and re-layouts  46.8 us (9%)
  matrix products  31.4 us (6%)
  between operations  15.3 us (3%)
    ppermute x31, waiting for transfers between devices, partner(): return lax.ppermute(value, axis, [(i, i ^ step) for i in range(size)])  120 us
    ppermute x31, starting transfers between devices, partner(): return lax.ppermute(value, axis, [(i, i ^ step) for i in range(size)])  70.9 us
    pallas_call x1, Pallas kernels, orthogonal_rows(): pl.pallas_call(partial(ns_kernel, spans), in_specs=[smem()] + [pl.BlockSp...  48.9 us
    unnamed x163, local copies, waits for them, and re-layouts  26.3 us
    ppermute x16, starting transfers between devices, partner_among(): return lax.ppermute(value, tuple(axes), pairs)  25.6 us
    pallas_call x1, Pallas kernels, query_side(): pl.pallas_call(query_kernel, in_specs=[smem()] * 5 + [vmem()] * 7, out_sp...  24.3 us
    ppermute x16, waiting for transfers between devices, partner_among(): return lax.ppermute(value, tuple(axes), pairs)  22.3 us
    dot_general x10, matrix products, dot_nt(): return lax.dot_general(left, right, NT, preferred_element_type=WIDE)  19.2 us
  transfers between devices with their start and end apart: 51, of which 20 were waited for; matrix products, arithmetic and copies ran while one was open for 26% of the time, Pallas kernels for 24%

profile of v4, /device:TPU:0, one launch (start us, length us, event | category | flops | bytes accessed | tf_op | source)
XLA Modules:
  0.0 533.9 jit_solution(13785249717441983016)
XLA Ops:
  7.2 3.1 collective-permute-start.2
  10.3 2.6 collective-permute-start.3
  14.3 1.9 convert_element_type.193
  23.5 1.7 collective-permute-start.1
  34.7 4.1 convolution_add_fusion.cos_ref
  41.3 2.1 broadcast_select_fusion.4
  52.4 5.0 fusion.46.sin_ref
  60.9 39.2 %collective-permute-done.6 = bf16[2048,384]{1,0:T(8,128)(2,1)} collective-permute-done((bf16[2048,384]{1,0:T(8,128)(2,1)S(1)}, bf16[2048,384]{1,0:T(8,128)(2,1)}, u32[]{:S(2)}, u32[]{:S(2)}) %collective-permute-start.6) | collective-permute-done | bytes 1572896 | tf_op jit(solution)/shard_map/ppermute | solution.py:38
  100.1 2.6 collective-permute-done.1
  102.7 6.7 %broadcast_select_fusion = (bf16[4608,384]{1,0:T(8,128)(2,1)}, bf16[4608,384]{1,0:T(8,128)(2,1)}) fusion(bf16[4608,384]{1,0:T(8,128)(2,1)} %collective-permute-done.1, bf16[4608,384]{1,0:T(8,128)(2,1)} %convert_dynamic-update-slice_fusion.1, pred[]{:T(512)S(6)} %eq.77), kind=kLoop, calls=%fused_computation.1 | loop fusion | flops 3538944 | bytes 14155777 | tf_op jit(solution)/shard_map/jit(_where)/select_n | solution.py:751
  109.3 15.8 %feed_forward.1 = (f32[512,768]{1,0:T(8,128)}, f32[512,768]{1,0:T(8,128)}, bf16[768,1536]{1,0:T(8,128)(2,1)}, bf16[768,1536]{1,0:T(8,128)(2,1)}, f32[1,1536]{1,0...) custom-call(bf16[512,384]{1,0:T(8,128)(2,1)} %get-tuple-element.215.xa_ref, ...), custom_call_target="tpu_custom_call" | custom-call | flops 15703474176 | bytes 14155776 | tf_op jit(solution)/shard_map/feed_forward/pallas_call | solution.py:204
  125.1 2.5 dynamic-slice_bitcast_fusion.1
  130.8 2.7 fusion.54
  133.5 3.3 broadcast_select_fusion.2
  136.8 2.7 add_convert_fusion.1
  139.4 2.7 fusion.53
  142.1 2.7 add_convert_fusion
  144.9 2.0 pad_maximum_fusion.d_ref
  146.9 9.9 %collective-permute-done.13 = bf16[384,1536]{1,0:T(8,128)(2,1)} collective-permute-done((bf16[384,1536]{1,0:T(8,128)(2,1)}, bf16[384,1536]{1,0:T(8,128)(2,1)}, u32[]{:S(2)}, u32[]{:S(2)}) %collective-permute-start.13) | collective-permute-done | bytes 1179680 | tf_op jit(solution)/shard_map/ppermute | solution.py:38
  156.9 3.1 fusion.81
  159.9 20.7 %collective-permute-done.14 = bf16[384,1536]{1,0:T(8,128)(2,1)} collective-permute-done((bf16[384,1536]{1,0:T(8,128)(2,1)}, bf16[384,1536]{1,0:T(8,128)(2,1)}, u32[]{:S(2)}, u32[]{:S(2)}) %collective-permute-start.14) | collective-permute-done | bytes 1179680 | tf_op jit(solution)/shard_map/ppermute | solution.py:38
  180.7 3.1 fusion.82
  183.8 1.8 pad_maximum_fusion.2
  185.6 19.1 %project_rows.1 = (bf16[4096,384]{1,0:T(8,128)(2,1)}, bf16[4096,384]{1,0:T(8,128)(2,1)}, bf16[4096,384]{1,0:T(8,128)(2,1)}) custom-call(bf16[4096,384]{1,0:T(8,128)(2,1)} %all-gather.4.cloned.1.call-done.near, bf16[4096,384]{1,0:T(8,128)(2,1)} %collective-permute-done.far, bf16[1536,384]{1,0:T(8,128)(2,1)} %get-tuple-element.147.w_near, ...), custom_call_target="tpu_custom_call" | custom-call | flops 26575110144 | bytes 22020096 | tf_op jit(solution)/shard_map/project_rows/pallas_call | solution.py:132
  204.8 24.3 %query_side.1 = (bf16[512,384]{1,0:T(8,128)(2,1)}, bf16[512,384]{1,0:T(8,128)(2,1)}, f32[4,16,128]{2,1,0:T(8,128)}) custom-call(s32[4]{0:T(128)} %copy-done.63, s32[4]{0:T(128)} %and_select_fusion.9.first, s32[4]{0:T(128)} %get-tuple-element.216.last, s32[32]{0:T(128)} %get-tuple-element.121.natural, s32[1]{0:T(128)} %bitcast.6.base, ...), custom_call_target="tpu_custom_call" | custom-call | flops 19327352832 | bytes 12582912 | tf_op jit(solution)/shard_map/query_side/pallas_call | solution.py:402
  232.4 3.9 collective-permute-done.10
  236.4 9.3 %collective-permute-start.11 = (f32[8,16,128]{2,1,0:T(8,128)S(1)}, f32[8,16,128]{2,1,0:T(8,128)S(1)}, u32[]{:S(2)}, u32[]{:S(2)}) collective-permute-start(f32[8,16,128]{2,1,0:T(8,128)S(1)} %pad_maximum_fusion.15), channel_id=1, source_target_pairs={{0,4},{2,6},{4,0},{6,2},{8,12},{10,14},{12,8},{14,10},{1,5},{3,7},... | collective-permute-start | bytes 196616 | tf_op jit(solution)/shard_map/ppermute | solution.py:38
  248.0 4.4 collective-permute-start.12
  252.3 3.6 outer_pair.3
  257.0 6.1 %collective-permute-start.17 = (bf16[384,768]{1,0:T(8,128)(2,1)S(1)}, bf16[384,768]{1,0:T(8,128)(2,1)S(1)}, u32[]{:S(2)}, u32[]{:S(2)}) collective-permute-start(bf16[384,768]{1,0:T(8,128)(2,1)S(1)} %dynamic-slice_bitcast_fusion.3), channel_id=1, source_target_pairs={{0,16},{16,0},{1,17},{17,1},{2,18},{18,2},{3,19},{19,3},{4,20},{20... | collective-permute-start | bytes 1769480 | tf_op jit(solution)/shard_map/ppermute | solution.py:38
  263.8 14.9 %key_side.1 = (bf16[512,384]{1,0:T(8,128)(2,1)}, bf16[512,384]{1,0:T(8,128)(2,1)}) custom-call(s32[4]{0:T(128)} %copy-done.63, s32[4]{0:T(128)} %get-tuple-element.140.first, s32[4]{0:T(128)} %and_select_fusion.4.last, s32[32]{0:T(128)} %get-tuple-element.121.natural, s32[32]{0:T(128)} %get-tuple-element.120.by_partner, s32[32]{0:T(128)} %get-tuple-element.119.stat_place, ...), custom_call_target="tpu_custom_call" | custom-call | flops 19327352832 | bytes 12582912 | tf_op jit(solution)/shard_map/key_side/pallas_call | solution.py:531
  278.7 3.7 outer_pair.2
  293.0 8.1 %collective-permute-start.18 = (bf16[384,768]{1,0:T(8,128)(2,1)}, bf16[384,768]{1,0:T(8,128)(2,1)S(1)}, u32[]{:S(2)}, u32[]{:S(2)}) collective-permute-start(bf16[384,768]{1,0:T(8,128)(2,1)} %dynamic-slice_bitcast_fusion.2), channel_id=1, source_target_pairs={{0,16},{16,0},{1,17},{17,1},{2,18},{18,2},{3,19},{19,3},{4,20},{20... | collective-permute-start | bytes 1769480 | tf_op jit(solution)/shard_map/ppermute | solution.py:38
  302.4 1.8 convert_element_type.223
  304.2 10.3 %collective-permute-done.18 = bf16[384,768]{1,0:T(8,128)(2,1)S(1)} collective-permute-done((bf16[384,768]{1,0:T(8,128)(2,1)}, bf16[384,768]{1,0:T(8,128)(2,1)S(1)}, u32[]{:S(2)}, u32[]{:S(2)}) %collective-permute-start.18) | collective-permute-done | bytes 589856 | tf_op jit(solution)/shard_map/ppermute | solution.py:38
  316.0 7.2 %collective-permute-start.19 = (bf16[4,48,1536]{2,1,0:T(8,128)(2,1)S(1)}, bf16[4,48,1536]{2,1,0:T(8,128)(2,1)S(1)}, u32[]{:S(2)}, u32[]{:S(2)}) collective-permute-start(bf16[4,48,1536]{2,1,0:T(8,128)(2,1)S(1)} %fusion.17), channel_id=1, source_target_pairs={{0,2},{2,0},{4,6},{6,4},{8,10},{10,8},{12,14},{14,12},{1,3},{3,1},... | collective-permute-start | bytes 1769480 | tf_op jit(solution)/shard_map/ppermute | solution.py:38
  324.7 11.2 %collective-permute-done.19 = bf16[4,48,1536]{2,1,0:T(8,128)(2,1)S(1)} collective-permute-done((bf16[4,48,1536]{2,1,0:T(8,128)(2,1)S(1)}, bf16[4,48,1536]{2,1,0:T(8,128)(2,1)S(1)}, u32[]{:S(2)}, u32[]{:S(2)}) %collective-permute-start.19) | collective-permute-done | bytes 589856 | tf_op jit(solution)/shard_map/ppermute | solution.py:38
  336.5 3.9 collective-permute-start.20
  340.5 4.1 collective-permute-done.22
  344.7 4.4 collective-permute-done.21
  351.1 1.8 constant_dynamic-slice_fusion.1
  355.1 2.1 copy.80
  357.3 2.2 copy.81
  364.4 2.4 add_convert_fusion.2
  374.1 3.7 collective-permute-start.25
  379.3 10.2 %collective-permute-done.23 = bf16[48,1536]{1,0:T(8,128)(2,1)S(1)} collective-permute-done((bf16[48,1536]{1,0:T(8,128)(2,1)S(1)}, bf16[48,1536]{1,0:T(8,128)(2,1)S(1)}, u32[]{:S(2)}, u32[]{:S(2)}) %collective-permute-start.23) | collective-permute-done | bytes 147488 | tf_op jit(solution)/shard_map/ppermute | solution.py:54
  389.6 1.9 collective-permute-start.26
  391.5 3.4 collective-permute-start.27
  397.1 4.3 collective-permute-done.26
  402.4 1.9 collective-permute-start.29
  404.3 3.4 collective-permute-start.28
  412.1 3.4 collective-permute-done.31
  415.5 3.3 collective-permute-done.32
  422.0 1.9 collective-permute-start.30
  426.8 1.8 pad_maximum_fusion.3.far_a
  430.0 48.9 %orthogonal_rows.1 = bf16[192,1536]{1,0:T(8,128)(2,1)} custom-call(s32[1]{0:T(128)} %bitcast.43.high, bf16[768,1536]{1,0:T(8,128)(2,1)} %constant_dynamic-update-slice_fusion.4.near_a, bf16[768,1536]{1,0:T(8,128)(2,1)} %pad_maximum_fusion.3.far_a, bf16[768,1152]{1,0:T(8,128)(2,1)} %copy-done.53, bf16[768,1152]{1,0:T(8,128)(2,1)} %pad_maximum_fusion.4.far_b), custom_call_target="tpu_custom_call" | custom-call | flops 45298483200 | bytes 9437184 | tf_op jit(solution)/shard_map/orthogonal_rows/pallas_call | solution.py:640
  480.1 2.8 collective-permute-start.41
  482.9 13.4 %collective-permute-start.40 = (bf16[48,1536]{1,0:T(8,128)(2,1)S(1)}, bf16[48,1536]{1,0:T(8,128)(2,1)S(1)}, u32[]{:S(2)}, u32[]{:S(2)}) collective-permute-start(bf16[48,1536]{1,0:T(8,128)(2,1)S(1)} %get-tuple-element.172), channel_id=1, source_target_pairs={{0,8},{2,10},{4,12},{6,14},{8,0},{10,2},{12,4},{14,6},{1,9},{3,11}... | collective-permute-start | bytes 442376 | tf_op jit(solution)/shard_map/ppermute | solution.py:38
  497.4 9.6 %collective-permute-done.40 = bf16[48,1536]{1,0:T(8,128)(2,1)S(1)} collective-permute-done((bf16[48,1536]{1,0:T(8,128)(2,1)S(1)}, bf16[48,1536]{1,0:T(8,128)(2,1)S(1)}, u32[]{:S(2)}, u32[]{:S(2)}) %collective-permute-start.40) | collective-permute-done | bytes 147488 | tf_op jit(solution)/shard_map/ppermute | solution.py:38
  508.6 1.8 fusion.34
  518.0 2.4 convert_element_type.242
  520.4 1.8 slice_add_fusion
  522.2 1.8 fusion
  524.1 3.0 copy.87
  (356 shorter events, 103.0 us)
Async XLA Ops:
  7.2 129.6 %all-gather.4.cloned.1.call-start = ((), (), s32[]{:S(2)}) async-start(), calls=%async_computation.1 | async-start | bytes 3538944 | tf_op jit(solution)/shard_map/all_gather | solution.py:733
  7.2 36.1 %collective-permute-start.2 = (bf16[512,384]{1,0:T(8,128)(2,1)}, bf16[512,384]{1,0:T(8,128)(2,1)}, u32[]{:S(2)}, u32[]{:S(2)}) collective-permute-start(bf16[512,384]{1,0:T(8,128)(2,1)} %param.19), channel_id=1, source_target_pairs={{0,4},{2,6},{4,0},{6,2},{8,12},{10,14},{12,8},{14,10},{1,5},{3,7},... | collective-permute-start | bytes 1179656 | tf_op jit(solution)/shard_map/ppermute | solution.py:38
  10.3 34.1 %collective-permute-start.3 = (bf16[512,384]{1,0:T(8,128)(2,1)}, bf16[512,384]{1,0:T(8,128)(2,1)}, u32[]{:S(2)}, u32[]{:S(2)}) collective-permute-start(bf16[512,384]{1,0:T(8,128)(2,1)} %param.19), channel_id=1, source_target_pairs={{0,8},{2,10},{4,12},{6,14},{8,0},{10,2},{12,4},{14,6},{1,9},{3,11}... | collective-permute-start | bytes 1179656 | tf_op jit(solution)/shard_map/ppermute | solution.py:38
  12.9 32.8 %collective-permute-start.4 = (bf16[512,384]{1,0:T(8,128)(2,1)}, bf16[512,384]{1,0:T(8,128)(2,1)}, u32[]{:S(2)}, u32[]{:S(2)}) collective-permute-start(bf16[512,384]{1,0:T(8,128)(2,1)} %param.19), channel_id=1, source_target_pairs={{0,12},{2,14},{4,8},{6,10},{8,4},{10,6},{12,0},{14,2},{1,13},{3,15... | collective-permute-start | bytes 1179656 | tf_op jit(solution)/shard_map/ppermute | solution.py:38
  12.9 289.4 %reduce-scatter.2.cloned.1.call-start = ((), (), s32[]{:S(2)}) async-start(), calls=%async_computation.2 | async-start | bytes 2654208 | tf_op jit(solution)/shard_map/reduce_scatter | solution.py:854
  14.2 27.1 %collective-permute-start.8 = (bf16[1024,384]{1,0:T(8,128)(2,1)S(1)}, bf16[1024,384]{1,0:T(8,128)(2,1)}, u32[]{:S(2)}, u32[]{:S(2)}) collective-permute-start(bf16[1024,384]{1,0:T(8,128)(2,1)S(1)} %pad_maximum_fusion.7), channel_id=1, source_target_pairs={{0,1},{1,0},{2,3},{3,2},{4,5},{5,4},{6,7},{7,6},{8,9},{9,8},{10,11... | collective-permute-start | bytes 2359304 | tf_op jit(solution)/shard_map/ppermute | solution.py:38
  23.5 79.1 %collective-permute-start.1 = (bf16[4608,384]{1,0:T(8,128)(2,1)}, bf16[4608,384]{1,0:T(8,128)(2,1)}, u32[]{:S(2)}, u32[]{:S(2)}) collective-permute-start(bf16[4608,384]{1,0:T(8,128)(2,1)} %convert_dynamic-update-slice_fusion.1), channel_id=1, source_target_pairs={{0,16},{16,0},{1,17},{17,1},{2,18},{18,2},{3,19},{19,3},{4,20},{20... | collective-permute-start | bytes 10616840 | tf_op jit(solution)/shard_map/ppermute | solution.py:38
  46.8 53.3 %collective-permute-start.6 = (bf16[2048,384]{1,0:T(8,128)(2,1)S(1)}, bf16[2048,384]{1,0:T(8,128)(2,1)}, u32[]{:S(2)}, u32[]{:S(2)}) collective-permute-start(bf16[2048,384]{1,0:T(8,128)(2,1)S(1)} %constant_dynamic-update-slice_fusion), channel_id=1, source_target_pairs={{0,2},{2,0},{4,6},{6,4},{8,10},{10,8},{12,14},{14,12},{1,3},{3,1},... | collective-permute-start | bytes 4718600 | tf_op jit(solution)/shard_map/ppermute | solution.py:38
  57.5 73.4 %collective-permute-start.5 = (bf16[2048,384]{1,0:T(8,128)(2,1)S(1)}, bf16[2048,384]{1,0:T(8,128)(2,1)}, u32[]{:S(2)}, u32[]{:S(2)}) collective-permute-start(bf16[2048,384]{1,0:T(8,128)(2,1)S(1)} %constant_dynamic-update-slice_fusion), channel_id=1, source_target_pairs={{0,1},{1,0},{2,3},{3,2},{4,5},{5,4},{6,7},{7,6},{8,9},{9,8},{10,11... | collective-permute-start | bytes 4718600 | tf_op jit(solution)/shard_map/ppermute | solution.py:38
  100.1 42.0 %collective-permute-start.7 = (bf16[2048,384]{1,0:T(8,128)(2,1)}, bf16[2048,384]{1,0:T(8,128)(2,1)}, u32[]{:S(2)}, u32[]{:S(2)}) collective-permute-start(bf16[2048,384]{1,0:T(8,128)(2,1)} %collective-permute-done.6), channel_id=1, source_target_pairs={{0,1},{1,0},{2,3},{3,2},{4,5},{5,4},{6,7},{7,6},{8,9},{9,8},{10,11... | collective-permute-start | bytes 4718600 | tf_op jit(solution)/shard_map/ppermute | solution.py:38
  127.7 29.2 %collective-permute-start.13 = (bf16[384,1536]{1,0:T(8,128)(2,1)}, bf16[384,1536]{1,0:T(8,128)(2,1)}, u32[]{:S(2)}, u32[]{:S(2)}) collective-permute-start(bf16[384,1536]{1,0:T(8,128)(2,1)} %dynamic-slice_bitcast_fusion.1), channel_id=1, source_target_pairs={{0,16},{16,0},{1,17},{17,1},{2,18},{18,2},{3,19},{19,3},{4,20},{20... | collective-permute-start | bytes 3538952 | tf_op jit(solution)/shard_map/ppermute | solution.py:38
  130.5 50.2 %collective-permute-start.14 = (bf16[384,1536]{1,0:T(8,128)(2,1)}, bf16[384,1536]{1,0:T(8,128)(2,1)}, u32[]{:S(2)}, u32[]{:S(2)}) collective-permute-start(bf16[384,1536]{1,0:T(8,128)(2,1)} %dynamic-slice_bitcast_fusion), channel_id=1, source_target_pairs={{0,16},{16,0},{1,17},{17,1},{2,18},{18,2},{3,19},{19,3},{4,20},{20... | collective-permute-start | bytes 3538952 | tf_op jit(solution)/shard_map/ppermute | solution.py:38
  136.8 48.9 %collective-permute-start = (bf16[4096,384]{1,0:T(8,128)(2,1)}, bf16[4096,384]{1,0:T(8,128)(2,1)}, u32[]{:S(2)}, u32[]{:S(2)}) collective-permute-start(bf16[4096,384]{1,0:T(8,128)(2,1)} %all-gather.4.cloned.1.call-done.near), channel_id=1, source_target_pairs={{0,1},{1,0},{2,3},{3,2},{4,5},{5,4},{6,7},{7,6},{8,9},{9,8},{10,11... | collective-permute-start | bytes 9437192 | tf_op jit(solution)/shard_map/ppermute | solution.py:38
  146.9 33.8 %copy-start.18 = (bf16[768,1536]{1,0:T(8,128)(2,1)S(1)}, bf16[768,1536]{1,0:T(8,128)(2,1)}, u32[]{:S(2)}) copy-start(bf16[768,1536]{1,0:T(8,128)(2,1)} %get-tuple-element.44) | copy-start | bytes 7077892
  185.6 324.9 %all-gather.6.cloned.1.call-start = ((), (), s32[]{:S(2)}) async-start(), calls=%async_computation.3 | async-start | bytes 1327104 | tf_op jit(solution)/shard_map/all_gather | solution.py:866
  232.1 4.2 collective-permute-start.10
  232.4 13.3 %copy-start = (f32[512,768]{1,0:T(8,128)}, f32[512,768]{1,0:T(8,128)S(1)}, u32[]{:S(2)}) copy-start(f32[512,768]{1,0:T(8,128)S(1)} %maximum_add_fusion.1) | copy-start | bytes 4718596
  236.4 11.6 %collective-permute-start.11 = (f32[8,16,128]{2,1,0:T(8,128)S(1)}, f32[8,16,128]{2,1,0:T(8,128)S(1)}, u32[]{:S(2)}, u32[]{:S(2)}) collective-permute-start(f32[8,16,128]{2,1,0:T(8,128)S(1)} %pad_maximum_fusion.15), channel_id=1, source_target_pairs={{0,4},{2,6},{4,0},{6,2},{8,12},{10,14},{12,8},{14,10},{1,5},{3,7},... | collective-permute-start | bytes 196616 | tf_op jit(solution)/shard_map/ppermute | solution.py:38
  246.5 117.8 %collective-permute-start.9 = (bf16[512,384]{1,0:T(8,128)(2,1)}, bf16[512,384]{1,0:T(8,128)(2,1)}, u32[]{:S(2)}, u32[]{:S(2)}) collective-permute-start(bf16[512,384]{1,0:T(8,128)(2,1)} %select_convert_fusion.1), channel_id=1, source_target_pairs={{0,1},{1,0},{2,3},{3,2},{4,5},{5,4},{6,7},{7,6},{8,9},{9,8},{10,11... | collective-permute-start | bytes 1179656 | tf_op jit(solution)/shard_map/ppermute | solution.py:38
  248.0 15.1 %collective-permute-start.12 = (f32[16,16,128]{2,1,0:T(8,128)S(1)}, f32[16,16,128]{2,1,0:T(8,128)S(1)}, u32[]{:S(2)}, u32[]{:S(2)}) collective-permute-start(f32[16,16,128]{2,1,0:T(8,128)S(1)} %pad_maximum_fusion.14), channel_id=1, source_target_pairs={{0,8},{2,10},{4,12},{6,14},{8,0},{10,2},{12,4},{14,6},{1,9},{3,11}... | collective-permute-start | bytes 393224 | tf_op jit(solution)/shard_map/ppermute | solution.py:38
  257.0 44.4 %collective-permute-start.17 = (bf16[384,768]{1,0:T(8,128)(2,1)S(1)}, bf16[384,768]{1,0:T(8,128)(2,1)S(1)}, u32[]{:S(2)}, u32[]{:S(2)}) collective-permute-start(bf16[384,768]{1,0:T(8,128)(2,1)S(1)} %dynamic-slice_bitcast_fusion.3), channel_id=1, source_target_pairs={{0,16},{16,0},{1,17},{17,1},{2,18},{18,2},{3,19},{19,3},{4,20},{20... | collective-permute-start | bytes 1769480 | tf_op jit(solution)/shard_map/ppermute | solution.py:38
  291.2 10.3 %collective-permute-start.15 = (bf16[512,384]{1,0:T(8,128)(2,1)S(1)}, bf16[512,384]{1,0:T(8,128)(2,1)S(1)}, u32[]{:S(2)}, u32[]{:S(2)}) collective-permute-start(bf16[512,384]{1,0:T(8,128)(2,1)S(1)} %select_convert_fusion), channel_id=1, source_target_pairs={{0,1},{1,0},{2,3},{3,2},{4,5},{5,4},{6,7},{7,6},{8,9},{9,8},{10,11... | collective-permute-start | bytes 1179656 | tf_op jit(solution)/shard_map/ppermute | solution.py:38
  293.0 21.4 %collective-permute-start.18 = (bf16[384,768]{1,0:T(8,128)(2,1)}, bf16[384,768]{1,0:T(8,128)(2,1)S(1)}, u32[]{:S(2)}, u32[]{:S(2)}) collective-permute-start(bf16[384,768]{1,0:T(8,128)(2,1)} %dynamic-slice_bitcast_fusion.2), channel_id=1, source_target_pairs={{0,16},{16,0},{1,17},{17,1},{2,18},{18,2},{3,19},{19,3},{4,20},{20... | collective-permute-start | bytes 1769480 | tf_op jit(solution)/shard_map/ppermute | solution.py:38
  302.2 21.0 %collective-permute-start.16 = (f32[2,512]{1,0:T(2,128)S(1)}, f32[2,512]{1,0:T(2,128)S(1)}, u32[]{:S(2)}, u32[]{:S(2)}) collective-permute-start(f32[2,512]{1,0:T(2,128)S(1)} %pad_maximum_fusion.17), channel_id=1, source_target_pairs={{0,1},{1,0},{2,3},{3,2},{4,5},{5,4},{6,7},{7,6},{8,9},{9,8},{10,11... | collective-permute-start | bytes 12296 | tf_op jit(solution)/shard_map/ppermute | solution.py:38
  316.0 19.8 %collective-permute-start.19 = (bf16[4,48,1536]{2,1,0:T(8,128)(2,1)S(1)}, bf16[4,48,1536]{2,1,0:T(8,128)(2,1)S(1)}, u32[]{:S(2)}, u32[]{:S(2)}) collective-permute-start(bf16[4,48,1536]{2,1,0:T(8,128)(2,1)S(1)} %fusion.17), channel_id=1, source_target_pairs={{0,2},{2,0},{4,6},{6,4},{8,10},{10,8},{12,14},{14,12},{1,3},{3,1},... | collective-permute-start | bytes 1769480 | tf_op jit(solution)/shard_map/ppermute | solution.py:38
  324.7 15.8 %copy-start.43 = (f32[3840]{0:T(1024)S(1)}, f32[3840]{0:T(1024)}, u32[]{:S(2)}) copy-start(f32[3840]{0:T(1024)} %custom-call) | copy-start | bytes 46084
  335.9 18.6 %copy-start.44 = (f32[1,768]{1,0:T(1,128)S(1)}, f32[1,768]{1,0:T(1,128)}, u32[]{:S(2)}) copy-start(f32[1,768]{1,0:T(1,128)} %slice_add_fusion.4) | copy-start | bytes 9220
  336.0 8.7 %collective-permute-start.22 = (bf16[48,1536]{1,0:T(8,128)(2,1)S(1)}, bf16[48,1536]{1,0:T(8,128)(2,1)S(1)}, u32[]{:S(2)}, u32[]{:S(2)}) collective-permute-start(bf16[48,1536]{1,0:T(8,128)(2,1)S(1)} %get-tuple-element.160), channel_id=1, source_target_pairs={{0,12},{2,14},{4,8},{6,10},{8,4},{10,6},{12,0},{14,2},{1,13},{3,15... | collective-permute-start | bytes 442376 | tf_op jit(solution)/shard_map/ppermute | solution.py:38
  336.1 13.0 %collective-permute-start.21 = (bf16[48,1536]{1,0:T(8,128)(2,1)S(1)}, bf16[48,1536]{1,0:T(8,128)(2,1)S(1)}, u32[]{:S(2)}, u32[]{:S(2)}) collective-permute-start(bf16[48,1536]{1,0:T(8,128)(2,1)S(1)} %get-tuple-element.161), channel_id=1, source_target_pairs={{0,8},{2,10},{4,12},{6,14},{8,0},{10,2},{12,4},{14,6},{1,9},{3,11}... | collective-permute-start | bytes 442376 | tf_op jit(solution)/shard_map/ppermute | solution.py:38
  336.5 12.6 %collective-permute-start.20 = (bf16[48,1536]{1,0:T(8,128)(2,1)S(1)}, bf16[48,1536]{1,0:T(8,128)(2,1)S(1)}, u32[]{:S(2)}, u32[]{:S(2)}) collective-permute-start(bf16[48,1536]{1,0:T(8,128)(2,1)S(1)} %get-tuple-element.159), channel_id=1, source_target_pairs={{0,4},{2,6},{4,0},{6,2},{8,12},{10,14},{12,8},{14,10},{1,5},{3,7},... | collective-permute-start | bytes 442376 | tf_op jit(solution)/shard_map/ppermute | solution.py:38
  350.6 167.4 %all-gather.8.cloned.1.call-start = ((), (), s32[]{:S(2)}) async-start(), calls=%async_computation.4 | async-start | bytes 2654208 | tf_op jit(solution)/shard_map/all_gather | solution.py:866
  350.7 3.8 collective-permute-start.42
  354.5 7.6 %collective-permute-start.43 = (f32[3840]{0:T(1024)S(1)}, f32[3840]{0:T(1024)}, u32[]{:S(2)}, u32[]{:S(2)}) collective-permute-start(f32[3840]{0:T(1024)S(1)} %add.472), channel_id=1, source_target_pairs={{0,4},{2,6},{4,0},{6,2},{8,12},{10,14},{12,8},{14,10},{1,5},{3,7},... | collective-permute-start | bytes 46088 | tf_op jit(solution)/shard_map/ppermute | solution.py:38
  362.9 4.7 collective-permute-start.44
  369.3 20.2 %collective-permute-start.23 = (bf16[48,1536]{1,0:T(8,128)(2,1)S(1)}, bf16[48,1536]{1,0:T(8,128)(2,1)S(1)}, u32[]{:S(2)}, u32[]{:S(2)}) collective-permute-start(bf16[48,1536]{1,0:T(8,128)(2,1)S(1)} %get-tuple-element.185), channel_id=1, source_target_pairs={{4,0},{6,2},{8,12},{10,14},{5,1},{7,3},{9,13},{11,15},{20,16},{22,... | collective-permute-start | bytes 442376 | tf_op jit(solution)/shard_map/ppermute | solution.py:54
  370.6 7.3 %collective-permute-start.45 = (f32[3840]{0:T(1024)S(1)}, f32[3840]{0:T(1024)S(1)}, u32[]{:S(2)}, u32[]{:S(2)}) collective-permute-start(f32[3840]{0:T(1024)S(1)} %add.474), channel_id=1, source_target_pairs={{0,16},{16,0},{1,17},{17,1},{2,18},{18,2},{3,19},{19,3},{4,20},{20... | collective-permute-start | bytes 46088 | tf_op jit(solution)/shard_map/ppermute | solution.py:38
  372.8 16.7 %collective-permute-start.24 = (bf16[48,1536]{1,0:T(8,128)(2,1)S(1)}, bf16[48,1536]{1,0:T(8,128)(2,1)S(1)}, u32[]{:S(2)}, u32[]{:S(2)}) collective-permute-start(bf16[48,1536]{1,0:T(8,128)(2,1)S(1)} %get-tuple-element.184), channel_id=1, source_target_pairs={{8,0},{10,2},{4,12},{6,14},{9,1},{11,3},{5,13},{7,15},{24,16},{26,... | collective-permute-start | bytes 442376 | tf_op jit(solution)/shard_map/ppermute | solution.py:54
  374.1 15.4 %collective-permute-start.25 = (bf16[48,1536]{1,0:T(8,128)(2,1)S(1)}, bf16[48,1536]{1,0:T(8,128)(2,1)S(1)}, u32[]{:S(2)}, u32[]{:S(2)}) collective-permute-start(bf16[48,1536]{1,0:T(8,128)(2,1)S(1)} %get-tuple-element.183), channel_id=1, source_target_pairs={{12,0},{14,2},{0,12},{2,14},{13,1},{15,3},{1,13},{3,15},{28,16},{3... | collective-permute-start | bytes 442376 | tf_op jit(solution)/shard_map/ppermute | solution.py:54
  377.9 1.3 collective-permute-start.46
  389.6 11.8 %collective-permute-start.26 = (bf16[192,1536]{1,0:T(8,128)(2,1)S(1)}, bf16[192,1536]{1,0:T(8,128)(2,1)S(1)}, u32[]{:S(2)}, u32[]{:S(2)}) collective-permute-start(bf16[192,1536]{1,0:T(8,128)(2,1)S(1)} %pad_maximum_fusion.8), channel_id=1, source_target_pairs={{2,0},{0,2},{14,12},{12,14},{3,1},{1,3},{15,13},{13,15},{18,16},{1... | collective-permute-start | bytes 1769480 | tf_op jit(solution)/shard_map/ppermute | solution.py:54
  391.5 16.2 %collective-permute-start.27 = (bf16[192,1536]{1,0:T(8,128)(2,1)S(1)}, bf16[192,1536]{1,0:T(8,128)(2,1)S(1)}, u32[]{:S(2)}, u32[]{:S(2)}) collective-permute-start(bf16[192,1536]{1,0:T(8,128)(2,1)S(1)} %pad_maximum_fusion.8), channel_id=1, source_target_pairs={{16,0},{18,2},{28,12},{30,14},{0,16},{2,18},{12,28},{14,30},{17,1}... | collective-permute-start | bytes 1769480 | tf_op jit(solution)/shard_map/ppermute | solution.py:54
  395.6 13.0 %copy-start.14 = (f32[384,384]{0,1:T(8,128)S(1)}, f32[384,384]{0,1:T(8,128)}, u32[]{:S(2)}) copy-start(f32[384,384]{0,1:T(8,128)} %copy.81) | copy-start | bytes 1769476
  395.6 13.0 %copy-start.23 = (f32[48,1536]{1,0:T(8,128)S(1)}, f32[48,1536]{1,0:T(8,128)}, u32[]{:S(2)}) copy-start(f32[48,1536]{1,0:T(8,128)} %copy-done.22) | copy-start | bytes 884740
  402.4 24.2 %collective-permute-start.29 = (bf16[384,1536]{1,0:T(8,128)(2,1)}, bf16[384,1536]{1,0:T(8,128)(2,1)S(1)}, u32[]{:S(2)}, u32[]{:S(2)}) collective-permute-start(bf16[384,1536]{1,0:T(8,128)(2,1)} %get-tuple-element.174), channel_id=1, source_target_pairs={{1,0},{0,1},{3,2},{2,3},{13,12},{12,13},{15,14},{14,15},{17,16},{1... | collective-permute-start | bytes 3538952 | tf_op jit(solution)/shard_map/ppermute | solution.py:54
  404.3 17.6 %collective-permute-start.28 = (bf16[192,1536]{1,0:T(8,128)(2,1)S(1)}, bf16[192,1536]{1,0:T(8,128)(2,1)S(1)}, u32[]{:S(2)}, u32[]{:S(2)}) collective-permute-start(bf16[192,1536]{1,0:T(8,128)(2,1)S(1)} %collective-permute-done.26), channel_id=1, source_target_pairs={{16,0},{18,2},{28,12},{30,14},{0,16},{2,18},{12,28},{14,30},{17,1}... | collective-permute-start | bytes 1769480 | tf_op jit(solution)/shard_map/ppermute | solution.py:54
  408.8 6.7 %collective-permute-start.31 = (bf16[48,1152]{1,0:T(8,128)(2,1)S(1)}, bf16[48,1152]{1,0:T(8,128)(2,1)S(1)}, u32[]{:S(2)}, u32[]{:S(2)}) collective-permute-start(bf16[48,1152]{1,0:T(8,128)(2,1)S(1)} %get-tuple-element.193), channel_id=1, source_target_pairs={{0,4},{2,6},{12,8},{14,10},{1,5},{3,7},{13,9},{15,11},{16,20},{18,... | collective-permute-start | bytes 331784 | tf_op jit(solution)/shard_map/ppermute | solution.py:54
  410.1 8.7 %collective-permute-start.32 = (bf16[48,1152]{1,0:T(8,128)(2,1)S(1)}, bf16[48,1152]{1,0:T(8,128)(2,1)S(1)}, u32[]{:S(2)}, u32[]{:S(2)}) collective-permute-start(bf16[48,1152]{1,0:T(8,128)(2,1)S(1)} %get-tuple-element.192), channel_id=1, source_target_pairs={{12,4},{14,6},{0,8},{2,10},{13,5},{15,7},{1,9},{3,11},{28,20},{30,... | collective-permute-start | bytes 331784 | tf_op jit(solution)/shard_map/ppermute | solution.py:54
  411.4 7.4 %collective-permute-start.33 = (bf16[48,1152]{1,0:T(8,128)(2,1)S(1)}, bf16[48,1152]{1,0:T(8,128)(2,1)S(1)}, u32[]{:S(2)}, u32[]{:S(2)}) collective-permute-start(bf16[48,1152]{1,0:T(8,128)(2,1)S(1)} %get-tuple-element.191), channel_id=1, source_target_pairs={{8,4},{10,6},{4,8},{6,10},{9,5},{11,7},{5,9},{7,11},{24,20},{26,22... | collective-permute-start | bytes 331784 | tf_op jit(solution)/shard_map/ppermute | solution.py:54
  418.8 1.5 collective-permute-start.34
  419.5 5.3 collective-permute-start.35
  420.3 4.5 collective-permute-start.36
  422.0 4.7 collective-permute-start.30
  424.1 4.5 collective-permute-start.37
  424.9 3.7 collective-permute-start.38
  430.0 66.8 %copy-start.39 = (f32[4,768]{1,0:T(4,128)S(1)}, f32[4,768]{1,0:T(4,128)}, u32[]{:S(2)}) copy-start(f32[4,768]{1,0:T(4,128)} %param.24) | copy-start | bytes 36868
  430.0 66.8 %copy-start.45 = (f32[4,768]{1,0:T(4,128)S(1)}, f32[4,768]{1,0:T(4,128)}, u32[]{:S(2)}) copy-start(f32[4,768]{1,0:T(4,128)} %param.31) | copy-start | bytes 36868
  478.9 28.3 %copy-start.30 = (f32[48,384]{1,0:T(8,128)S(1)}, f32[48,384]{1,0:T(8,128)}, u32[]{:S(2)}) copy-start(f32[48,384]{1,0:T(8,128)} %get-tuple-element.156) | copy-start | bytes 221188
  478.9 28.3 %copy-start.31 = (f32[48,384]{1,0:T(8,128)S(1)}, f32[48,384]{1,0:T(8,128)}, u32[]{:S(2)}) copy-start(f32[48,384]{1,0:T(8,128)} %get-tuple-element.157) | copy-start | bytes 221188
  478.9 28.3 %copy-start.32 = (f32[48,384]{1,0:T(8,128)S(1)}, f32[48,384]{1,0:T(8,128)}, u32[]{:S(2)}) copy-start(f32[48,384]{1,0:T(8,128)} %get-tuple-element.158) | copy-start | bytes 221188
  478.9 29.1 %copy-start.36 = (f32[384,48]{0,1:T(8,128)S(1)}, f32[384,48]{0,1:T(8,128)}, u32[]{:S(2)}) copy-start(f32[384,48]{0,1:T(8,128)} %copy.97) | copy-start | bytes 221188
  478.9 29.8 %copy-start.28 = (f32[1536,48]{0,1:T(8,128)S(1)}, f32[1536,48]{0,1:T(8,128)}, u32[]{:S(2)}) copy-start(f32[1536,48]{0,1:T(8,128)} %copy.98) | copy-start | bytes 884740
  480.1 17.3 %collective-permute-start.41 = (bf16[48,1536]{1,0:T(8,128)(2,1)S(1)}, bf16[48,1536]{1,0:T(8,128)(2,1)S(1)}, u32[]{:S(2)}, u32[]{:S(2)}) collective-permute-start(bf16[48,1536]{1,0:T(8,128)(2,1)S(1)} %get-tuple-element.171), channel_id=1, source_target_pairs={{0,12},{2,14},{4,8},{6,10},{8,4},{10,6},{12,0},{14,2},{1,13},{3,15... | collective-permute-start | bytes 442376 | tf_op jit(solution)/shard_map/ppermute | solution.py:38
  482.9 24.2 %collective-permute-start.40 = (bf16[48,1536]{1,0:T(8,128)(2,1)S(1)}, bf16[48,1536]{1,0:T(8,128)(2,1)S(1)}, u32[]{:S(2)}, u32[]{:S(2)}) collective-permute-start(bf16[48,1536]{1,0:T(8,128)(2,1)S(1)} %get-tuple-element.172), channel_id=1, source_target_pairs={{0,8},{2,10},{4,12},{6,14},{8,0},{10,2},{12,4},{14,6},{1,9},{3,11}... | collective-permute-start | bytes 442376 | tf_op jit(solution)/shard_map/ppermute | solution.py:38
  496.3 10.8 %collective-permute-start.39 = (bf16[48,1536]{1,0:T(8,128)(2,1)S(1)}, bf16[48,1536]{1,0:T(8,128)(2,1)S(1)}, u32[]{:S(2)}, u32[]{:S(2)}) collective-permute-start(bf16[48,1536]{1,0:T(8,128)(2,1)S(1)} %get-tuple-element.173), channel_id=1, source_target_pairs={{0,4},{2,6},{4,0},{6,2},{8,12},{10,14},{12,8},{14,10},{1,5},{3,7},... | collective-permute-start | bytes 442376 | tf_op jit(solution)/shard_map/ppermute | solution.py:38
  (55 other events, 366.5 us)
Sparse Core Ops, SparseCore 0:
  13.1 97.7 all-gather.3
  185.7 82.7 reduce-scatter.1
  350.7 42.6 all-gather.5
  395.4 61.5 all-gather.7
